TPU v7x, 32 devices: a whole 2x2x4 slice. The times are simulated.
32 devices in a mesh: dp: 8 (over y, x, core), mp: 4 (over z).
Axes of the slice: x: 2, y: 2, z: 4, core: 2. Of those that a mesh axis runs over, the one named last changes fastest.
Arguments:
- hidden: float32 [8, 3072, 1024], P('dp', None, 'mp'), may hold values from -0.1875 to 0.1875
- wq: float32 [1024, 1024], P('dp', 'mp'), may hold values from -0.1875 to 0.1875
- wk: float32 [1024, 1024], P('dp', 'mp'), may hold values from -0.1875 to 0.1875
- wv: float32 [1024, 1024], P('dp', 'mp'), may hold values from -0.1875 to 0.1875
- wo: float32 [1024, 1024], P('mp', 'dp'), may hold values from -0.1875 to 0.1875
- w_up: float32 [1024, 4096], P('dp', 'mp'), may hold values from -0.1875 to 0.1875
- w_gate: float32 [1024, 4096], P('dp', 'mp'), may hold values from -0.1875 to 0.1875
- w_down: float32 [4096, 1024], P('mp', 'dp'), may hold values from -0.09375 to 0.09375
- s_qk: float32 [1024], P('mp'), may hold values from 0.5 to 2
- s_u: float32 [4096], P('mp'), may hold values from 0.5 to 2
- s_v: float32 [4096], P('mp'), may hold values from 0.5 to 2
- alpha_a: float32 [1024], P('mp'), may hold values from 0.1 to 0.5
- alpha_m: float32 [1024], P('mp'), may hold values from 0.1 to 0.5
- doc_ids: int32 [8, 3072], P('dp'), may hold values from 0 to 4, as said below
- valid: int32 [8, 3072], P('dp'), may hold values from 0 to 1, as said below
- cotangent: float32 [8, 3072, 1024], P('dp', None, 'mp'), may hold values from -6 to 6
Outputs:
- out_hidden: float32 [8, 3072, 1024], P('dp', None, 'mp')
- grad_hidden: float32 [8, 3072, 1024], P('dp', None, 'mp')
- grad_wq: float32 [1024, 1024], P('dp', 'mp')
- grad_wk: float32 [1024, 1024], P('dp', 'mp')
- grad_wv: float32 [1024, 1024], P('dp', 'mp')
- grad_wo: float32 [1024, 1024], P('mp', 'dp')
- grad_w_up: float32 [1024, 4096], P('dp', 'mp')
- grad_w_gate: float32 [1024, 4096], P('dp', 'mp')
- grad_w_down: float32 [4096, 1024], P('mp', 'dp')
- grad_s_qk: float32 [1024], P('mp')
- grad_s_u: float32 [4096], P('mp')
- grad_s_v: float32 [4096], P('mp')
- grad_alpha_a: float32 [1024], P('mp')
- grad_alpha_m: float32 [1024], P('mp')
Inputs may be any that keep to these rules, and one draw needn't show every extreme that they name: `doc_ids`: within a row ids start at 0 and never fall; the first document holds 1024 to 1536 slots, and the last slot of every row has id 4. `valid`: padding is one run of 1 to 384 slots at the end of each row.
All inputs are finite; a program needn't handle non-finite values.
Results may differ from a plain program's by a relative error of at most 0.018.
The roundings to bfloat16 on the way count: a program that leaves them out, or rounds other values in their place, can miss the bound.
Values may be sent and summed in bfloat16 or wider, within the bound.
A program may use at most 256 MiB of HBM per device.

v0:
```python
import math

import jax
import jax.numpy as jnp
from jax import lax
from jax.sharding import PartitionSpec as P

D = 1024
DK = 64


EPSILON = 1e-06
ROPE_BASE = 10000.0
NEG_LARGE = -1e30


def rope_tables(positions, head_size):
    half_size = head_size // 2
    freq_index = jnp.arange(half_size, dtype=jnp.float32)
    inverse = jnp.exp(freq_index * (-2.0 * math.log(ROPE_BASE) / head_size))
    angles = positions.astype(jnp.float32)[..., None] * inverse
    return (jnp.cos(angles), jnp.sin(angles))


def rotate(vector, cosine, sine):
    half_size = vector.shape[-1] // 2
    first_half = vector[..., :half_size]
    second_half = vector[..., half_size:]
    cosine = cosine[..., None, :]
    sine = sine[..., None, :]
    return jnp.concatenate(
        [first_half * cosine - second_half * sine, second_half * cosine + first_half * sine],
        axis=-1,
    )


def normalize(vector):
    return vector * lax.rsqrt(jnp.sum(vector * vector, axis=-1, keepdims=True) + EPSILON)


def positions_of(doc_ids):
    slot_index = jnp.arange(doc_ids.shape[-1], dtype=jnp.int32)
    earlier = jnp.concatenate([doc_ids[..., :1] - 1, doc_ids[..., :-1]], axis=-1)
    starts = jnp.where(doc_ids != earlier, slot_index, jnp.zeros_like(slot_index))
    return slot_index - lax.cummax(starts, axis=starts.ndim - 1)


def block_mask(seg_ids, valid_row, start, block):
    key_slot = jnp.arange(seg_ids.shape[0], dtype=jnp.int32)
    query_slot = start + jnp.arange(block, dtype=jnp.int32)
    query_ids = lax.dynamic_slice_in_dim(seg_ids, start, block, 0)
    same_doc = query_ids[:, None] == seg_ids[None, :]
    causal = key_slot[None, :] <= query_slot[:, None]
    usable = (valid_row[None, :] == 1) | (key_slot[None, :] == query_slot[:, None])
    return same_doc & causal & usable


def head_post(raw, cosine, sine, gain):
    heads_here = gain.shape[0] // DK
    shaped = raw.reshape(raw.shape[0], heads_here, DK)
    return normalize(rotate(shaped, cosine, sine)) * gain.reshape(heads_here, DK)


def swiglu(upward_raw, gating_raw, gain_up, gain_gate):
    return upward_raw * gain_up * jax.nn.silu(gating_raw * (gain_gate * math.sqrt(D)))


def widen(shard):
    return lax.all_gather(shard, "mp", axis=1, tiled=True)


def narrow(term):
    return lax.psum_scatter(
        term.astype(jnp.bfloat16), "mp", scatter_dimension=1, tiled=True
    ).astype(jnp.float32)


def token_total(partial_value):
    return lax.psum(partial_value, "mp")


def mix_with(resid, unit, branch_scale, alpha):
    mixed = resid + alpha * (unit - resid)
    mixed_scale = lax.rsqrt(token_total(jnp.sum(mixed * mixed, axis=1)) + EPSILON)[:, None]
    return (mixed * mixed_scale, (unit, branch_scale, mixed_scale))


def residual_forward(resid, branch, alpha):
    branch_scale = lax.rsqrt(token_total(jnp.sum(branch * branch, axis=1)) + EPSILON)[:, None]
    return mix_with(resid, branch * branch_scale, branch_scale, alpha)


def residual_backward(grad_out, result, resid, alpha, kept):
    unit, branch_scale, mixed_scale = kept
    grad_mixed = mixed_scale * (
        grad_out - result * token_total(jnp.sum(grad_out * result, axis=1))[:, None]
    )
    grad_alpha = jnp.sum(grad_mixed * (unit - resid), axis=0)
    grad_resid = grad_mixed * (1.0 - alpha)
    grad_unit = grad_mixed * alpha
    grad_branch = branch_scale * (
        grad_unit - unit * token_total(jnp.sum(grad_unit * unit, axis=1))[:, None]
    )
    return (grad_resid, grad_branch, grad_alpha)


def masked_scores(query_block, keys, seg_ids, valid_row, start, block, scale):
    scores = (
        jnp.einsum("qhd,khd->hqk", query_block, keys, preferred_element_type=jnp.float32) * scale
    )
    return jnp.where(block_mask(seg_ids, valid_row, start, block)[None], scores, NEG_LARGE)


def attend_forward(query, keys, values, seg_ids, valid_row):
    slots, heads_here, head_size = query.shape
    block = min(512, slots)
    scale = math.sqrt(head_size)

    def one_block(start):
        query_block = lax.dynamic_slice_in_dim(query, start, block, 0)
        scores = masked_scores(query_block, keys, seg_ids, valid_row, start, block, scale)
        peak = jnp.max(scores, axis=-1, keepdims=True)
        expo = jnp.exp(scores - peak)
        total = jnp.sum(expo, axis=-1, keepdims=True)
        probs = (expo / total).astype(jnp.bfloat16)
        output = jnp.einsum("hqk,khd->qhd", probs, values, preferred_element_type=jnp.float32)
        return (output, peak[..., 0] + jnp.log(total[..., 0]))

    starts = jnp.arange(slots // block, dtype=jnp.int32) * block
    outputs, logsum = lax.map(one_block, starts)
    return (outputs.reshape(slots, heads_here, head_size), logsum)


def attend_backward(query, keys, values, output, grad_out, logsum, seg_ids, valid_row):
    slots, heads_here, head_size = query.shape
    block = min(512, slots)
    scale = math.sqrt(head_size)
    delta = jnp.sum(grad_out.astype(jnp.float32) * output, axis=-1)

    def one_block(carry, pieces):
        grad_keys, grad_values = carry
        start, lse_block = pieces
        query_block = lax.dynamic_slice_in_dim(query, start, block, 0)
        grad_block = lax.dynamic_slice_in_dim(grad_out, start, block, 0)
        delta_block = jnp.swapaxes(lax.dynamic_slice_in_dim(delta, start, block, 0), 0, 1)
        scores = masked_scores(query_block, keys, seg_ids, valid_row, start, block, scale)
        probs = jnp.exp(scores - lse_block[..., None])
        grad_values = grad_values + jnp.einsum(
            "hqk,qhd->khd",
            probs.astype(jnp.bfloat16),
            grad_block,
            preferred_element_type=jnp.float32,
        )
        grad_probs = jnp.einsum(
            "qhd,khd->hqk", grad_block, values, preferred_element_type=jnp.float32
        )
        grad_scores = (probs * (grad_probs - delta_block[..., None])).astype(jnp.bfloat16)
        grad_query = (
            jnp.einsum("hqk,khd->qhd", grad_scores, keys, preferred_element_type=jnp.float32)
            * scale
        )
        grad_keys = (
            grad_keys
            + jnp.einsum(
                "hqk,qhd->khd", grad_scores, query_block, preferred_element_type=jnp.float32
            )
            * scale
        )
        return ((grad_keys, grad_values), grad_query)

    zero_block = jnp.zeros(keys.shape, jnp.float32)
    starts = jnp.arange(slots // block, dtype=jnp.int32) * block
    (grad_keys, grad_values), grad_query = lax.scan(
        one_block, (zero_block, zero_block), (starts, logsum)
    )
    return (grad_query.reshape(slots, heads_here, head_size), grad_keys, grad_values)


def row_forward(pieces):
    query, keys, values, seg_ids, valid_row = pieces
    return attend_forward(query, keys, values, seg_ids, valid_row)


def row_backward(pieces):
    query, keys, values, output, grad_out, logsum, seg_ids, valid_row = pieces
    return attend_backward(query, keys, values, output, grad_out, logsum, seg_ids, valid_row)


def on_device(
    hidden,
    wq,
    wk,
    wv,
    wo,
    w_up,
    w_gate,
    w_down,
    s_qk,
    s_u,
    s_v,
    alpha_a,
    alpha_m,
    doc_ids,
    valid,
    cotangent,
):
    row_count, slots, part = hidden.shape
    tokens = row_count * slots
    heads_here = s_qk.shape[0] // DK
    low_query = wq.astype(jnp.bfloat16)
    low_keys = wk.astype(jnp.bfloat16)
    low_values = wv.astype(jnp.bfloat16)
    low_output = wo.astype(jnp.bfloat16)
    low_upward = w_up.astype(jnp.bfloat16)
    low_gating = w_gate.astype(jnp.bfloat16)
    low_downward = w_down.astype(jnp.bfloat16)
    full_query, full_keys, full_values, full_output, full_upward, full_gating, full_downward = (
        lax.all_gather(low_query, "dp", axis=0, tiled=True),
        lax.all_gather(low_keys, "dp", axis=0, tiled=True),
        lax.all_gather(low_values, "dp", axis=0, tiled=True),
        lax.all_gather(low_output, "dp", axis=1, tiled=True),
        lax.all_gather(low_upward, "dp", axis=0, tiled=True),
        lax.all_gather(low_gating, "dp", axis=0, tiled=True),
        lax.all_gather(low_downward, "dp", axis=1, tiled=True),
    )
    positions = positions_of(doc_ids).reshape(tokens)
    cosine, sine = rope_tables(positions, DK)

    def post_heads(raw, gain):
        return head_post(raw, cosine, sine, gain)

    resid = hidden.reshape(tokens, part)
    wide_in = widen(resid.astype(jnp.bfloat16))
    query_raw = jnp.dot(wide_in, full_query, preferred_element_type=jnp.float32)
    keys_raw = jnp.dot(wide_in, full_keys, preferred_element_type=jnp.float32)
    query_post, query_pull = jax.vjp(post_heads, query_raw, s_qk)
    keys_post, keys_pull = jax.vjp(post_heads, keys_raw, s_qk)
    shape_four = (row_count, slots, heads_here, DK)
    query_low = query_post.astype(jnp.bfloat16).reshape(shape_four)
    keys_low = keys_post.astype(jnp.bfloat16).reshape(shape_four)
    values_low = (
        jnp.dot(wide_in, full_values, preferred_element_type=jnp.float32)
        .astype(jnp.bfloat16)
        .reshape(shape_four)
    )
    attended, logsum = lax.map(row_forward, (query_low, keys_low, values_low, doc_ids, valid))
    merged = attended.reshape(tokens, heads_here * DK).astype(jnp.bfloat16)
    branch_attn = narrow(jnp.dot(merged, full_output, preferred_element_type=jnp.float32))
    middle, kept_attn = residual_forward(resid, branch_attn, alpha_a)
    middle_wide = widen(middle.astype(jnp.bfloat16))
    upward_raw = jnp.dot(middle_wide, full_upward, preferred_element_type=jnp.float32)
    gating_raw = jnp.dot(middle_wide, full_gating, preferred_element_type=jnp.float32)
    activated, swiglu_pull = jax.vjp(swiglu, upward_raw, gating_raw, s_u, s_v)
    hidden_units = activated.astype(jnp.bfloat16)
    down_term = jnp.dot(hidden_units, full_downward, preferred_element_type=jnp.float32)
    branch_mlp = narrow(down_term)
    result, kept_mlp = residual_forward(middle, branch_mlp, alpha_m)
    back_query, back_keys, back_values, back_output, back_upward, back_gating, back_downward = (
        lax.all_gather(low_query, "dp", axis=0, tiled=True),
        lax.all_gather(low_keys, "dp", axis=0, tiled=True),
        lax.all_gather(low_values, "dp", axis=0, tiled=True),
        lax.all_gather(low_output, "dp", axis=1, tiled=True),
        lax.all_gather(low_upward, "dp", axis=0, tiled=True),
        lax.all_gather(low_gating, "dp", axis=0, tiled=True),
        lax.all_gather(low_downward, "dp", axis=1, tiled=True),
    )
    grad_result = cotangent.reshape(tokens, part)
    grad_middle, grad_branch_mlp, grad_alpha_mlp = residual_backward(
        grad_result, result, middle, alpha_m, kept_mlp
    )
    grad_down_wide = widen(grad_branch_mlp.astype(jnp.bfloat16))
    grad_units = jnp.einsum(
        "te,fe->tf", grad_down_wide, back_downward, preferred_element_type=jnp.float32
    )
    grad_w_downward = jnp.einsum(
        "tf,te->fe", hidden_units, grad_down_wide, preferred_element_type=jnp.float32
    )
    grad_upward, grad_gating, grad_gain_up, grad_gain_gate = swiglu_pull(grad_units)
    grad_upward = grad_upward.astype(jnp.bfloat16)
    grad_gating = grad_gating.astype(jnp.bfloat16)
    grad_w_upward = jnp.einsum(
        "te,tf->ef", middle_wide, grad_upward, preferred_element_type=jnp.float32
    )
    grad_w_gating = jnp.einsum(
        "te,tf->ef", middle_wide, grad_gating, preferred_element_type=jnp.float32
    )
    middle_term = jnp.einsum(
        "tf,ef->te", grad_upward, back_upward, preferred_element_type=jnp.float32
    )
    middle_term = middle_term + jnp.einsum(
        "tf,ef->te", grad_gating, back_gating, preferred_element_type=jnp.float32
    )
    grad_middle = grad_middle + narrow(middle_term)
    grad_resid, grad_branch_attn, grad_alpha_attn = residual_backward(
        grad_middle, middle, resid, alpha_a, kept_attn
    )
    grad_attn_wide = widen(grad_branch_attn.astype(jnp.bfloat16))
    grad_merged = jnp.einsum(
        "te,he->th", grad_attn_wide, back_output, preferred_element_type=jnp.float32
    ).astype(jnp.bfloat16)
    grad_w_output = jnp.einsum(
        "th,te->he", merged, grad_attn_wide, preferred_element_type=jnp.float32
    )
    grad_query_four, grad_keys_four, grad_values_four = lax.map(
        row_backward,
        (
            query_low,
            keys_low,
            values_low,
            attended,
            grad_merged.reshape(shape_four),
            logsum,
            doc_ids,
            valid,
        ),
    )
    grad_query_raw, grad_gain_query = query_pull(grad_query_four.reshape(tokens, heads_here, DK))
    grad_keys_raw, grad_gain_keys = keys_pull(grad_keys_four.reshape(tokens, heads_here, DK))
    grad_query_low = grad_query_raw.astype(jnp.bfloat16)
    grad_keys_low = grad_keys_raw.astype(jnp.bfloat16)
    grad_values_low = grad_values_four.reshape(tokens, heads_here * DK).astype(jnp.bfloat16)
    grad_w_query = jnp.einsum(
        "te,th->eh", wide_in, grad_query_low, preferred_element_type=jnp.float32
    )
    grad_w_keys = jnp.einsum(
        "te,th->eh", wide_in, grad_keys_low, preferred_element_type=jnp.float32
    )
    grad_w_values = jnp.einsum(
        "te,th->eh", wide_in, grad_values_low, preferred_element_type=jnp.float32
    )
    input_term = jnp.einsum(
        "th,eh->te", grad_query_low, back_query, preferred_element_type=jnp.float32
    )
    input_term = input_term + jnp.einsum(
        "th,eh->te", grad_keys_low, back_keys, preferred_element_type=jnp.float32
    )
    input_term = input_term + jnp.einsum(
        "th,eh->te", grad_values_low, back_values, preferred_element_type=jnp.float32
    )
    grad_resid = grad_resid + narrow(input_term)
    (
        owned_query,
        owned_keys,
        owned_values,
        owned_output,
        owned_upward,
        owned_gating,
        owned_downward,
    ) = (
        lax.psum_scatter(grad_w_query, "dp", scatter_dimension=0, tiled=True),
        lax.psum_scatter(grad_w_keys, "dp", scatter_dimension=0, tiled=True),
        lax.psum_scatter(grad_w_values, "dp", scatter_dimension=0, tiled=True),
        lax.psum_scatter(grad_w_output, "dp", scatter_dimension=1, tiled=True),
        lax.psum_scatter(grad_w_upward, "dp", scatter_dimension=0, tiled=True),
        lax.psum_scatter(grad_w_gating, "dp", scatter_dimension=0, tiled=True),
        lax.psum_scatter(grad_w_downward, "dp", scatter_dimension=1, tiled=True),
    )
    summed_qk, summed_up, summed_gate, summed_attn, summed_mlp = lax.psum(
        (
            grad_gain_query + grad_gain_keys,
            grad_gain_up,
            grad_gain_gate,
            grad_alpha_attn,
            grad_alpha_mlp,
        ),
        "dp",
    )
    return (
        result.reshape(row_count, slots, part),
        grad_resid.reshape(row_count, slots, part),
        owned_query,
        owned_keys,
        owned_values,
        owned_output,
        owned_upward,
        owned_gating,
        owned_downward,
        summed_qk,
        summed_up,
        summed_gate,
        summed_attn,
        summed_mlp,
    )


def solution(mesh):
    return jax.shard_map(
        on_device,
        mesh=mesh,
        in_specs=(
            P("dp", None, "mp"),
            P("dp", "mp"),
            P("dp", "mp"),
            P("dp", "mp"),
            P("mp", "dp"),
            P("dp", "mp"),
            P("dp", "mp"),
            P("mp", "dp"),
            P("mp"),
            P("mp"),
            P("mp"),
            P("mp"),
            P("mp"),
            P("dp", None),
            P("dp", None),
            P("dp", None, "mp"),
        ),
        out_specs=(
            P("dp", None, "mp"),
            P("dp", None, "mp"),
            P("dp", "mp"),
            P("dp", "mp"),
            P("dp", "mp"),
            P("mp", "dp"),
            P("dp", "mp"),
            P("dp", "mp"),
            P("mp", "dp"),
            P("mp"),
            P("mp"),
            P("mp"),
            P("mp"),
            P("mp"),
        ),
        check_vma=False,
    )
```

profile of v0, /device:TPU:17, one launch (start us, length us, event | category | flops | bytes accessed | tf_op | source)
XLA Modules:
  0.0 2326.0 jit_solution(1214167417439974353)
XLA Ops:
  56.4 68.3 %all-gather.8.cloned.1.call-done = bf16[3072,1024]{1,0:T(8,128)(2,1)} async-done(((bf16[3072,256]{1,0:T(8,128)(2,1)}), bf16[3072,1024]{1,0:T(8,128)(2,1)}) %all-gather.8.cloned.1.call-update) | async-done | bytes 6291472 | tf_op jit(solution)/shard_map/all_gather | solution.py:69
  139.5 253.8 %while.47 = (s32[]{:T(128)}, f32[6,512,4,64]{1,3,2,0:T(8,128)}, f32[6,4,512]{2,1,0:T(4,128)}, s32[6]{0:T(128)S(1)}, s32[3072]{0:T(1024)S(1)}, /*index=5*/s32[307...) while((s32[]{:T(128)}, f32[6,512,4,64]{1,3,2,0:T(8,128)}, ...), condition=%wide.region_7.8_spmd, body=%wide.region_4.7_spmd.sunk | while | flops 1695548928 | bytes 92119256 | solution.py:130
  405.7 110.7 %reduce-scatter.12.cloned.1.call-done = bf16[3072,256]{1,0:T(8,128)(2,1)} async-done(((bf16[3072,1024]{1,0:T(8,128)(2,1)}), bf16[3072,256]{1,0:T(8,128)(2,1)}) %reduce-scatter.12.cloned.1.call-update) | async-done | bytes 1572880 | tf_op jit(solution)/shard_map/reduce_scatter | solution.py:73
  550.7 116.3 %all-gather.10.cloned.1.call-done = bf16[3072,1024]{1,0:T(8,128)(2,1)} async-done(((bf16[3072,256]{1,0:T(8,128)(2,1)}), bf16[3072,1024]{1,0:T(8,128)(2,1)}) %all-gather.10.cloned.1.call-update) | async-done | bytes 6291472 | tf_op jit(solution)/shard_map/all_gather | solution.py:69
  679.4 18.6 all-gather.12.cloned.1.call-done
  698.0 16.7 multiply_convert_fusion.3
  714.8 13.2 all-gather.16.cloned.1.call-done
  739.1 110.8 %reduce-scatter.14.cloned.1.call-done = bf16[3072,256]{1,0:T(8,128)(2,1)} async-done(((bf16[3072,1024]{1,0:T(8,128)(2,1)}), bf16[3072,256]{1,0:T(8,128)(2,1)}) %reduce-scatter.14.cloned.1.call-update) | async-done | bytes 1572880 | tf_op jit(solution)/shard_map/reduce_scatter | solution.py:73
  918.1 128.2 %all-gather.18.cloned.1.call-done = bf16[3072,1024]{1,0:T(8,128)(2,1)} async-done(((bf16[3072,256]{1,0:T(8,128)(2,1)}), bf16[3072,1024]{1,0:T(8,128)(2,1)}) %all-gather.18.cloned.1.call-update) | async-done | bytes 6291472 | tf_op jit(solution)/shard_map/all_gather | solution.py:69
  1046.3 26.4 %multiply_reduce_fusion = (f32[1024]{0:T(1024)}, f32[1024]{0:T(1024)}, f32[3072,1024]{1,0:T(8,128)}, bf16[3072,1024]{1,0:T(8,128)(2,1)}) fusion(f32[3072,1024]{1,0:T(8,128)} %fusion.69, f32[3072,1024]{1,0:T(8,128)} %get-tuple-element.370, f32[1024]{0:T(1024)S(1)} %broadcast_multiply_fusion.1, f32[1024]{0:T(1024)S(1)} %copy-done.65, ...), kind=kOutput, calls=%fused_computation.56 | convolution fusion | flops 6505363456 | bytes 52445184 | tf_op jit(solution)/shard_map/te,fe->tf/dot_general | solution.py:272
  1085.6 15.4 add_convert_fusion.1
  1101.0 112.4 %reduce-scatter.16.cloned.1.call-done = bf16[3072,256]{1,0:T(8,128)(2,1)} async-done(((bf16[3072,1024]{1,0:T(8,128)(2,1)}), bf16[3072,256]{1,0:T(8,128)(2,1)}) %reduce-scatter.16.cloned.1.call-update) | async-done | bytes 1572880 | tf_op jit(solution)/shard_map/reduce_scatter | solution.py:73
  1263.0 110.4 %all-gather.20.cloned.1.call-done = bf16[3072,1024]{1,0:T(8,128)(2,1)} async-done(((bf16[3072,256]{1,0:T(8,128)(2,1)}), bf16[3072,1024]{1,0:T(8,128)(2,1)}) %all-gather.20.cloned.1.call-update) | async-done | bytes 6291472 | tf_op jit(solution)/shard_map/all_gather | solution.py:69
  1390.2 473.8 %while.48 = (s32[]{:T(128)}, f32[3072,4,64]{0,2,1:T(8,128)}, f32[3072,4,64]{0,2,1:T(8,128)}, f32[6,512,4,64]{1,0,3,2:T(8,128)}, s32[6]{0:T(128)S(1)}, /*index=5*...) while((s32[]{:T(128)}, f32[3072,4,64]{0,2,1:T(8,128)}, ...), condition=%wide.region_29.30_spmd.clone, body=%wide.region_28.29_spmd.clone.sunk | while | flops 4102950400 | bytes 139034864 | solution.py:173
  1421.8 17.0 multiply_convert_fusion.10
  1486.3 13.8 fusion.163
  1500.1 17.0 multiply_convert_fusion.10
  1565.5 13.8 fusion.163
  1579.2 17.0 multiply_convert_fusion.10
  1644.6 13.8 fusion.163
  1658.4 17.0 multiply_convert_fusion.10
  1723.8 13.8 fusion.163
  1737.6 17.0 multiply_convert_fusion.10
  1803.0 13.8 fusion.163
  1816.7 17.0 multiply_convert_fusion.10
  1948.0 13.8 fusion.62
  1968.5 22.5 all-reduce.4
  2000.9 112.1 %reduce-scatter.18.cloned.1.call-done = bf16[3072,256]{1,0:T(8,128)(2,1)} async-done(((bf16[3072,1024]{1,0:T(8,128)(2,1)}), bf16[3072,256]{1,0:T(8,128)(2,1)}) %reduce-scatter.18.cloned.1.call-update) | async-done | bytes 1572880 | tf_op jit(solution)/shard_map/reduce_scatter | solution.py:73
  2116.4 51.5 %reduce-scatter.32.cloned.1.call-done = f32[1024,128]{1,0:T(8,128)} async-done(((f32[1024,1024]{1,0:T(8,128)}), f32[1024,128]{1,0:T(8,128)}) %reduce-scatter.32.cloned.1.call-update) | async-done | bytes 524304 | tf_op jit(solution)/shard_map/reduce_scatter | solution.py:356
  2167.9 55.5 %reduce-scatter.28.cloned.1.call-done = f32[128,1024]{1,0:T(8,128)} async-done(((f32[1024,1024]{1,0:T(8,128)}), f32[128,1024]{1,0:T(8,128)}) %reduce-scatter.28.cloned.1.call-update) | async-done | bytes 524304 | tf_op jit(solution)/shard_map/reduce_scatter | solution.py:354
  2223.5 55.0 %reduce-scatter.30.cloned.1.call-done = f32[128,1024]{1,0:T(8,128)} async-done(((f32[1024,1024]{1,0:T(8,128)}), f32[128,1024]{1,0:T(8,128)}) %reduce-scatter.30.cloned.1.call-update) | async-done | bytes 524304 | tf_op jit(solution)/shard_map/reduce_scatter | solution.py:355
  2278.5 39.9 %reduce-scatter.26.cloned.1.call-done = f32[256,128]{1,0:T(8,128)} async-done(((f32[256,1024]{1,0:T(8,128)}), f32[256,128]{1,0:T(8,128)}) %reduce-scatter.26.cloned.1.call-update) | async-done | bytes 131088 | tf_op jit(solution)/shard_map/reduce_scatter | solution.py:353
  (431 shorter events, 915.1 us)
Async XLA Ops:
  8.1 116.6 %all-gather.8.cloned.1.call-start = ((), (), s32[]{:S(2)}) async-start(), calls=%async_computation.11 | async-start | bytes 7864320 | tf_op jit(solution)/shard_map/all_gather | solution.py:69
  11.5 504.9 %reduce-scatter.12.cloned.1.call-start = ((), (), s32[]{:S(2)}) async-start(), calls=%async_computation.12 | async-start | bytes 7864320 | tf_op jit(solution)/shard_map/reduce_scatter | solution.py:73
  12.1 122.6 %copy-start.49 = (f32[4,64]{1,0:T(4,128)}, f32[4,64]{1,0:T(4,128)S(1)}, u32[]{:S(2)}) copy-start(f32[4,64]{1,0:T(4,128)S(1)} %mul.529) | copy-start | bytes 3076
  44.9 84.6 %copy-start.25 = (bf16[1024,256]{1,0:T(8,128)(2,1)}, bf16[1024,256]{1,0:T(8,128)(2,1)S(1)}, u32[]{:S(2)}) copy-start(bf16[1024,256]{1,0:T(8,128)(2,1)S(1)} %all_gather.42) | copy-start | bytes 1572868
  54.9 74.7 %copy-start.26 = (bf16[1024,256]{1,0:T(8,128)(2,1)}, bf16[1024,256]{1,0:T(8,128)(2,1)S(1)}, u32[]{:S(2)}) copy-start(bf16[1024,256]{1,0:T(8,128)(2,1)S(1)} %all_gather.41) | copy-start | bytes 1572868
  56.4 75.0 %copy-start.17 = (f32[3072,32]{0,1:T(8,128)}, f32[3072,32]{0,1:T(8,128)S(1)}, u32[]{:S(2)}) copy-start(f32[3072,32]{0,1:T(8,128)S(1)} %get-tuple-element.363) | copy-start | bytes 1179652
  56.4 75.0 %copy-start.19 = (f32[3072,32]{0,1:T(8,128)}, f32[3072,32]{0,1:T(8,128)S(1)}, u32[]{:S(2)}) copy-start(f32[3072,32]{0,1:T(8,128)S(1)} %get-tuple-element.364) | copy-start | bytes 1179652
  403.8 125.6 %copy-start.51 = (f32[256]{0:T(256)S(1)}, f32[256]{0:T(256)}, u32[]{:S(2)}) copy-start(f32[256]{0:T(256)} %param.31) | copy-start | bytes 3076
  403.9 146.9 %all-gather.14.cloned.1.call-start = ((), (), s32[]{:S(2)}) async-start(), calls=%async_computation.15 | async-start | bytes 2359296 | tf_op jit(solution)/shard_map/all_gather | solution.py:223
  405.6 261.4 %all-gather.10.cloned.1.call-start = ((), (), s32[]{:S(2)}) async-start(), calls=%async_computation.13 | async-start | bytes 7864320 | tf_op jit(solution)/shard_map/all_gather | solution.py:69
  546.9 151.1 %all-gather.12.cloned.1.call-start = ((), (), s32[]{:S(2)}) async-start(), calls=%async_computation.14 | async-start | bytes 2359296 | tf_op jit(solution)/shard_map/all_gather | solution.py:222
  548.8 179.2 %all-gather.16.cloned.1.call-start = ((), (), s32[]{:S(2)}) async-start(), calls=%async_computation.16 | async-start | bytes 2359296 | tf_op jit(solution)/shard_map/all_gather | solution.py:224
  550.6 299.3 %reduce-scatter.14.cloned.1.call-start = ((), (), s32[]{:S(2)}) async-start(), calls=%async_computation.17 | async-start | bytes 7864320 | tf_op jit(solution)/shard_map/reduce_scatter | solution.py:73
  550.7 534.9 %copy-start.58 = (f32[1024]{0:T(1024)}, f32[1024]{0:T(1024)S(1)}, u32[]{:S(2)}) copy-start(f32[1024]{0:T(1024)S(1)} %broadcast_multiply_fusion.1) | copy-start | bytes 12292
  550.7 147.3 %copy-start.65 = (f32[1024]{0:T(1024)S(1)}, f32[1024]{0:T(1024)}, u32[]{:S(2)}) copy-start(f32[1024]{0:T(1024)} %param.29) | copy-start | bytes 12292
  739.1 124.1 %copy-start.54 = (f32[256]{0:T(256)S(1)}, f32[256]{0:T(256)}, u32[]{:S(2)}) copy-start(f32[256]{0:T(256)} %param.32) | copy-start | bytes 3076
  739.1 307.2 %all-gather.18.cloned.1.call-start = ((), (), s32[]{:S(2)}) async-start(), calls=%async_computation.18 | async-start | bytes 7864320 | tf_op jit(solution)/shard_map/all_gather | solution.py:69
  918.1 295.4 %reduce-scatter.16.cloned.1.call-start = ((), (), s32[]{:S(2)}) async-start(), calls=%async_computation.19 | async-start | bytes 7864320 | tf_op jit(solution)/shard_map/reduce_scatter | solution.py:73
  1072.7 12.9 copy-start.64
  1101.0 272.5 %all-gather.20.cloned.1.call-start = ((), (), s32[]{:S(2)}) async-start(), calls=%async_computation.20 | async-start | bytes 7864320 | tf_op jit(solution)/shard_map/all_gather | solution.py:69
  1101.0 128.3 %copy-start.44 = (f32[3072]{0:T(1024)S(1)}, f32[3072]{0:T(1024)}, u32[]{:S(2)}) copy-start(f32[3072]{0:T(1024)} %copy-done.43) | copy-start | bytes 36868
  1101.0 128.3 %copy-start.52 = (f32[256]{0:T(256)S(1)}, f32[256]{0:T(256)}, u32[]{:S(2)}) copy-start(f32[256]{0:T(256)} %param.31) | copy-start | bytes 3076
  1253.3 737.7 %reduce-scatter.22.cloned.1.call-start = ((), (), s32[]{:S(2)}) async-start(), calls=%async_computation.23 | async-start | bytes 1179648 | tf_op jit(solution)/shard_map/reduce_scatter | solution.py:351
  1261.6 111.9 %copy-start.29 = (bf16[256,1024]{1,0:T(8,128)(2,1)S(1)}, bf16[256,1024]{1,0:T(8,128)(2,1)}, u32[]{:S(2)}) copy-start(bf16[256,1024]{1,0:T(8,128)(2,1)} %all_gather.44) | copy-start | bytes 1572868
  1883.7 109.0 %reduce-scatter.24.cloned.1.call-start = ((), (), s32[]{:S(2)}) async-start(), calls=%async_computation.24 | async-start | bytes 1179648 | tf_op jit(solution)/shard_map/reduce_scatter | solution.py:352
  1891.4 107.8 %reduce-scatter.20.cloned.1.call-start = ((), (), s32[]{:S(2)}) async-start(), calls=%async_computation.22 | async-start | bytes 1179648 | tf_op jit(solution)/shard_map/reduce_scatter | solution.py:350
  1903.1 209.9 %reduce-scatter.18.cloned.1.call-start = ((), (), s32[]{:S(2)}) async-start(), calls=%async_computation.21 | async-start | bytes 7864320 | tf_op jit(solution)/shard_map/reduce_scatter | solution.py:73
  1923.0 244.9 %reduce-scatter.32.cloned.1.call-start = ((), (), s32[]{:S(2)}) async-start(), calls=%async_computation.28 | async-start | bytes 4718592 | tf_op jit(solution)/shard_map/reduce_scatter | solution.py:356
  1935.2 288.3 %reduce-scatter.28.cloned.1.call-start = ((), (), s32[]{:S(2)}) async-start(), calls=%async_computation.26 | async-start | bytes 4718592 | tf_op jit(solution)/shard_map/reduce_scatter | solution.py:354
  1947.3 331.1 %reduce-scatter.30.cloned.1.call-start = ((), (), s32[]{:S(2)}) async-start(), calls=%async_computation.27 | async-start | bytes 4718592 | tf_op jit(solution)/shard_map/reduce_scatter | solution.py:355
  1961.9 356.5 %reduce-scatter.26.cloned.1.call-start = ((), (), s32[]{:S(2)}) async-start(), calls=%async_computation.25 | async-start | bytes 1179648 | tf_op jit(solution)/shard_map/reduce_scatter | solution.py:353
  1962.2 150.8 %copy-start.13 = (f32[3072,256]{1,0:T(8,128)S(1)}, f32[3072,256]{1,0:T(8,128)}, u32[]{:S(2)}) copy-start(f32[3072,256]{1,0:T(8,128)} %get-tuple-element.340) | copy-start | bytes 9437188
  (64 other events, 303.2 us)
Sparse Core Ops, SparseCore 0:
  11.6 113.0 all-gather.7
  404.0 112.3 reduce-scatter.11
  918.2 128.0 all-gather.17
  1101.1 112.3 reduce-scatter.15
Sparse Core Ops, SparseCore 1:
  406.2 29.1 all-gather.13
  547.0 120.0 all-gather.9
  668.8 29.1 all-gather.11
  699.9 28.0 all-gather.15
  739.2 110.7 reduce-scatter.13
  1253.3 120.0 all-gather.19
  1883.8 36.7 reduce-scatter.21
  1923.5 35.9 reduce-scatter.23
  1963.1 36.0 reduce-scatter.19
  2001.5 111.4 reduce-scatter.17
  2116.8 51.1 reduce-scatter.31
  2172.2 51.2 reduce-scatter.27
  2227.3 51.2 reduce-scatter.29
  2282.6 35.8 reduce-scatter.25
where the time goes:
time: 2330 us
  waiting for transfers between devices  1110 us (48%)
  matrix products  696 us (30%)
  other arithmetic  203 us (9%)
  blocking collectives  158 us (7%)
  local copies, waits for them, and re-layouts  117 us (5%)
  loops' own time  24.6 us (1%)
    reduce_scatter x4, waiting for transfers between devices, narrow(): lax.psum_scatter(term.astype(jnp.bfloat16), 'mp', scatter_dimension=1, ti...  446 us
    all_gather x4, waiting for transfers between devices, widen(): return lax.all_gather(shard, 'mp', axis=1, tiled=True)  423 us
    dot_general x12, matrix products, masked_scores(): jnp.einsum('qhd,khd->hqk', query_block, keys, preferred_element_type=jnp....  134 us
    dot_general x6, matrix products, one_block(): jnp.einsum('qhd,khd->hqk', grad_block, values, preferred_element_type=jnp...  102 us
    psum x8, blocking collectives, token_total(): return lax.psum(partial_value, 'mp')  94.6 us
    dot_general x6, matrix products, one_block(): jnp.einsum('hqk,qhd->khd', probs.astype(jnp.bfloat16), grad_block, prefer...  81.8 us
    dot_general x6, matrix products, one_block(): jnp.einsum('hqk,khd->qhd', probs, values, preferred_element_type=jnp.floa...  74.4 us
    dynamic_update_slice x12, local copies, waits for them, and re-layouts, attend_forward(): outputs, logsum = lax.map(one_block, starts)  72.4 us
  transfers between devices with their start and end apart: 18, of which 15 were waited for; matrix products, arithmetic and copies ran while one was open for 6% of the time, Pallas kernels for 0%

commit v1 on v0

v1 whole, which is shorter than its diff:
```python
import functools
import math

import jax
import jax.numpy as jnp
import numpy as np
from jax import lax
from jax.experimental import pallas as pl
from jax.experimental.pallas import tpu as pltpu
from jax.sharding import Mesh
from jax.sharding import PartitionSpec as P

DK = 64
HALF = DK // 2
EXT = 128
EPSILON = 1e-06
ROPE_BASE = 10000.0
VMEM_LIMIT = 56 * 1024 * 1024
F32 = jnp.float32
BF16 = jnp.bfloat16
DP = ("chip", "core")


def dot(left, right, dims=((1,), (0,)), precision=None):
    return lax.dot_general(
        left, right, (dims, ((), ())), precision=precision, preferred_element_type=F32
    )


NT = ((1,), (1,))
TN = ((0,), (0,))


def grid_params(dims):
    return pltpu.CompilerParams(
        dimension_semantics=("arbitrary",) * dims, vmem_limit_bytes=VMEM_LIMIT
    )


ANY = pl.BlockSpec(memory_space=pl.ANY)


def remote_params(collective, **more):
    return pltpu.CompilerParams(
        collective_id=collective,
        has_side_effects=True,
        vmem_limit_bytes=VMEM_LIMIT,
        **more,
    )


def to_member(source, target, send, receive, member):
    return pltpu.make_async_remote_copy(
        src_ref=source,
        dst_ref=target,
        send_sem=send,
        recv_sem=receive,
        device_id={"mp": member},
        device_id_type=pl.DeviceIdType.MESH,
    )


def flip(index, mask):
    bit = 1
    while bit <= mask:
        if mask & bit:
            index = index + bit - 2 * bit * lax.rem(lax.div(index, bit), 2)
        bit *= 2
    return index


def greet(member):
    pl.semaphore_signal(
        pltpu.get_barrier_semaphore(),
        inc=1,
        device_id={"mp": member},
        device_id_type=pl.DeviceIdType.MESH,
    )


def greet_all(size):
    me = lax.axis_index("mp")
    for k in range(1, size):
        greet(flip(me, k))
    pl.semaphore_wait(pltpu.get_barrier_semaphore(), size - 1)


def greet_line(size):
    me = lax.axis_index("mp")

    @pl.when(me > 0)
    def _():
        greet(me - 1)

    @pl.when(me < size - 1)
    def _():
        greet(me + 1)

    inside = (me > 0) & (me < size - 1)

    @pl.when(inside)
    def _():
        pl.semaphore_wait(pltpu.get_barrier_semaphore(), 2)

    @pl.when(jnp.logical_not(inside))
    def _():
        pl.semaphore_wait(pltpu.get_barrier_semaphore(), 1)


class Exchange:
    def __init__(self, size, source, target, piece, place, send, receive, local):
        me = lax.axis_index("mp")
        self.local = pltpu.make_async_copy(piece(source, me), place(target, me), local)
        self.remote = [
            to_member(
                piece(source, flip(me, k)),
                place(target, me),
                send.at[k],
                receive.at[k],
                flip(me, k),
            )
            for k in range(1, size)
        ]

    def start(self):
        for copy in self.remote:
            copy.start()
        self.local.start()

    def wait(self):
        self.local.wait()
        for copy in self.remote:
            copy.wait()


def exchange_semaphores(size):
    return [
        pltpu.SemaphoreType.DMA((size,)),
        pltpu.SemaphoreType.DMA((size,)),
        pltpu.SemaphoreType.DMA,
    ]


def row_part(rows):
    return lambda ref, j: ref.at[pl.ds(pl.multiple_of(j * rows, rows), rows), :]


def column_part(columns):
    return lambda ref, j: ref.at[:, pl.ds(pl.multiple_of(j * columns, columns), columns)]


def spread_tokens_kernel(size, source, target, send, receive, local):
    greet_all(size)
    tokens, part = source.shape
    exchange = Exchange(
        size,
        source,
        target,
        row_part(tokens // size),
        column_part(part),
        send,
        receive,
        local,
    )
    exchange.start()
    exchange.wait()


def spread_tokens(value, size, collective):
    tokens, part = value.shape
    return pl.pallas_call(
        functools.partial(spread_tokens_kernel, size),
        in_specs=[ANY],
        out_specs=ANY,
        out_shape=jax.ShapeDtypeStruct((tokens // size, size * part), value.dtype),
        scratch_shapes=exchange_semaphores(size),
        compiler_params=remote_params(collective),
        name="spread_tokens",
    )(value)


def gather_parts_kernel(size, chunks, source, target, send_up, send_down, receive, local):
    me = lax.axis_index("mp")
    tokens = source.shape[0]
    rows = tokens // chunks
    greet_line(size)
    own = pltpu.make_async_copy(source, target.at[me], local)
    own.start()

    def hop(origin, chunk, ref, member, send):
        at = pl.ds(chunk * rows, rows)
        return to_member(
            ref.at[at, :],
            target.at[origin, at, :],
            send.at[origin, chunk],
            receive.at[origin, chunk],
            member,
        )

    for chunk in range(chunks):

        @pl.when(me < size - 1)
        def _():
            hop(me, chunk, source, me + 1, send_up).start()

        @pl.when(me > 0)
        def _():
            hop(me, chunk, source, me - 1, send_down).start()

    for distance in range(1, size):
        for chunk in range(chunks):
            below, above = me - distance, me + distance

            @pl.when(below >= 0)
            def _():
                hop(below, chunk, target.at[below], me, send_up).wait_recv()

                @pl.when(me < size - 1)
                def _():
                    hop(below, chunk, target.at[below], me + 1, send_up).start()

            @pl.when(above < size)
            def _():
                hop(above, chunk, target.at[above], me, send_down).wait_recv()

                @pl.when(me > 0)
                def _():
                    hop(above, chunk, target.at[above], me - 1, send_down).start()

    own.wait()
    for distance in range(size):
        for chunk in range(chunks):
            below, above = me - distance, me + distance

            @pl.when((below >= 0) & (me < size - 1))
            def _():
                hop(below, chunk, source, me + 1, send_up).wait_send()

            @pl.when((above < size) & (me > 0))
            def _():
                hop(above, chunk, source, me - 1, send_down).wait_send()


def gather_parts(value, size, collective):
    tokens, part = value.shape
    chunks = 6
    semaphores = pltpu.SemaphoreType.DMA((size, chunks))
    return pl.pallas_call(
        functools.partial(gather_parts_kernel, size, chunks),
        in_specs=[ANY],
        out_specs=ANY,
        out_shape=jax.ShapeDtypeStruct((size, tokens, part), value.dtype),
        scratch_shapes=[semaphores, semaphores, semaphores, pltpu.SemaphoreType.DMA],
        compiler_params=remote_params(collective),
        name="gather_parts",
    )(value)


def sum_parts_kernel(size, chunks, term, out, up, down, sent_up, sent_down, got_up, got_down):
    me = lax.axis_index("mp")
    rows = out.shape[0] // chunks
    greet_line(size)

    def hop(slots, goal, chunk, member, send, receive):
        at = pl.ds(chunk * rows, rows)
        return to_member(
            slots.at[goal, at, :],
            slots.at[goal, at, :],
            send.at[goal, chunk],
            receive.at[goal, chunk],
            member,
        )

    for order in range(size - 1):
        for chunk in range(chunks):
            at = pl.ds(chunk * rows, rows)
            for slots, goal, ahead, first, step, send, receive in (
                (up, size - 1 - order, me < size - 1 - order, me == 0, 1, sent_up, got_up),
                (down, order, me > order, me == size - 1, -1, sent_down, got_down),
            ):

                @pl.when(ahead & first)
                def _():
                    slots[goal, at, :] = term[goal, at, :]

                @pl.when(ahead & jnp.logical_not(first))
                def _():
                    hop(slots, goal, chunk, me, send, receive).wait_recv()
                    slots[goal, at, :] = (
                        slots[goal, at, :].astype(F32) + term[goal, at, :].astype(F32)
                    ).astype(BF16)

                @pl.when(ahead)
                def _():
                    hop(slots, goal, chunk, me + step, send, receive).start()

    for chunk in range(chunks):
        at = pl.ds(chunk * rows, rows)
        out[at, :] = term[me, at, :].astype(F32)

        @pl.when(me > 0)
        def _():
            hop(up, me, chunk, me, sent_up, got_up).wait_recv()
            out[at, :] += up[me, at, :].astype(F32)

        @pl.when(me < size - 1)
        def _():
            hop(down, me, chunk, me, sent_down, got_down).wait_recv()
            out[at, :] += down[me, at, :].astype(F32)

    for order in range(size - 1):
        for chunk in range(chunks):

            @pl.when(me < size - 1 - order)
            def _():
                hop(up, size - 1 - order, chunk, me, sent_up, got_up).wait_send()

            @pl.when(me > order)
            def _():
                hop(down, order, chunk, me, sent_down, got_down).wait_send()


def sum_parts(term, collective):
    size, tokens, part = term.shape
    chunks = 6
    semaphores = pltpu.SemaphoreType.DMA((size, chunks))
    return pl.pallas_call(
        functools.partial(sum_parts_kernel, size, chunks),
        in_specs=[pl.BlockSpec(memory_space=pltpu.VMEM)],
        out_specs=pl.BlockSpec(memory_space=pltpu.VMEM),
        out_shape=jax.ShapeDtypeStruct((tokens, part), F32),
        scratch_shapes=[pltpu.VMEM((size, tokens, part), BF16)] * 2 + [semaphores] * 4,
        compiler_params=remote_params(collective),
        name="sum_parts",
    )(term)


def paired_place(heads):
    head, feature = np.divmod(np.arange(heads * DK), DK)
    return (feature // HALF) * (heads * HALF) + head * HALF + feature % HALF


def placing_matrix(place, heads):
    head, feature = np.divmod(np.arange(heads * DK), DK)
    matrix = np.zeros((heads * DK, heads * EXT), np.float32)
    matrix[place, head * EXT + feature] = 1
    return matrix


def head_sum_matrix(heads):
    lane = np.arange(heads * HALF) // HALF
    return (lane[:, None] == lane[None, :]).astype(np.float32)


def project_kernel(
    wide, weight, cosine, sine, gain, place_pair, place_plain, sums, q, k, v, rq, rk
):
    parts = wide.shape[0]
    heads = q.shape[0]
    pair = heads * HALF
    width = heads * DK
    raw = dot(wide[0], weight[0])
    for part in range(1, parts):
        raw += dot(wide[part], weight[part])
    rows = raw.shape[0]
    lane = lax.broadcasted_iota(jnp.int32, (rows, EXT), 1)
    cos = cosine[...]
    sin = sine[...]
    gain_first = gain[:, :pair]
    gain_second = gain[:, pair:]
    for offset, out, scale_out, factor in ((0, q, rq, math.sqrt(DK)), (width, k, rk, 1.0)):
        first = raw[:, offset : offset + pair]
        second = raw[:, offset + pair : offset + width]
        turned_first = first * cos - second * sin
        turned_second = second * cos + first * sin
        total = dot(
            turned_first * turned_first + turned_second * turned_second,
            sums[...],
            precision=lax.Precision.HIGHEST,
        )
        scale = lax.rsqrt(total + EPSILON)
        scale_out[...] = scale
        both = jnp.concatenate(
            [turned_first * scale * gain_first, turned_second * scale * gain_second], axis=1
        ).astype(BF16)
        padded = dot(both, place_pair[...]) * factor
        for head in range(heads):
            piece = padded[:, head * EXT : (head + 1) * EXT]
            if factor == 1.0:
                piece = jnp.where(lane < DK, piece, 1.0)
            out[head] = piece.astype(BF16)
    padded = dot(raw[:, 2 * width :].astype(BF16), place_plain[...])
    for head in range(heads):
        piece = padded[:, head * EXT : (head + 1) * EXT]
        v[head] = jnp.where(lane < DK, piece, 1.0).astype(BF16)


def project(wide, weight, cosine, sine, gain, place_pair, place_plain, sums):
    parts, tokens, part = wide.shape
    width = gain.shape[1]
    heads = width // DK
    block = min(512, tokens)
    padded = jax.ShapeDtypeStruct((heads, tokens, EXT), BF16)
    scale = jax.ShapeDtypeStruct((tokens, heads * HALF), F32)

    def whole(array):
        return pl.BlockSpec(array.shape, lambda i: (0,) * array.ndim)

    rows = pl.BlockSpec((block, heads * HALF), lambda i: (i, 0))
    headed = pl.BlockSpec((heads, block, EXT), lambda i: (0, i, 0))
    return pl.pallas_call(
        project_kernel,
        grid=(tokens // block,),
        in_specs=[
            pl.BlockSpec((parts, block, part), lambda i: (0, i, 0)),
            whole(weight),
            rows,
            rows,
            whole(gain),
            whole(place_pair),
            whole(place_plain),
            whole(sums),
        ],
        out_specs=[headed, headed, headed, rows, rows],
        out_shape=[padded, padded, padded, scale, scale],
        compiler_params=grid_params(1),
        cost_estimate=pl.CostEstimate(
            flops=2 * tokens * parts * part * width * 3,
            bytes_accessed=20 << 20,
            transcendentals=0,
        ),
        name="project",
    )(wide, weight, cosine, sine, gain, place_pair, place_plain, sums)


def split_three(value):
    high = value.astype(BF16).astype(F32)
    rest = value - high
    middle = rest.astype(BF16).astype(F32)
    return high, middle, rest - middle


def attend_kernel(low, q, k, v, qdoc, kdoc, collect, attended, qback, acc):
    heads, rows, _ = q.shape
    block = kdoc.shape[2]
    index = pl.program_id(0)
    acc[...] = jnp.zeros_like(acc)

    def step(j, diagonal):
        slots = pl.ds(pl.multiple_of(j * block, block), block)
        mask = qdoc[...] == kdoc[j]
        if diagonal:
            row = lax.broadcasted_iota(jnp.int32, (rows, block), 0)
            column = lax.broadcasted_iota(jnp.int32, (rows, block), 1)
            mask = (mask & (column < row)) | (column == row)
        for head in range(heads):
            scores = dot(q[head], k[head, slots, :], NT)
            weight = jnp.where(mask, jnp.exp(scores), 0.0).astype(BF16)
            acc[head] += dot(weight, v[head, slots, :])

    def earlier(j, carry):
        step(j, False)
        return carry

    lax.fori_loop(low[index], index, earlier, 0)
    step(index, True)

    lane = lax.broadcasted_iota(jnp.int32, (rows, EXT), 1)
    merged = jnp.zeros((rows, heads * DK), F32)
    for head in range(heads):
        both = acc[head]
        total = pltpu.roll(both, DK, 1)
        output = jnp.where(lane < DK, both / total, 0.0).astype(BF16)
        merged += dot(output, collect[head])
        high, middle, rest = split_three(-jnp.log(both))
        qback[head] = jnp.where(
            lane < DK,
            q[head].astype(F32),
            jnp.where(
                lane == DK,
                high,
                jnp.where(lane == DK + 1, middle, jnp.where(lane == DK + 2, rest, 0.0)),
            ),
        ).astype(BF16)
    attended[...] = merged.astype(BF16)


def attend(low, q, k, v, qdoc, kdoc, collect):
    heads, tokens, _ = q.shape
    block = kdoc.shape[2]
    width = heads * DK

    def whole(array):
        return pl.BlockSpec(array.shape, lambda i, low: (0,) * array.ndim)

    headed = pl.BlockSpec((heads, block, EXT), lambda i, low: (0, i, 0))
    return pl.pallas_call(
        attend_kernel,
        grid_spec=pltpu.PrefetchScalarGridSpec(
            num_scalar_prefetch=1,
            grid=(tokens // block,),
            in_specs=[
                headed,
                whole(k),
                whole(v),
                pl.BlockSpec((block, 1), lambda i, low: (i, 0)),
                whole(kdoc),
                whole(collect),
            ],
            out_specs=[pl.BlockSpec((block, width), lambda i, low: (i, 0)), headed],
            scratch_shapes=[pltpu.VMEM((heads, block, EXT), F32)],
        ),
        out_shape=[
            jax.ShapeDtypeStruct((tokens, width), BF16),
            jax.ShapeDtypeStruct((heads, tokens, EXT), BF16),
        ],
        compiler_params=grid_params(1),
        cost_estimate=pl.CostEstimate(
            flops=40_000_000_000, bytes_accessed=16 << 20, transcendentals=0
        ),
        name="attend",
    )(low, q, k, v, qdoc, kdoc, collect)


def gather_heads(padded, matrix, heads):
    total = None
    for head in range(heads):
        value = padded[head]
        high = value.astype(BF16)
        rest = (value - high.astype(F32)).astype(BF16)
        term = dot(high, matrix[head]) + dot(rest, matrix[head])
        total = term if total is None else total + term
    return total


def unrope(grad, unit, gain, scale, cos, sin, sums):
    pair = cos.shape[1]
    grad_gain = jnp.sum(grad * unit, axis=0, keepdims=True)
    dy = grad * gain
    prod = dy * unit
    total = dot(prod[:, :pair] + prod[:, pair:], sums, precision=lax.Precision.HIGHEST)
    first = scale * (dy[:, :pair] - unit[:, :pair] * total)
    second = scale * (dy[:, pair:] - unit[:, pair:] * total)
    raw = jnp.concatenate([first * cos + second * sin, second * cos - first * sin], axis=1)
    return raw.astype(BF16), grad_gain


def attend_back_kernel(
    low,
    qback,
    dout,
    attended,
    k,
    v,
    qdoc,
    kdoc,
    cosine,
    sine,
    rq,
    rk,
    gain,
    weight,
    place_plain,
    collect_plain,
    collect_pair,
    sums,
    dq_out,
    dk_out,
    dv_out,
    term_out,
    gain_out,
    dk,
    dv,
    dq,
    dox,
    dq_low,
):
    heads, rows, _ = qback.shape
    steps = pl.num_programs(0) // 2
    step_at = pl.program_id(0)
    width = heads * DK
    scale = math.sqrt(DK)

    @pl.when(step_at == 0)
    def _():
        dk[...] = jnp.zeros_like(dk)
        dv[...] = jnp.zeros_like(dv)
        gain_out[...] = jnp.zeros_like(gain_out)

    @pl.when(step_at < steps)
    def _():
        index = step_at
        lane = lax.broadcasted_iota(jnp.int32, (rows, EXT), 1)
        spread_grad = dot(dout[...], place_plain[...])
        spread_out = dot(attended[...], place_plain[...])
        for head in range(heads):
            piece = spread_grad[:, head * EXT : (head + 1) * EXT]
            other = spread_out[:, head * EXT : (head + 1) * EXT]
            delta = jnp.sum(piece * other, axis=1, keepdims=True)
            high, middle, rest = split_three(-delta)
            dox[head] = jnp.where(
                lane < DK,
                piece,
                jnp.where(
                    lane == DK,
                    high,
                    jnp.where(lane == DK + 1, middle, jnp.where(lane == DK + 2, rest, 0.0)),
                ),
            ).astype(BF16)
        dq[...] = jnp.zeros_like(dq)

        def step(j, diagonal):
            slots = pl.ds(pl.multiple_of(j * rows, rows), rows)
            mask = kdoc[slots, :] == qdoc[0]
            if diagonal:
                key = lax.broadcasted_iota(jnp.int32, (rows, rows), 0)
                query = lax.broadcasted_iota(jnp.int32, (rows, rows), 1)
                mask = (mask & (key < query)) | (key == query)
            for head in range(heads):
                keys = k[head, slots, :]
                scores = dot(keys, qback[head], NT)
                probs = jnp.where(mask, jnp.exp(scores), 0.0)
                dv[head, slots, :] += dot(probs.astype(BF16), dox[head])
                dprobs = dot(v[head, slots, :], dox[head], NT)
                dscores = (probs * dprobs).astype(BF16)
                dk[head, slots, :] += dot(dscores, qback[head])
                dq[head] += dot(dscores, keys, TN)

        def earlier(j, carry):
            step(j, False)
            return carry

        lax.fori_loop(low[index], index, earlier, 0)
        step(index, True)

        grad = gather_heads(dq, collect_pair, heads) * scale
        query = dot(qback[0], collect_pair[0])
        for head in range(1, heads):
            query += dot(qback[head], collect_pair[head])
        unit = query * (1.0 / scale) / gain[...]
        raw, grad_gain = unrope(
            grad, unit, gain[...], rq[...], cosine[...], sine[...], sums[...]
        )
        gain_out[...] += grad_gain
        dq_out[...] = raw
        dq_low[pl.ds(pl.multiple_of(index * rows, rows), rows), :] = raw

    @pl.when(step_at >= steps)
    def _():
        index = step_at - steps
        slots = pl.ds(pl.multiple_of(index * rows, rows), rows)
        grad = gather_heads([dk[head, slots, :] for head in range(heads)], collect_pair, heads)
        keys = dot(k[0, slots, :], collect_pair[0])
        for head in range(1, heads):
            keys += dot(k[head, slots, :], collect_pair[head])
        raw, grad_gain = unrope(
            grad, keys / gain[...], gain[...], rk[...], cosine[...], sine[...], sums[...]
        )
        gain_out[...] += grad_gain
        dk_out[...] = raw
        dvalues = gather_heads(
            [dv[head, slots, :] for head in range(heads)], collect_plain, heads
        ).astype(BF16)
        dv_out[...] = dvalues
        dquery = dq_low[slots, :]
        for part in range(weight.shape[0]):
            term = dot(dquery, weight[part, :, :width], NT)
            term += dot(raw, weight[part, :, width : 2 * width], NT)
            term += dot(dvalues, weight[part, :, 2 * width :], NT)
            term_out[part] = term.astype(BF16)


def attend_back(
    low,
    qback,
    dout,
    attended,
    k,
    v,
    qdoc,
    kdoc,
    cosine,
    sine,
    rq,
    rk,
    gain,
    weight,
    place_plain,
    collect_plain,
    collect_pair,
    sums,
):
    heads, tokens, _ = k.shape
    block = qdoc.shape[2]
    width = heads * DK
    steps = tokens // block
    parts, part = weight.shape[:2]

    def whole(array):
        return pl.BlockSpec(array.shape, lambda i, low: (0,) * array.ndim)

    def now(i):
        return jnp.minimum(i, steps - 1)

    def after(i):
        return jnp.maximum(i - steps, 0)

    def both(i):
        return lax.rem(i, steps)

    def rows(columns, at):
        return pl.BlockSpec((block, columns), lambda i, low: (at(i), 0))

    return pl.pallas_call(
        attend_back_kernel,
        grid_spec=pltpu.PrefetchScalarGridSpec(
            num_scalar_prefetch=1,
            grid=(2 * steps,),
            in_specs=[
                pl.BlockSpec((heads, block, EXT), lambda i, low: (0, now(i), 0)),
                rows(width, now),
                rows(width, now),
                whole(k),
                whole(v),
                pl.BlockSpec((1, 1, block), lambda i, low: (now(i), 0, 0)),
                whole(kdoc),
                rows(width // 2, both),
                rows(width // 2, both),
                rows(width // 2, now),
                rows(width // 2, after),
                whole(gain),
                whole(weight),
                whole(place_plain),
                whole(collect_plain),
                whole(collect_pair),
                whole(sums),
            ],
            out_specs=[
                rows(width, now),
                rows(width, after),
                rows(width, after),
                pl.BlockSpec((parts, block, part), lambda i, low: (0, after(i), 0)),
                pl.BlockSpec((1, width), lambda i, low: (0, 0)),
            ],
            scratch_shapes=[
                pltpu.VMEM((heads, tokens, EXT), F32),
                pltpu.VMEM((heads, tokens, EXT), F32),
                pltpu.VMEM((heads, block, EXT), F32),
                pltpu.VMEM((heads, block, EXT), BF16),
                pltpu.VMEM((tokens, width), BF16),
            ],
        ),
        out_shape=[
            jax.ShapeDtypeStruct((tokens, width), BF16),
            jax.ShapeDtypeStruct((tokens, width), BF16),
            jax.ShapeDtypeStruct((tokens, width), BF16),
            jax.ShapeDtypeStruct((parts, tokens, part), BF16),
            jax.ShapeDtypeStruct((1, width), F32),
        ],
        compiler_params=grid_params(1),
        cost_estimate=pl.CostEstimate(
            flops=80_000_000_000, bytes_accessed=30 << 20, transcendentals=0
        ),
        name="attend_back",
    )(
        low,
        qback,
        dout,
        attended,
        k,
        v,
        qdoc,
        kdoc,
        cosine,
        sine,
        rq,
        rk,
        gain,
        weight,
        place_plain,
        collect_plain,
        collect_pair,
        sums,
    )


def whole_matrix(ref):
    _, chips, rows, units = ref.shape
    return ref[...].reshape(chips * rows, units)


def first_step():
    return (pl.program_id(0) == 0) & (pl.program_id(1) == 0)


def last_step():
    return (pl.program_id(0) == pl.num_programs(0) - 1) & (
        pl.program_id(1) == pl.num_programs(1) - 1
    )


def feed_kernel(
    size,
    x,
    w_up,
    w_gate,
    w_down,
    s_u,
    s_v,
    cotangent,
    up_out,
    gate_out,
    units_out,
    branch,
    spread,
    acc,
    send,
    receive,
    local,
):
    exchange = Exchange(
        size,
        cotangent,
        spread,
        row_part(spread.shape[0]),
        column_part(cotangent.shape[1]),
        send,
        receive,
        local,
    )

    @pl.when(first_step())
    def _():
        greet_all(size)
        exchange.start()

    part = pl.program_id(1)
    up = dot(x[...], whole_matrix(w_up))
    gate = dot(x[...], whole_matrix(w_gate))
    up_out[0] = up.astype(BF16)
    gate_out[0] = gate.astype(BF16)
    scaled = gate * s_v[0]
    units = (up * s_u[0] * (scaled / (1.0 + jnp.exp(-scaled)))).astype(BF16)
    units_out[0] = units
    term = dot(units, whole_matrix(w_down), NT)

    @pl.when(part == 0)
    def _():
        acc[...] = term

    @pl.when(part > 0)
    def _():
        acc[...] += term

    @pl.when(part == pl.num_programs(1) - 1)
    def _():
        branch[...] = acc[...].astype(BF16)

    @pl.when(last_step())
    def _():
        exchange.wait()


def packed_specs(packed, width):
    _, chips, _, units = packed.shape
    return [
        pl.BlockSpec((1, chips, width // chips, units), lambda t, m, w=w: (m, 0, w, 0))
        for w in range(3)
    ]


def feed(x, packed, s_u, s_v, cotangent, collective):
    tokens, width = x.shape
    parts, _, _, units = packed.shape
    size = parts
    block = min(512, tokens)
    rows = pl.BlockSpec((block, width), lambda t, m: (t, 0))
    vector = pl.BlockSpec((1, 1, units), lambda t, m: (m, 0, 0))
    piece = pl.BlockSpec((1, block, units), lambda t, m: (m, t, 0))
    hidden = jax.ShapeDtypeStruct((parts, tokens, units), BF16)
    slots, part = cotangent.shape
    return pl.pallas_call(
        functools.partial(feed_kernel, size),
        grid=(tokens // block, parts),
        in_specs=[rows, *packed_specs(packed, width), vector, vector, ANY],
        out_specs=[piece, piece, piece, rows, ANY],
        out_shape=[
            hidden,
            hidden,
            hidden,
            jax.ShapeDtypeStruct((tokens, width), BF16),
            jax.ShapeDtypeStruct((slots // size, size * part), BF16),
        ],
        scratch_shapes=[pltpu.VMEM((block, width), F32), *exchange_semaphores(size)],
        compiler_params=remote_params(collective),
        cost_estimate=pl.CostEstimate(
            flops=6 * tokens * width * parts * units, bytes_accessed=60 << 20, transcendentals=0
        ),
        name="feed",
    )(x, packed, packed, packed, s_u, s_v, cotangent)


def feed_back_kernel(
    size,
    dbranch,
    w_up,
    w_gate,
    w_down,
    s_u,
    s_v,
    up_in,
    gate_in,
    result,
    dup_out,
    dgate_out,
    dx,
    grad_u,
    grad_v,
    spread,
    acc,
    sum_u,
    sum_v,
    send,
    receive,
    local,
):
    exchange = Exchange(
        size,
        result,
        spread,
        column_part(spread.shape[1]),
        row_part(result.shape[0]),
        send,
        receive,
        local,
    )

    @pl.when(first_step())
    def _():
        greet_all(size)
        exchange.start()

    block = pl.program_id(0)
    part = pl.program_id(1)
    dunits = dot(dbranch[...], whole_matrix(w_down))
    up = up_in[0].astype(F32)
    gate = gate_in[0].astype(F32)
    scaled = gate * s_v[0]
    sigmoid = 1.0 / (1.0 + jnp.exp(-scaled))
    silu = scaled * sigmoid
    slope = sigmoid * (1.0 + scaled - silu)
    through_up = dunits * silu
    through_gate = dunits * up * s_u[0] * slope
    dup = (through_up * s_u[0]).astype(BF16)
    dgate = (through_gate * s_v[0]).astype(BF16)
    dup_out[0] = dup
    dgate_out[0] = dgate
    term = dot(dup, whole_matrix(w_up), NT) + dot(dgate, whole_matrix(w_gate), NT)
    part_u = jnp.sum(through_up * up, axis=0, keepdims=True)
    part_v = jnp.sum(through_gate * gate, axis=0, keepdims=True)

    @pl.when(block == 0)
    def _():
        sum_u[part] = part_u
        sum_v[part] = part_v

    @pl.when(block > 0)
    def _():
        sum_u[part] += part_u
        sum_v[part] += part_v

    @pl.when(part == 0)
    def _():
        acc[...] = term

    @pl.when(part > 0)
    def _():
        acc[...] += term

    @pl.when(part == pl.num_programs(1) - 1)
    def _():
        dx[...] = acc[...].astype(BF16)

    @pl.when(last_step())
    def _():
        grad_u[...] = sum_u[...]
        grad_v[...] = sum_v[...]
        exchange.wait()


def feed_back(dbranch, packed, s_u, s_v, up, gate, result, collective):
    tokens, width = dbranch.shape
    parts, _, _, units = packed.shape
    size = parts
    block = min(512, tokens)
    rows = pl.BlockSpec((block, width), lambda t, m: (t, 0))
    vector = pl.BlockSpec((1, 1, units), lambda t, m: (m, 0, 0))
    piece = pl.BlockSpec((1, block, units), lambda t, m: (m, t, 0))
    vectors = pl.BlockSpec((parts, 1, units), lambda t, m: (0, 0, 0))
    hidden = jax.ShapeDtypeStruct((parts, tokens, units), BF16)
    sums = jax.ShapeDtypeStruct((parts, 1, units), F32)
    mine = result.shape[0]
    return pl.pallas_call(
        functools.partial(feed_back_kernel, size),
        grid=(tokens // block, parts),
        in_specs=[rows, *packed_specs(packed, width), vector, vector, piece, piece, ANY],
        out_specs=[piece, piece, rows, vectors, vectors, ANY],
        out_shape=[
            hidden,
            hidden,
            jax.ShapeDtypeStruct((tokens, width), BF16),
            sums,
            sums,
            jax.ShapeDtypeStruct((size * mine, width // size), BF16),
        ],
        scratch_shapes=[
            pltpu.VMEM((block, width), F32),
            pltpu.VMEM((parts, 1, units), F32),
            pltpu.VMEM((parts, 1, units), F32),
            *exchange_semaphores(size),
        ],
        compiler_params=remote_params(collective),
        cost_estimate=pl.CostEstimate(
            flops=6 * tokens * width * parts * units, bytes_accessed=70 << 20, transcendentals=0
        ),
        name="feed_back",
    )(dbranch, packed, packed, packed, s_u, s_v, up, gate, result)


def feed_grads_kernel(
    size,
    x,
    dbranch,
    dup,
    dgate,
    units,
    dmerged,
    grads,
    dattended,
    x_turned,
    d_turned,
    send,
    receive,
    local,
):
    exchange = Exchange(
        size,
        dmerged,
        dattended,
        column_part(dattended.shape[1]),
        row_part(dmerged.shape[0]),
        send,
        receive,
        local,
    )

    @pl.when(first_step())
    def _():
        greet_all(size)
        exchange.start()
        x_turned[...] = x[...].T
        d_turned[...] = dbranch[...].T

    _, chips, rows, _ = grads.shape
    for which, left, right in (
        (0, x_turned, dup),
        (1, x_turned, dgate),
        (2, d_turned, units),
    ):

        @pl.when(pl.program_id(0) == which)
        def _():
            total = dot(left[...], right[0])
            grads[0] = total.astype(BF16).reshape(chips, rows, total.shape[1])

    @pl.when(last_step())
    def _():
        exchange.wait()


def feed_grads(x, dbranch, dup, dgate, units_in, dmerged, chips, collective):
    tokens, width = x.shape
    parts, _, units = dup.shape
    size = parts
    rows = width // chips
    mine = dmerged.shape[0]
    whole = pl.BlockSpec((tokens, width), lambda w, m: (0, 0))

    def piece(which):
        def at(w, m):
            return (jnp.where(w == which, m, jnp.where(w < which, 0, parts - 1)), 0, 0)

        return pl.BlockSpec((1, tokens, units), at)

    return pl.pallas_call(
        functools.partial(feed_grads_kernel, size),
        grid=(3, parts),
        in_specs=[whole, whole, piece(0), piece(1), piece(2), ANY],
        out_specs=[pl.BlockSpec((1, chips, rows, units), lambda w, m: (m, 0, w, 0)), ANY],
        out_shape=[
            jax.ShapeDtypeStruct((parts, chips, 3 * rows, units), BF16),
            jax.ShapeDtypeStruct((size * mine, width // size), BF16),
        ],
        scratch_shapes=[
            pltpu.VMEM((width, tokens), BF16),
            pltpu.VMEM((width, tokens), BF16),
            *exchange_semaphores(size),
        ],
        compiler_params=remote_params(collective),
        cost_estimate=pl.CostEstimate(
            flops=6 * tokens * width * parts * units, bytes_accessed=40 << 20, transcendentals=0
        ),
        name="feed_grads",
    )(x, dbranch, dup, dgate, units_in, dmerged)


def rope_tables(positions, head_size):
    half_size = head_size // 2
    freq_index = jnp.arange(half_size, dtype=F32)
    inverse = jnp.exp(freq_index * (-2.0 * math.log(ROPE_BASE) / head_size))
    angles = positions.astype(F32)[..., None] * inverse
    return (jnp.cos(angles), jnp.sin(angles))


def document_starts(doc_ids):
    slot_index = jnp.arange(doc_ids.shape[-1], dtype=jnp.int32)
    earlier = jnp.concatenate([doc_ids[..., :1] - 1, doc_ids[..., :-1]], axis=-1)
    starts = jnp.where(doc_ids != earlier, slot_index, jnp.zeros_like(slot_index))
    return lax.cummax(starts, axis=starts.ndim - 1)


def row_scale(value):
    return lax.rsqrt(jnp.sum(value * value, axis=-1, keepdims=True) + EPSILON)


def residual_forward(resid, branch, alpha):
    branch_scale = row_scale(branch)
    unit = branch * branch_scale
    mixed = resid + alpha * (unit - resid)
    mixed_scale = row_scale(mixed)
    return (mixed * mixed_scale, (unit, branch_scale, mixed_scale))


def residual_backward(grad_out, result, resid, alpha, kept):
    unit, branch_scale, mixed_scale = kept
    grad_mixed = mixed_scale * (
        grad_out - result * jnp.sum(grad_out * result, axis=-1, keepdims=True)
    )
    grad_alpha = jnp.sum(grad_mixed * (unit - resid), axis=0)
    grad_resid = grad_mixed * (1.0 - alpha)
    grad_unit = grad_mixed * alpha
    grad_branch = branch_scale * (
        grad_unit - unit * jnp.sum(grad_unit * unit, axis=-1, keepdims=True)
    )
    return (grad_resid, grad_branch, grad_alpha)


def other_core(value):
    return lax.ppermute(value, "core", [(0, 1), (1, 0)])


def make_on_device(chips, size):
    def on_device(
        hidden,
        wq,
        wk,
        wv,
        wo,
        w_up,
        w_gate,
        w_down,
        s_qk,
        s_u,
        s_v,
        alpha_a,
        alpha_m,
        doc_ids,
        valid,
        cotangent,
    ):
        _, slots, part = hidden.shape
        width = part * size
        heads = s_qk.shape[0] // DK
        rows = wq.shape[0]
        units = w_up.shape[1] // 2
        mine = slots // size
        block = min(512, slots)
        me = lax.axis_index("mp")
        core = lax.axis_index("core")
        everyone = ("mp", "chip", "core")

        place = paired_place(heads)
        in_pairs = (
            lambda w: w.reshape(w.shape[0], heads, 2, HALF)
            .transpose(0, 2, 1, 3)
            .reshape(w.shape[0], heads * DK)
        )
        low_qkv = jnp.concatenate([in_pairs(wq), in_pairs(wk), wv], axis=1).astype(BF16)
        full_qkv = lax.all_gather(low_qkv, DP, axis=0, tiled=True).reshape(size, part, 3 * part)

        stacked = jnp.stack([w_up, w_gate, w_down.T]).astype(BF16).reshape(3, rows, 2, units)
        keep = lax.dynamic_index_in_dim(stacked, core, 2, keepdims=False)
        give = lax.dynamic_index_in_dim(stacked, 1 - core, 2, keepdims=False)
        low_wo = wo.astype(BF16).T.reshape(rows // 2, 2 * part)
        given = jnp.concatenate([give.reshape(3 * rows, units), low_wo])
        got = other_core(given)

        def in_order(own, other):
            return jnp.where(core == 0, jnp.stack([own, other], 1), jnp.stack([other, own], 1))

        pair = in_order(keep, got[: 3 * rows].reshape(3, rows, units))
        pair_wo = in_order(low_wo[None], got[3 * rows :][None])
        packed = jnp.concatenate([pair.reshape(6 * rows, units), pair_wo.reshape(rows, units)])
        packed = lax.all_gather(packed, ("mp", "chip"), axis=0).reshape(
            size, chips, 7 * rows, units
        )
        wide = gather_parts(hidden[0].astype(BF16), size, 0)
        full_wo = packed[:, :, 6 * rows :].reshape(size, width, part)
        vectors = jnp.concatenate([s_u, s_v * math.sqrt(width), alpha_a, alpha_m])
        vectors = lax.all_gather(vectors, "mp", axis=0)
        s_up = lax.dynamic_slice_in_dim(vectors[:, : 2 * units], core * units, units, 1)
        s_gate = lax.dynamic_slice_in_dim(
            vectors[:, 2 * units : 4 * units], core * units, units, 1
        )
        s_up = s_up[:, None, :]
        s_gate = s_gate[:, None, :]
        alpha_attn = vectors[:, 4 * units : 4 * units + part].reshape(width)
        alpha_mlp = vectors[:, 4 * units + part :].reshape(width)

        docs = doc_ids[0]
        starts = document_starts(docs)
        slot = jnp.arange(slots, dtype=jnp.int32)
        cosine, sine = rope_tables(slot - starts, DK)
        cosine = jnp.tile(cosine, (1, heads))
        sine = jnp.tile(sine, (1, heads))
        low = starts[::block] // block
        key_docs = jnp.where(valid[0] == 1, docs, -1)
        to_pair = placing_matrix(place, heads)
        to_plain = placing_matrix(np.arange(heads * DK), heads)
        place_pair = jnp.asarray(to_pair, BF16)
        place_plain = jnp.asarray(to_plain, BF16)
        collect_pair = jnp.asarray(to_pair.T.reshape(heads, EXT, heads * DK), BF16)
        collect_plain = jnp.asarray(to_plain.T.reshape(heads, EXT, heads * DK), BF16)
        sums = jnp.asarray(head_sum_matrix(heads))
        gain = in_pairs(s_qk[None, :])

        q, k, v, rq, rk = project(
            wide, full_qkv, cosine, sine, gain, place_pair, place_plain, sums
        )
        attended, qback = attend(
            low,
            q,
            k,
            v,
            docs[:, None],
            key_docs.reshape(slots // block, 1, block),
            collect_plain,
        )
        merged = spread_tokens(attended, size, 1)
        resid = lax.dynamic_slice_in_dim(wide, me * mine, mine, 1)
        resid = resid.transpose(1, 0, 2).reshape(mine, width).astype(F32)
        merged_parts = merged.reshape(mine, size, part)
        branch_attn = jnp.einsum("tmh,mdh->td", merged_parts, full_wo, preferred_element_type=F32)
        middle, kept_attn = residual_forward(resid, branch_attn, alpha_attn)

        middle_low = middle.astype(BF16)
        x = jnp.concatenate([middle_low, other_core(middle_low)])
        up, gate, hidden_units, down_term, spread_cot = feed(
            x, packed, s_up, s_gate, cotangent[0].astype(BF16), 2
        )
        branch_mlp = down_term[:mine].astype(F32) + other_core(down_term[mine:]).astype(F32)
        result, kept_mlp = residual_forward(middle, branch_mlp, alpha_mlp)

        grad_middle, grad_branch_mlp, grad_alpha_mlp = residual_backward(
            spread_cot.astype(F32), result, middle, alpha_mlp, kept_mlp
        )
        grad_branch_mlp = grad_branch_mlp.astype(BF16)
        dbranch = jnp.concatenate([grad_branch_mlp, other_core(grad_branch_mlp)])
        dup, dgate, dx, grad_u, grad_v, out_low = feed_back(
            dbranch, packed, s_up, s_gate, up, gate, result.astype(BF16), 3
        )
        out_hidden = out_low.astype(F32)
        grad_middle = (
            grad_middle + dx[:mine].astype(F32) + other_core(dx[mine:]).astype(F32)
        )

        grad_resid, grad_branch_attn, grad_alpha_attn = residual_backward(
            grad_middle, middle, resid, alpha_attn, kept_attn
        )
        grad_branch_attn = grad_branch_attn.astype(BF16)
        grad_merged = jnp.einsum(
            "td,mdh->tmh", grad_branch_attn, full_wo, preferred_element_type=F32
        ).astype(BF16)
        grads, dattended = feed_grads(
            x, dbranch, dup, dgate, hidden_units, grad_merged.reshape(mine, width), chips, 4
        )
        total = lax.psum_scatter(
            grads.reshape(size * chips, 6 * rows, units), ("mp", "chip"), scatter_dimension=0
        )
        total = total.reshape(3, 2, rows, units)
        keep = lax.dynamic_index_in_dim(total, core, 1, keepdims=False)
        got = other_core(lax.dynamic_index_in_dim(total, 1 - core, 1, keepdims=False))
        owned = jnp.where(
            core == 0,
            jnp.concatenate([keep, got], axis=2),
            jnp.concatenate([got, keep], axis=2),
        ).astype(F32)
        owned_upward, owned_gating, owned_downward = owned[0], owned[1], owned[2].T
        grad_wo = jnp.einsum(
            "td,tmh->mdh", grad_branch_attn, merged_parts, preferred_element_type=F32
        ).astype(BF16)
        owned_output = lax.psum_scatter(
            grad_wo.reshape(size * chips * 2, rows, part), everyone, scatter_dimension=0
        )
        owned_output = owned_output.astype(F32).T
        dq, dk, dv, term, grad_gain = attend_back(
            low,
            qback,
            dattended,
            attended,
            k,
            v,
            docs.reshape(slots // block, 1, block),
            key_docs[:, None],
            cosine,
            sine,
            rq,
            rk,
            gain,
            full_qkv,
            place_plain,
            collect_plain,
            collect_pair,
            sums,
        )
        own = lax.dynamic_slice_in_dim(term, me * mine, mine, 1).astype(F32)
        own = own + grad_resid.reshape(mine, size, part).transpose(1, 0, 2)
        term = lax.dynamic_update_slice_in_dim(term, own.astype(BF16), me * mine, 1)
        grad_hidden = sum_parts(term, 5)

        grad_qkv = [
            jnp.einsum("mtd,tf->mdf", wide, d, preferred_element_type=F32)
            .astype(BF16)
            .reshape(width, part)
            for d in (dq, dk, dv)
        ]
        owned = lax.psum_scatter(
            jnp.concatenate(grad_qkv, axis=1), DP, scatter_dimension=0, tiled=True
        ).astype(F32)
        out_pairs = (
            lambda w: w.reshape(w.shape[0], 2, heads, HALF)
            .transpose(0, 2, 1, 3)
            .reshape(w.shape[0], heads * DK)
        )
        owned_query = out_pairs(owned[:, :part])
        owned_keys = out_pairs(owned[:, part : 2 * part])
        owned_values = owned[:, 2 * part :]

        zero = jnp.zeros((size, 2, units), F32)
        placed_u = lax.dynamic_update_slice(zero, grad_u, (0, core, 0))
        placed_v = lax.dynamic_update_slice(zero, grad_v * math.sqrt(width), (0, core, 0))
        placed_qk = lax.dynamic_update_slice(
            jnp.zeros((size, part), F32), out_pairs(grad_gain), (me, 0)
        )
        summed = lax.psum(
            jnp.concatenate(
                [
                    placed_u.reshape(size, 2 * units),
                    placed_v.reshape(size, 2 * units),
                    placed_qk,
                    grad_alpha_attn.reshape(size, part),
                    grad_alpha_mlp.reshape(size, part),
                ],
                axis=1,
            ),
            everyone,
        )
        summed = lax.dynamic_index_in_dim(summed, me, 0, keepdims=False)
        bounds = [2 * units, 4 * units, 4 * units + part, 4 * units + 2 * part]
        summed_up, summed_gate, summed_qk, summed_attn, summed_mlp = jnp.split(summed, bounds)
        return (
            out_hidden[None],
            grad_hidden[None],
            owned_query,
            owned_keys,
            owned_values,
            owned_output,
            owned_upward,
            owned_gating,
            owned_downward,
            summed_qk,
            summed_up,
            summed_gate,
            summed_attn,
            summed_mlp,
        )

    return on_device


def solution(mesh):
    rows, size = mesh.shape["dp"], mesh.shape["mp"]
    paired = Mesh(mesh.devices.reshape(rows // 2, 2, size), ("chip", "core", "mp"))
    return jax.shard_map(
        make_on_device(rows // 2, size),
        mesh=paired,
        in_specs=(
            P(DP, None, "mp"),
            P(DP, "mp"),
            P(DP, "mp"),
            P(DP, "mp"),
            P("mp", DP),
            P(DP, "mp"),
            P(DP, "mp"),
            P("mp", DP),
            P("mp"),
            P("mp"),
            P("mp"),
            P("mp"),
            P("mp"),
            P(DP, None),
            P(DP, None),
            P(DP, None, "mp"),
        ),
        out_specs=(
            P(DP, None, "mp"),
            P(DP, None, "mp"),
            P(DP, "mp"),
            P(DP, "mp"),
            P(DP, "mp"),
            P("mp", DP),
            P(DP, "mp"),
            P(DP, "mp"),
            P("mp", DP),
            P("mp"),
            P("mp"),
            P("mp"),
            P("mp"),
            P("mp"),
        ),
        check_vma=False,
    )
```

time: 2330 us -> 1130 us (0.48)
  the two profiles are of different devices: /device:TPU:17 before, /device:TPU:0 now
where the time goes in v1:
time: 1130 us
  Pallas kernels  687 us (61%)
  waiting for transfers between devices  214 us (19%)
  blocking collectives  75 us (7%)
  local copies, waits for them, and re-layouts  58.6 us (5%)
  other arithmetic  51.1 us (5%)
  matrix products  25.3 us (2%)
  between operations  15.8 us (1%)
    pallas_call x1, Pallas kernels, gather_parts(): pl.pallas_call(functools.partial(gather_parts_kernel, size, chunks), in_s...  238 us
    pallas_call x1, Pallas kernels, sum_parts(): pl.pallas_call(functools.partial(sum_parts_kernel, size, chunks), in_spec...  168 us
    reduce_scatter x1, waiting for transfers between devices, on_device(): lax.psum_scatter(grad_wo.reshape(size * chips * 2, rows, part), everyone,...  135 us
    pallas_call x1, Pallas kernels, attend_back(): pl.pallas_call(attend_back_kernel, grid_spec=pltpu.PrefetchScalarGridSpec...  83 us
    reduce_scatter x1, waiting for transfers between devices, on_device(): lax.psum_scatter(grads.reshape(size * chips, 6 * rows, units), ('mp', 'ch...  71.1 us
    psum x1, blocking collectives, on_device(): lax.psum(jnp.concatenate([placed_u.reshape(size, 2 * units), placed_v.res...  61.8 us
    pallas_call x1, Pallas kernels, feed_back(): pl.pallas_call(functools.partial(feed_back_kernel, size), grid=(tokens //...  43.4 us
    pallas_call x1, Pallas kernels, feed(): pl.pallas_call(functools.partial(feed_kernel, size), grid=(tokens // bloc...  40.8 us
  transfers between devices with their start and end apart: 11, of which 5 were waited for; matrix products, arithmetic and copies ran while one was open for 6% of the time, Pallas kernels for 43%

profile of v1, /device:TPU:0, one launch (start us, length us, event | category | flops | bytes accessed | tf_op | source)
XLA Modules:
  0.0 1127.9 jit_solution(5365491109696210512)
XLA Ops:
  24.5 3.2 convert_bitcast_fusion.3.source
  27.7 238.3 %gather_parts.1.wide = bf16[4,3072,256]{2,1,0:T(8,128)(2,1)} custom-call(bf16[3072,256]{1,0:T(8,128)(2,1)} %convert_bitcast_fusion.3.source), custom_call_target="tpu_custom_call" | custom-call | tf_op jit(solution)/shard_map/gather_parts/pallas_call | solution.py:248
  272.4 13.1 %all-gather.2 = f32[4,1,2560]{2,1,0:T(1,128)S(1)} all-gather(f32[1,1,2560]{2,1,0:T(1,128)S(1)} %reshape.387), channel_id=2, replica_groups=mesh['chip'=4,'core'=2,'mp'=4] {'mp'}, dimensions={0}, use_global_device_ids=true | all-gather | bytes 51200 | tf_op jit(solution)/shard_map/all_gather | solution.py:1220
  287.3 2.7 copy.144
  290.1 19.8 %project.1 = (bf16[4,3072,128]{2,1,0:T(8,128)(2,1)}, bf16[4,3072,128]{2,1,0:T(8,128)(2,1)}, bf16[4,3072,128]{2,1,0:T(8,128)(2,1)}, f32[3072,128]{1,0:T(8,128)}, f32[3072,128]{1,0:T(8,128)}) custom-call(bf16[4,3072,256]{2,1,0:T(8,128)(2,1)} %gather_parts.1.wide, bf16[4,256,768]{2,1,0:T(8,128)(2,1)} %bitcast.190, f32[3072,128]{1,0:T(8,128)} %copy.146.cosine, ...), custom_call_target="tpu_custom_call" | custom-call | flops 4831838208 | bytes 20971520 | tf_op jit(solution)/shard_map/project/pallas_call | solution.py:411
  309.9 23.9 %attend.1 = (bf16[3072,256]{1,0:T(8,128)(2,1)}, bf16[4,3072,128]{2,1,0:T(8,128)(2,1)}) custom-call(s32[6]{0:T(128)} %and_select_fusion.low, bf16[4,3072,128]{2,1,0:T(8,128)(2,1)} %get-tuple-element.39.q, bf16[4,3072,128]{2,1,0:T(8,128)(2,1)} %get-tuple-element.40.k, bf16[4,3072,128]{2,1,0:T(8,128)(2,1)} %get-tuple-element.41.v, s32[3072,1]{1,0:T(8,128)} %copy.148.qdoc, ...), custom_call_target="tpu_custom_call" | custom-call | flops 40000000000 | bytes 16777216 | tf_op jit(solution)/shard_map/attend/pallas_call | solution.py:497
  333.8 30.4 %spread_tokens.1 = bf16[768,1024]{1,0:T(8,128)(2,1)} custom-call(bf16[3072,256]{1,0:T(8,128)(2,1)} %get-tuple-element.42.source.attended), custom_call_target="tpu_custom_call" | custom-call | tf_op jit(solution)/shard_map/spread_tokens/pallas_call | solution.py:171
  370.7 4.1 fusion.3
  379.2 3.2 convert_bitcast_fusion.2.cotangent
  382.4 3.9 pad_maximum_fusion.x
  386.3 40.8 %feed.1 = (bf16[4,1536,512]{2,1,0:T(8,128)(2,1)}, bf16[4,1536,512]{2,1,0:T(8,128)(2,1)}, bf16[4,1536,512]{2,1,0:T(8,128)(2,1)}, bf16[1536,1024]{1,0:T(8,128)(2,1)}, bf16[768,1024]{1,0:T(8,128)(2,1)}) custom-call(bf16[1536,1024]{1,0:T(8,128)(2,1)} %pad_maximum_fusion.x, bf16[4,4,896,512]{3,2,1,0:T(8,128)(2,1)} %bitcast.209, ...), custom_call_target="tpu_custom_call" | custom-call | flops 19327352832 | bytes 62914560 | tf_op jit(solution)/shard_map/feed/pallas_call | solution.py:882
  429.1 3.2 collective-permute-done.2
  436.0 3.1 multiply_reduce_fusion
  441.0 3.2 collective-permute-done.3
  446.1 43.4 %feed_back.1 = (bf16[4,1536,512]{2,1,0:T(8,128)(2,1)}, bf16[4,1536,512]{2,1,0:T(8,128)(2,1)}, bf16[1536,1024]{1,0:T(8,128)(2,1)}, f32[4,1,512]{2,1,0:T(1,128)}, ...) custom-call(bf16[1536,1024]{1,0:T(8,128)(2,1)} %pad_maximum_fusion.1.dbranch, bf16[4,4,896,512]{3,2,1,0:T(8,128)(2,1)} %bitcast.212, ...), custom_call_target="tpu_custom_call" | custom-call | flops 19327352832 | bytes 73400320 | tf_op jit(solution)/shard_map/feed_back/pallas_call | solution.py:1003
  489.6 2.7 slice.92
  493.6 2.8 broadcast_select_fusion.kdoc
  496.5 3.0 multiply_reduce_fusion.3
  499.5 4.2 broadcast_multiply_fusion
  510.2 39.2 %feed_grads.1 = (bf16[4,4,768,512]{3,2,1,0:T(8,128)(2,1)}, bf16[3072,256]{1,0:T(8,128)(2,1)}) custom-call(bf16[1536,1024]{1,0:T(8,128)(2,1)} %pad_maximum_fusion.x, bf16[1536,1024]{1,0:T(8,128)(2,1)} %pad_maximum_fusion.1.dbranch, bf16[4,1536,512]{2,1,0:T(8,128)(2,1)} %get-tuple-element.49.dup, bf16[4,1536,512]{2,1,0:T(8,128)(2,1)} %get-tuple-element.50.dgate, ...), custom_call_target="tpu_custom_call" | custom-call | flops 19327352832 | bytes 41943040 | tf_op jit(solution)/shard_map/feed_grads/pallas_call | solution.py:1095
  549.4 83.0 %attend_back.1 = (bf16[3072,256]{1,0:T(8,128)(2,1)}, bf16[3072,256]{1,0:T(8,128)(2,1)}, bf16[3072,256]{1,0:T(8,128)(2,1)}, bf16[4,3072,256]{2,1,0:T(8,128)(2,1)}, f32[1,256]{1,0:T(1,128)}) custom-call(s32[6]{0:T(128)} %and_select_fusion.low, bf16[4,3072,128]{2,1,0:T(8,128)(2,1)} %get-tuple-element.48.qback, bf16[3072,256]{1,0:T(8,128)(2,1)} %get-tuple-element.53.dout, ...), custom_call_target="tpu_custom_call" | custom-call | flops 80000000000 | bytes 31457280 | tf_op jit(solution)/shard_map/attend_back/pallas_call | solution.py:714
  632.4 4.0 fusion.15
  636.5 5.8 fusion.18
  642.6 5.8 fusion.21
  651.0 3.7 convert_bitcast_fusion.1
  657.6 3.5 bitcast_convert_fusion
  662.4 2.6 copy.163
  667.4 2.9 fusion.8.term
  670.3 168.3 %sum_parts.1 = f32[3072,256]{1,0:T(8,128)} custom-call(bf16[4,3072,256]{2,1,0:T(8,128)(2,1)} %fusion.8.term), custom_call_target="tpu_custom_call" | custom-call | tf_op jit(solution)/shard_map/sum_parts/pallas_call | solution.py:327
  838.7 61.8 %psum.7 = f32[4,2816]{1,0:T(4,128)S(1)} all-reduce(f32[4,2816]{1,0:T(4,128)S(1)} %constant_dynamic-update-slice_fusion), channel_id=1, replica_groups=mesh['chip'=4,'core'=2,'mp'=4] {'mp','chip','core'}, use_global_device_ids=true, to_apply=%region_15.16 | all-reduce | flops 11264 | bytes 90112 | tf_op jit(solution)/shard_map/psum | solution.py:1365
  903.0 71.1 %reduce-scatter.8.cloned.1.call-done = bf16[1,768,512]{2,1,0:T(8,128)(2,1)} async-done(((bf16[16,768,512]{2,1,0:T(8,128)(2,1)}), bf16[1,768,512]{2,1,0:T(8,128)(2,1)}) %reduce-scatter.8.cloned.1.call-update) | async-done | bytes 786448 | tf_op jit(solution)/shard_map/reduce_scatter | solution.py:1297
  977.7 134.5 %reduce-scatter.6.cloned.1.call-done = bf16[1,128,256]{2,1,0:T(8,128)(2,1)} async-done(((bf16[32,128,256]{2,1,0:T(8,128)(2,1)}), bf16[1,128,256]{2,1,0:T(8,128)(2,1)}) %reduce-scatter.6.cloned.1.call-update) | async-done | bytes 65552 | tf_op jit(solution)/shard_map/reduce_scatter | solution.py:1312
  (206 shorter events, 76.9 us)
Async XLA Ops:
  7.2 6.5 copy-start.13
  7.2 280.1 %all-gather.6.cloned.1.call-start = ((), (), s32[]{:S(2)}) async-start(), calls=%async_computation.3 | async-start | bytes 1769472 | tf_op jit(solution)/shard_map/all_gather | solution.py:1199
  11.1 355.7 %all-gather.8.cloned.1.call-start = ((), (), s32[]{:S(2)}) async-start(), calls=%async_computation.6 | async-start | bytes 15597568 | tf_op jit(solution)/shard_map/all_gather | solution.py:1214
  11.1 2.9 copy-start.16
  14.2 2.0 collective-permute-start
  17.5 884.4 %reduce-scatter.10.cloned.1.call-start = ((), (), s32[]{:S(2)}) async-start(), calls=%async_computation.7 | async-start | bytes 1769472
  27.7 238.3 %copy-start.23 = (f32[256]{0:T(256)S(1)}, f32[256]{0:T(256)}, u32[]{:S(2)}) copy-start(f32[256]{0:T(256)} %param.29) | copy-start | bytes 3076
  270.1 2.2 copy-start.21
  270.2 2.2 copy-start.22
  270.2 2.2 copy-start.24
  270.2 15.9 %copy-start.18 = (s32[1,3072]{1,0:T(1,128)S(1)}, s32[1,3072]{1,0:T(1,128)}, u32[]{:S(2)}) copy-start(s32[1,3072]{1,0:T(1,128)} %param.35) | copy-start | bytes 36868
  370.7 4.1 copy-start.2
  378.0 4.4 collective-permute-start.1
  427.1 5.2 copy-start.6
  428.8 3.5 collective-permute-start.2
  440.8 3.4 collective-permute-start.3
  492.2 4.2 collective-permute-start.4
  493.6 2.9 copy-start.1
  496.4 3.0 copy-start.9
  499.5 4.3 copy-start.3
  499.5 4.3 copy-start.5
  510.2 122.2 %slice-start = ((s8[6291456]{0:T(1024)(128)(4,1)}), s8[4194304]{0:T(1024)(128)(4,1)S(1)}, s32[]{:S(2)}) async-start(s8[6291456]{0:T(1024)(128)(4,1)} %bitcast.182), calls=%async_computation.8 | async-start | bytes 8388608
  549.4 83.0 %slice-start.1 = ((s8[6291456]{0:T(1024)(128)(4,1)}), s8[2097152]{0:T(1024)(128)(4,1)S(1)}, s32[]{:S(2)}) async-start(s8[6291456]{0:T(1024)(128)(4,1)} %bitcast.182), calls=%async_computation.9 | async-start | bytes 4194304
  650.3 323.7 %reduce-scatter.8.cloned.1.call-start = ((), (), s32[]{:S(2)}) async-start(), calls=%async_computation.5 | async-start | bytes 13369344 | tf_op jit(solution)/shard_map/reduce_scatter | solution.py:1297
  650.9 461.3 %reduce-scatter.6.cloned.1.call-start = ((), (), s32[]{:S(2)}) async-start(), calls=%async_computation.4 | async-start | bytes 2162688 | tf_op jit(solution)/shard_map/reduce_scatter | solution.py:1312
  654.7 2.6 copy-start.17
  654.7 2.7 copy-start.20
  654.7 2.7 copy-start.19
  657.3 4.3 copy-start.26
  657.3 5.1 copy-start.7
  975.3 138.5 %collective-permute-start.5 = (bf16[3,128,512]{2,1,0:T(8,128)(2,1)S(1)}, bf16[3,128,512]{2,1,0:T(8,128)(2,1)S(1)}, u32[]{:S(2)}, u32[]{:S(2)}) collective-permute-start(bf16[3,128,512]{2,1,0:T(8,128)(2,1)S(1)} %get-tuple-element.125), channel_id=1, source_target_pairs={{0,4},{4,0},{1,5},{5,1},{2,6},{6,2},{3,7},{7,3},{8,12},{12,8},{9,1... | collective-permute-start | bytes 1179656 | tf_op jit(solution)/shard_map/ppermute | solution.py:1159
  1114.5 4.7 copy-start.8
  (8 other events, 12.5 us)
Sparse Core Ops, SparseCore 0:
  11.2 28.6 all-gather.5
  42.6 229.9 all-gather.7
  650.5 51.6 reduce-scatter.9
  707.6 266.4 reduce-scatter.7
  976.3 135.8 reduce-scatter.5

commit v2 on v1

--- a/solution.py
+++ b/solution.py
@@ -15,7 +15,7 @@
 EXT = 128
 EPSILON = 1e-06
 ROPE_BASE = 10000.0
-VMEM_LIMIT = 56 * 1024 * 1024
+VMEM_LIMIT = 60 * 1024 * 1024
 F32 = jnp.float32
 BF16 = jnp.bfloat16
 DP = ("chip", "core")
@@ -49,15 +49,19 @@
     )
 
 
-def to_member(source, target, send, receive, member):
+def to_device(source, target, send, receive, where):
     return pltpu.make_async_remote_copy(
         src_ref=source,
         dst_ref=target,
         send_sem=send,
         recv_sem=receive,
-        device_id={"mp": member},
+        device_id=where,
         device_id_type=pl.DeviceIdType.MESH,
     )
+
+
+def to_member(source, target, send, receive, member):
+    return to_device(source, target, send, receive, {"mp": member})
 
 
 def flip(index, mask):
@@ -69,11 +73,15 @@
     return index
 
 
-def greet(member):
+def bits_below(count):
+    return [1 << k for k in range(count.bit_length() - 1)]
+
+
+def greet(where):
     pl.semaphore_signal(
         pltpu.get_barrier_semaphore(),
         inc=1,
-        device_id={"mp": member},
+        device_id=where,
         device_id_type=pl.DeviceIdType.MESH,
     )
 
@@ -81,30 +89,18 @@
 def greet_all(size):
     me = lax.axis_index("mp")
     for k in range(1, size):
-        greet(flip(me, k))
+        greet({"mp": flip(me, k)})
     pl.semaphore_wait(pltpu.get_barrier_semaphore(), size - 1)
 
 
-def greet_line(size):
-    me = lax.axis_index("mp")
-
-    @pl.when(me > 0)
-    def _():
-        greet(me - 1)
-
-    @pl.when(me < size - 1)
-    def _():
-        greet(me + 1)
-
-    inside = (me > 0) & (me < size - 1)
-
-    @pl.when(inside)
-    def _():
-        pl.semaphore_wait(pltpu.get_barrier_semaphore(), 2)
-
-    @pl.when(jnp.logical_not(inside))
-    def _():
-        pl.semaphore_wait(pltpu.get_barrier_semaphore(), 1)
+def greet_around(size, chips):
+    me, chip, core = (lax.axis_index(name) for name in ("mp", "chip", "core"))
+    for k in range(1, size):
+        greet({"mp": flip(me, k)})
+    for bit in bits_below(chips):
+        greet({"chip": flip(chip, bit)})
+    greet({"core": 1 - core})
+    pl.semaphore_wait(pltpu.get_barrier_semaphore(), size + len(bits_below(chips)))
 
 
 class Exchange:
@@ -179,160 +175,741 @@
     )(value)
 
 
-def gather_parts_kernel(size, chunks, source, target, send_up, send_down, receive, local):
-    me = lax.axis_index("mp")
-    tokens = source.shape[0]
+class Gather:
+    def __init__(self, block, index, bits, where, send, receive):
+        self.block, self.index, self.bits, self.where = block, index, bits, where
+        self.send, self.receive = send, receive
+
+    def copies(self, stage, incoming):
+        span = [0]
+        for bit in self.bits[:stage]:
+            span += [held | bit for held in span]
+        bit = self.bits[stage]
+        for order, held in enumerate(span):
+            ref = self.block(flip(self.index, held | bit if incoming else held))
+            slot = (1 << stage) - 1 + order
+            yield to_device(
+                ref,
+                ref,
+                self.send(slot),
+                self.receive(slot),
+                self.where(flip(self.index, bit)),
+            )
+
+    def start(self, stage):
+        if stage < len(self.bits):
+            for copy in self.copies(stage, False):
+                copy.start()
+
+    def arrive(self, stage):
+        if stage < len(self.bits):
+            for copy in self.copies(stage, True):
+                copy.wait_recv()
+
+    def close(self):
+        for stage in range(len(self.bits)):
+            for copy in self.copies(stage, False):
+                copy.wait_send()
+
+
+def gather_all_kernel(
+    size,
+    chips,
+    chunks,
+    split,
+    hidden,
+    qkv,
+    packed,
+    vectors,
+    wide,
+    full_qkv,
+    full,
+    full_vectors,
+    local,
+    hidden_up,
+    hidden_down,
+    hidden_got,
+    packed_up,
+    packed_down,
+    packed_got,
+    plane_sent,
+    plane_got,
+    qkv_sent,
+    qkv_got,
+    vector_sent,
+    vector_got,
+):
+    me, chip, core = (lax.axis_index(name) for name in ("mp", "chip", "core"))
+    tokens = hidden.shape[0]
     rows = tokens // chunks
-    greet_line(size)
-    own = pltpu.make_async_copy(source, target.at[me], local)
-    own.start()
-
-    def hop(origin, chunk, ref, member, send):
+    height = packed.shape[0]
+    owner = chip * 2 + core
+    bits = bits_below(chips)
+    stages = len(bits)
+    greet_around(size, chips)
+
+    own = [
+        pltpu.make_async_copy(qkv, full_qkv.at[owner], local.at[0]),
+        pltpu.make_async_copy(packed, full.at[me, chip], local.at[1]),
+        pltpu.make_async_copy(vectors, full_vectors.at[me], local.at[2]),
+        pltpu.make_async_copy(hidden, wide.at[me], local.at[3]),
+    ]
+    for copy in own:
+        copy.start()
+
+    def hidden_hop(origin, chunk, ref, member, send):
         at = pl.ds(chunk * rows, rows)
         return to_member(
             ref.at[at, :],
-            target.at[origin, at, :],
+            wide.at[origin, at, :],
             send.at[origin, chunk],
-            receive.at[origin, chunk],
+            hidden_got.at[origin, chunk],
             member,
         )
 
+    def packed_hop(origin, ref, member, send):
+        return to_member(
+            ref, full.at[origin, chip], send.at[origin], packed_got.at[origin], member
+        )
+
+    vector_copies = [
+        to_member(
+            vectors, full_vectors.at[me], vector_sent.at[k], vector_got.at[k], flip(me, k)
+        )
+        for k in range(1, size)
+    ]
+
+    def plane(origin, slot):
+        return [
+            Gather(
+                lambda i, at=at: full.at[origin, i, at, :],
+                chip,
+                order,
+                lambda i: {"chip": i},
+                lambda k, half=half: plane_sent.at[slot, half, k],
+                lambda k, half=half: plane_got.at[slot, half, k],
+            )
+            for half, (at, order) in enumerate(
+                (
+                    (pl.ds(0, split), bits),
+                    (pl.ds(split, height - split), bits[::-1]),
+                )
+            )
+        ]
+
+    gather_qkv = Gather(
+        lambda i: full_qkv.at[i],
+        owner,
+        [2 * bit for bit in bits] + [1],
+        lambda i: {"chip": lax.div(i, 2), "core": lax.rem(i, 2)},
+        lambda k: qkv_sent.at[k],
+        lambda k: qkv_got.at[k],
+    )
+
+    sources = {0: [(me >= 0, me, 0, None)]}
+    for distance in range(1, size):
+        sources[distance] = [
+            (me >= distance, me - distance, 2 * distance - 1, True),
+            (me + distance < size, me + distance, 2 * distance, False),
+        ]
+
+    own[0].wait()
+    gather_qkv.start(0)
+
+    @pl.when(me < size - 1)
+    def _():
+        packed_hop(me, packed, me + 1, packed_up).start()
+
+    @pl.when(me > 0)
+    def _():
+        packed_hop(me, packed, me - 1, packed_down).start()
+
+    own[1].wait()
+    for half in plane(me, 0):
+        half.start(0)
     for chunk in range(chunks):
 
         @pl.when(me < size - 1)
         def _():
-            hop(me, chunk, source, me + 1, send_up).start()
+            hidden_hop(me, chunk, hidden, me + 1, hidden_up).start()
 
         @pl.when(me > 0)
         def _():
-            hop(me, chunk, source, me - 1, send_down).start()
+            hidden_hop(me, chunk, hidden, me - 1, hidden_down).start()
+
+    for copy in vector_copies:
+        copy.start()
+    for stage in range(stages + 1):
+        gather_qkv.arrive(stage)
+        if stage < stages:
+            gather_qkv.start(stage + 1)
+
+    def advance(distance, stage):
+        for exists, origin, slot, _ in sources[distance]:
+
+            @pl.when(exists)
+            def _():
+                for half in plane(origin, slot):
+                    half.arrive(stage)
+                    half.start(stage + 1)
 
     for distance in range(1, size):
+        for exists, origin, slot, upward in sources[distance]:
+
+            @pl.when(exists)
+            def _():
+                block = full.at[origin, chip]
+                packed_hop(origin, block, me, packed_up).wait_recv()
+                if upward:
+
+                    @pl.when(me < size - 1)
+                    def _():
+                        packed_hop(origin, block, me + 1, packed_up).start()
+                else:
+
+                    @pl.when(me > 0)
+                    def _():
+                        packed_hop(origin, block, me - 1, packed_down).start()
+
+                for half in plane(origin, slot):
+                    half.start(0)
+
         for chunk in range(chunks):
-            below, above = me - distance, me + distance
-
-            @pl.when(below >= 0)
+            for exists, origin, _, upward in sources[distance]:
+
+                @pl.when(exists)
+                def _():
+                    block = wide.at[origin]
+                    hidden_hop(origin, chunk, block, me, hidden_up).wait_recv()
+                    if upward:
+
+                        @pl.when(me < size - 1)
+                        def _():
+                            hidden_hop(origin, chunk, block, me + 1, hidden_up).start()
+                    else:
+
+                        @pl.when(me > 0)
+                        def _():
+                            hidden_hop(origin, chunk, block, me - 1, hidden_down).start()
+
+            if chunk == chunks // 3:
+                for stage in range(stages - 1):
+                    advance(distance - 1, stage)
+        advance(distance - 1, stages - 1)
+    for stage in range(stages):
+        advance(size - 1, stage)
+
+    own[2].wait()
+    own[3].wait()
+    for copy in vector_copies:
+        copy.wait()
+    gather_qkv.close()
+    for distance in range(size):
+        for exists, origin, slot, upward in sources[distance]:
+
+            @pl.when(exists)
             def _():
-                hop(below, chunk, target.at[below], me, send_up).wait_recv()
-
-                @pl.when(me < size - 1)
-                def _():
-                    hop(below, chunk, target.at[below], me + 1, send_up).start()
-
-            @pl.when(above < size)
+                for half in plane(origin, slot):
+                    half.close()
+                block = full.at[origin, chip]
+                if upward is not False:
+
+                    @pl.when(me < size - 1)
+                    def _():
+                        packed_hop(origin, block, me, packed_up).wait_send()
+                        for chunk in range(chunks):
+                            hidden_hop(origin, chunk, wide.at[origin], me, hidden_up).wait_send()
+
+                if not upward:
+
+                    @pl.when(me > 0)
+                    def _():
+                        packed_hop(origin, block, me, packed_down).wait_send()
+                        for chunk in range(chunks):
+                            hidden_hop(
+                                origin, chunk, wide.at[origin], me, hidden_down
+                            ).wait_send()
+
+
+def gather_all(hidden, qkv, packed, vectors, size, chips, collective):
+    chunks = 6
+    height = packed.shape[0]
+    dma = pltpu.SemaphoreType.DMA
+    line = dma((size, chunks))
+    plane = dma((2 * size - 1, 2, max(chips - 1, 1)))
+    return pl.pallas_call(
+        functools.partial(gather_all_kernel, size, chips, chunks, height // 32 * 16),
+        in_specs=[ANY] * 4,
+        out_specs=[ANY] * 4,
+        out_shape=[
+            jax.ShapeDtypeStruct((size, *hidden.shape), BF16),
+            jax.ShapeDtypeStruct((2 * chips, *qkv.shape), BF16),
+            jax.ShapeDtypeStruct((size, chips, *packed.shape), BF16),
+            jax.ShapeDtypeStruct((size, *vectors.shape), F32),
+        ],
+        scratch_shapes=[
+            dma((4,)),
+            line,
+            line,
+            line,
+            dma((size,)),
+            dma((size,)),
+            dma((size,)),
+            plane,
+            plane,
+            dma((2 * chips - 1,)),
+            dma((2 * chips - 1,)),
+            dma((size,)),
+            dma((size,)),
+        ],
+        compiler_params=remote_params(collective),
+        name="gather_all",
+    )(hidden, qkv, packed, vectors)
+
+
+class LineSum:
+    def __init__(self, size, chunks, term, up, down, sems):
+        self.size, self.chunks = size, chunks
+        self.term, self.up, self.down = term, up, down
+        self.sent_up, self.sent_down, self.got_up, self.got_down = sems
+        self.me = lax.axis_index("mp")
+        self.rows = up.shape[1] // chunks
+
+    def at(self, chunk):
+        return pl.ds(chunk * self.rows, self.rows)
+
+    def hop(self, upward, goal, chunk, member):
+        slots = self.up if upward else self.down
+        send = self.sent_up if upward else self.sent_down
+        receive = self.got_up if upward else self.got_down
+        ref = slots.at[goal, self.at(chunk), :]
+        return to_member(ref, ref, send.at[goal, chunk], receive.at[goal, chunk], member)
+
+    def step(self, order, chunk):
+        me, last, at = self.me, self.size - 1, self.at(chunk)
+        for upward, goal, ahead, first, member in (
+            (True, last - order, me < last - order, me == 0, me + 1),
+            (False, order, me > order, me == last, me - 1),
+        ):
+            slots = self.up if upward else self.down
+
+            @pl.when(ahead & first)
             def _():
-                hop(above, chunk, target.at[above], me, send_down).wait_recv()
-
-                @pl.when(me > 0)
-                def _():
-                    hop(above, chunk, target.at[above], me - 1, send_down).start()
-
-    own.wait()
-    for distance in range(size):
-        for chunk in range(chunks):
-            below, above = me - distance, me + distance
-
-            @pl.when((below >= 0) & (me < size - 1))
+                slots[goal, at, :] = self.term(goal, at)
+
+            @pl.when(ahead & jnp.logical_not(first))
             def _():
-                hop(below, chunk, source, me + 1, send_up).wait_send()
-
-            @pl.when((above < size) & (me > 0))
+                self.hop(upward, goal, chunk, me).wait_recv()
+                slots[goal, at, :] = (
+                    slots[goal, at, :].astype(F32) + self.term(goal, at).astype(F32)
+                ).astype(BF16)
+
+            @pl.when(ahead)
             def _():
-                hop(above, chunk, source, me - 1, send_down).wait_send()
-
-
-def gather_parts(value, size, collective):
-    tokens, part = value.shape
-    chunks = 6
-    semaphores = pltpu.SemaphoreType.DMA((size, chunks))
-    return pl.pallas_call(
-        functools.partial(gather_parts_kernel, size, chunks),
-        in_specs=[ANY],
-        out_specs=ANY,
-        out_shape=jax.ShapeDtypeStruct((size, tokens, part), value.dtype),
-        scratch_shapes=[semaphores, semaphores, semaphores, pltpu.SemaphoreType.DMA],
-        compiler_params=remote_params(collective),
-        name="gather_parts",
-    )(value)
-
-
-def sum_parts_kernel(size, chunks, term, out, up, down, sent_up, sent_down, got_up, got_down):
-    me = lax.axis_index("mp")
-    rows = out.shape[0] // chunks
-    greet_line(size)
-
-    def hop(slots, goal, chunk, member, send, receive):
-        at = pl.ds(chunk * rows, rows)
-        return to_member(
-            slots.at[goal, at, :],
-            slots.at[goal, at, :],
-            send.at[goal, chunk],
-            receive.at[goal, chunk],
-            member,
-        )
-
-    for order in range(size - 1):
-        for chunk in range(chunks):
-            at = pl.ds(chunk * rows, rows)
-            for slots, goal, ahead, first, step, send, receive in (
-                (up, size - 1 - order, me < size - 1 - order, me == 0, 1, sent_up, got_up),
-                (down, order, me > order, me == size - 1, -1, sent_down, got_down),
-            ):
-
-                @pl.when(ahead & first)
-                def _():
-                    slots[goal, at, :] = term[goal, at, :]
-
-                @pl.when(ahead & jnp.logical_not(first))
-                def _():
-                    hop(slots, goal, chunk, me, send, receive).wait_recv()
-                    slots[goal, at, :] = (
-                        slots[goal, at, :].astype(F32) + term[goal, at, :].astype(F32)
-                    ).astype(BF16)
-
-                @pl.when(ahead)
-                def _():
-                    hop(slots, goal, chunk, me + step, send, receive).start()
-
-    for chunk in range(chunks):
-        at = pl.ds(chunk * rows, rows)
-        out[at, :] = term[me, at, :].astype(F32)
+                self.hop(upward, goal, chunk, member).start()
+
+    def result(self, chunk, out, out_at):
+        me, at = self.me, self.at(chunk)
+        out[out_at, :] = self.term(me, at).astype(F32)
 
         @pl.when(me > 0)
         def _():
-            hop(up, me, chunk, me, sent_up, got_up).wait_recv()
-            out[at, :] += up[me, at, :].astype(F32)
-
-        @pl.when(me < size - 1)
+            self.hop(True, me, chunk, me).wait_recv()
+            out[out_at, :] += self.up[me, at, :].astype(F32)
+
+        @pl.when(me < self.size - 1)
         def _():
-            hop(down, me, chunk, me, sent_down, got_down).wait_recv()
-            out[at, :] += down[me, at, :].astype(F32)
-
-    for order in range(size - 1):
+            self.hop(False, me, chunk, me).wait_recv()
+            out[out_at, :] += self.down[me, at, :].astype(F32)
+
+    def close(self):
+        for order in range(self.size - 1):
+            for chunk in range(self.chunks):
+
+                @pl.when(self.me < self.size - 1 - order)
+                def _():
+                    self.hop(True, self.size - 1 - order, chunk, self.me).wait_send()
+
+                @pl.when(self.me > order)
+                def _():
+                    self.hop(False, order, chunk, self.me).wait_send()
+
+
+class ChipSum:
+    def __init__(self, layers, bits, source, acc, got, load, send, receive):
+        self.layers, self.bits = layers, bits
+        self.acc, self.got, self.chip = acc, got, lax.axis_index("chip")
+        self.half = 1 << (len(bits) - 1)
+        self.load = [
+            pltpu.make_async_copy(
+                source(layer, flip(self.chip, self.combo(slot))),
+                acc.at[layer, slot],
+                load.at[layer, slot],
+            )
+            for layer in range(layers)
+            for slot in range(self.half)
+        ]
+        self.source, self.sent, self.received = source, send, receive
+
+    def combo(self, slot):
+        count = len(self.bits)
+        return sum(self.bits[count - 1 - j] for j in range(count - 1) if slot >> j & 1)
+
+    def copies(self, stage):
+        count = self.half >> stage
+        offset = 2 * self.half - 2 * count
+        where = {"chip": flip(self.chip, self.bits[stage])}
+        for layer in range(self.layers):
+            for slot in range(count):
+                if stage == 0:
+                    other = flip(self.chip, self.bits[0] | self.combo(slot))
+                    ref = self.source(layer, other)
+                else:
+                    ref = self.acc.at[layer, count + slot]
+                at = offset + slot
+                yield layer, slot, at, to_device(
+                    ref,
+                    self.got.at[layer, at],
+                    self.sent.at[layer, at],
+                    self.received.at[layer, at],
+                    where,
+                )
+
+    def start(self, stage):
+        if stage == 0:
+            for copy in self.load:
+                copy.start()
+        for _, _, _, copy in self.copies(stage):
+            copy.start()
+
+    def add(self, stage):
+        if stage == 0:
+            for copy in self.load:
+                copy.wait()
+        for layer, slot, at, copy in self.copies(stage):
+            copy.wait_recv()
+            self.acc[layer, slot] = (
+                self.acc[layer, slot].astype(F32) + self.got[layer, at].astype(F32)
+            ).astype(BF16)
+
+    def close(self):
+        for stage in range(len(self.bits)):
+            for _, _, _, copy in self.copies(stage):
+                copy.wait_send()
+
+
+def sum_all_kernel(
+    size,
+    chips,
+    chunks,
+    split,
+    term,
+    grads,
+    grad_wo,
+    grad_qkv,
+    vectors,
+    out,
+    owned,
+    owned_wo,
+    owned_qkv,
+    owned_vectors,
+    term_up,
+    term_down,
+    acc_a,
+    got_a,
+    up_a,
+    down_a,
+    acc_b,
+    got_b,
+    up_b,
+    down_b,
+    pair_wo,
+    other_wo,
+    acc_wo,
+    got_wo,
+    up_wo,
+    down_wo,
+    pair_qkv,
+    other_qkv,
+    acc_qkv,
+    got_qkv,
+    whole,
+    vector_sum,
+    vector_got,
+    vector_line,
+    local,
+    core_sent,
+    core_got,
+    vector_sent,
+    vector_received,
+    term_sems,
+    line_sems,
+    load_sems,
+    chip_sent,
+    chip_got,
+):
+    me, chip, core = (lax.axis_index(name) for name in ("mp", "chip", "core"))
+    bits = bits_below(chips)
+    stages = len(bits)
+    greet_around(size, chips)
+    other_core_is = {"core": 1 - core}
+
+    def sems(ref, which):
+        return [ref.at[which, k] for k in range(4)]
+
+    line = LineSum(
+        size, chunks, lambda goal, at: term[goal, at, :], term_up, term_down, sems(term_sems, 0)
+    )
+    sum_a = ChipSum(
+        size,
+        bits,
+        lambda m, c: grads.at[m, c, pl.ds(0, split), :],
+        acc_a,
+        got_a,
+        load_sems.at[0],
+        chip_sent.at[0],
+        chip_got.at[0],
+    )
+    sum_b = ChipSum(
+        size,
+        bits[::-1],
+        lambda m, c: grads.at[m, c, pl.ds(split, grads.shape[2] - split), :],
+        acc_b,
+        got_b,
+        load_sems.at[1],
+        chip_sent.at[1],
+        chip_got.at[1],
+    )
+    sum_wo = ChipSum(
+        size,
+        bits,
+        lambda m, c: pair_wo.at[m, c],
+        acc_wo,
+        got_wo,
+        load_sems.at[2],
+        chip_sent.at[2],
+        chip_got.at[2],
+    )
+    sum_qkv = ChipSum(
+        1,
+        bits,
+        lambda m, c: pair_qkv.at[c],
+        acc_qkv,
+        got_qkv,
+        load_sems.at[3],
+        chip_sent.at[3],
+        chip_got.at[3],
+    )
+    lines = [
+        LineSum(
+            size,
+            1,
+            lambda goal, at, acc=acc: acc[goal, 0, at, :],
+            up,
+            down,
+            sems(line_sems, which),
+        )
+        for which, (acc, up, down) in enumerate(
+            ((acc_a, up_a, down_a), (acc_b, up_b, down_b), (acc_wo, up_wo, down_wo))
+        )
+    ]
+
+    own = [
+        pltpu.make_async_copy(grad_wo.at[:, :, core], pair_wo, local.at[0]),
+        pltpu.make_async_copy(grad_qkv.at[:, core], pair_qkv, local.at[1]),
+    ]
+    given = [
+        to_device(
+            grad_wo.at[:, :, 1 - core], other_wo, core_sent.at[0], core_got.at[0], other_core_is
+        ),
+        to_device(
+            grad_qkv.at[:, 1 - core], other_qkv, core_sent.at[1], core_got.at[1], other_core_is
+        ),
+    ]
+    vector_copies = [
+        to_member(
+            vectors.at[flip(me, k)],
+            vector_line.at[k],
+            vector_sent.at[k],
+            vector_received.at[k],
+            flip(me, k),
+        )
+        for k in range(1, size)
+    ]
+    for copy in own + given:
+        copy.start()
+    sum_a.start(0)
+    sum_b.start(0)
+    for copy in vector_copies:
+        copy.start()
+
+    owner = chip * 2 + core
+    vector_bits = [1] + [2 * bit for bit in bits]
+
+    def vector_copy(stage):
+        partner = flip(owner, vector_bits[stage])
+        return to_device(
+            vector_sum.at[stage],
+            vector_got.at[stage],
+            vector_sent.at[size + stage],
+            vector_received.at[size + stage],
+            {"chip": lax.div(partner, 2), "core": lax.rem(partner, 2)},
+        )
+
+    def vector_step(stage):
+        if stage == 0:
+            total = vectors[me]
+            for k, copy in enumerate(vector_copies):
+                copy.wait_recv()
+                total = total + vector_line[k + 1]
+            vector_sum[0] = total
+        else:
+            vector_copy(stage - 1).wait_recv()
+            vector_sum[stage] = vector_sum[stage - 1] + vector_got[stage - 1]
+        if stage < len(vector_bits):
+            vector_copy(stage).start()
+
+    for chunk in range(chunks):
+        line.step(0, chunk)
+    for copy in own:
+        copy.wait()
+    for copy in given:
+        copy.wait_recv()
+    pair_wo[...] = (pair_wo[...].astype(F32) + other_wo[...].astype(F32)).astype(BF16)
+    pair_qkv[...] = (pair_qkv[...].astype(F32) + other_qkv[...].astype(F32)).astype(BF16)
+    sum_wo.start(0)
+    sum_qkv.start(0)
+    vector_step(0)
+    vector_step(1)
+    for order in range(1, size - 1):
         for chunk in range(chunks):
-
-            @pl.when(me < size - 1 - order)
-            def _():
-                hop(up, size - 1 - order, chunk, me, sent_up, got_up).wait_send()
-
-            @pl.when(me > order)
-            def _():
-                hop(down, order, chunk, me, sent_down, got_down).wait_send()
-
-
-def sum_parts(term, collective):
+            line.step(order, chunk)
+        if order - 1 < stages:
+            for part in (sum_a, sum_b, sum_wo, sum_qkv):
+                part.add(order - 1)
+                if order < stages:
+                    part.start(order)
+    for stage in range(size - 2, stages):
+        for part in (sum_a, sum_b, sum_wo, sum_qkv):
+            part.add(stage)
+            if stage + 1 < stages:
+                part.start(stage + 1)
+    lines[0].step(0, 0)
+    lines[1].step(0, 0)
+    lines[2].step(0, 0)
+    for stage in range(2, len(vector_bits) + 1):
+        vector_step(stage)
+    for chunk in range(chunks):
+        line.result(chunk, out, line.at(chunk))
+    for order in range(1, size - 1):
+        for part in lines:
+            part.step(order, 0)
+    owned_vectors[...] = vector_sum[len(vector_bits)]
+    owned_qkv[...] = acc_qkv[0, 0].astype(F32)
+    lines[0].result(0, whole, pl.ds(0, split))
+    lines[1].result(0, whole, pl.ds(split, whole.shape[0] - split))
+    lines[2].result(0, owned_wo, slice(None))
+
+    matrices, rows, columns = owned.shape
+    columns = columns // 2
+    place = pl.ds(pl.multiple_of(core * columns, columns), columns)
+    swaps = []
+    for matrix in range(matrices):
+        mine = pl.ds(pl.multiple_of((2 * matrix + core) * rows, rows), rows)
+        theirs = pl.ds(pl.multiple_of((2 * matrix + 1 - core) * rows, rows), rows)
+        swaps.append(
+            to_device(
+                whole.at[theirs, :],
+                owned.at[matrix, :, place],
+                core_sent.at[2 + matrix],
+                core_got.at[2 + matrix],
+                other_core_is,
+            )
+        )
+        swaps[-1].start()
+        copy = pltpu.make_async_copy(
+            whole.at[mine, :], owned.at[matrix, :, place], local.at[2 + matrix]
+        )
+        copy.start()
+        swaps.append(copy)
+    for copy in swaps:
+        copy.wait()
+
+    for copy in given + vector_copies:
+        copy.wait_send()
+    for stage in range(len(vector_bits)):
+        vector_copy(stage).wait_send()
+    for part in (sum_a, sum_b, sum_wo, sum_qkv):
+        part.close()
+    line.close()
+    for part in lines:
+        part.close()
+
+
+def sum_all(term, grads, grad_wo, grad_qkv, vectors, chips, collective):
     size, tokens, part = term.shape
+    height, units = grads.shape[2:]
+    rows = height // 6
     chunks = 6
-    semaphores = pltpu.SemaphoreType.DMA((size, chunks))
+    split = height // 32 * 16
+    half, blocks = max(chips // 2, 1), max(chips - 1, 1)
+    stages = chips.bit_length()
+    dma = pltpu.SemaphoreType.DMA
+    vmem = pl.BlockSpec(memory_space=pltpu.VMEM)
+    wo_block, qkv_block = grad_wo.shape[3:], grad_qkv.shape[2:]
+    long = vectors.shape[1:]
+
+    def sums(layers, block):
+        return [
+            pltpu.VMEM((layers, half, *block), BF16),
+            pltpu.VMEM((layers, blocks, *block), BF16),
+        ]
+
+    def line(block):
+        return [pltpu.VMEM((size, *block), BF16)] * 2
+
     return pl.pallas_call(
-        functools.partial(sum_parts_kernel, size, chunks),
-        in_specs=[pl.BlockSpec(memory_space=pltpu.VMEM)],
-        out_specs=pl.BlockSpec(memory_space=pltpu.VMEM),
-        out_shape=jax.ShapeDtypeStruct((tokens, part), F32),
-        scratch_shapes=[pltpu.VMEM((size, tokens, part), BF16)] * 2 + [semaphores] * 4,
+        functools.partial(sum_all_kernel, size, chips, chunks, split),
+        in_specs=[vmem, ANY, ANY, ANY, vmem],
+        out_specs=[vmem] * 5,
+        out_shape=[
+            jax.ShapeDtypeStruct((tokens, part), F32),
+            jax.ShapeDtypeStruct((3, rows, 2 * units), F32),
+            jax.ShapeDtypeStruct(wo_block, F32),
+            jax.ShapeDtypeStruct(qkv_block, F32),
+            jax.ShapeDtypeStruct(long, F32),
+        ],
+        scratch_shapes=[
+            *line((tokens, part)),
+            *sums(size, (split, units)),
+            *line((split, units)),
+            *sums(size, (height - split, units)),
+            *line((height - split, units)),
+            pltpu.VMEM((size, chips, *wo_block), BF16),
+            pltpu.VMEM((size, chips, *wo_block), BF16),
+            *sums(size, wo_block),
+            *line(wo_block),
+            pltpu.VMEM((chips, *qkv_block), BF16),
+            pltpu.VMEM((chips, *qkv_block), BF16),
+            *sums(1, qkv_block),
+            pltpu.VMEM((height, units), F32),
+            pltpu.VMEM((stages + 1, *long), F32),
+            pltpu.VMEM((stages + 1, *long), F32),
+            pltpu.VMEM((size, *long), F32),
+            dma((5,)),
+            dma((5,)),
+            dma((5,)),
+            dma((size + stages,)),
+            dma((size + stages,)),
+            dma((1, 4, size, chunks)),
+            dma((3, 4, size, 1)),
+            dma((4, size, half)),
+            dma((4, size, blocks)),
+            dma((4, size, blocks)),
+        ],
         compiler_params=remote_params(collective),
-        name="sum_parts",
-    )(term)
+        name="sum_all",
+    )(term, grads, grad_wo, grad_qkv, vectors)
 
 
 def paired_place(heads):
@@ -1187,7 +1764,6 @@
         block = min(512, slots)
         me = lax.axis_index("mp")
         core = lax.axis_index("core")
-        everyone = ("mp", "chip", "core")
 
         place = paired_place(heads)
         in_pairs = (
@@ -1196,8 +1772,6 @@
             .reshape(w.shape[0], heads * DK)
         )
         low_qkv = jnp.concatenate([in_pairs(wq), in_pairs(wk), wv], axis=1).astype(BF16)
-        full_qkv = lax.all_gather(low_qkv, DP, axis=0, tiled=True).reshape(size, part, 3 * part)
-
         stacked = jnp.stack([w_up, w_gate, w_down.T]).astype(BF16).reshape(3, rows, 2, units)
         keep = lax.dynamic_index_in_dim(stacked, core, 2, keepdims=False)
         give = lax.dynamic_index_in_dim(stacked, 1 - core, 2, keepdims=False)
@@ -1211,13 +1785,13 @@
         pair = in_order(keep, got[: 3 * rows].reshape(3, rows, units))
         pair_wo = in_order(low_wo[None], got[3 * rows :][None])
         packed = jnp.concatenate([pair.reshape(6 * rows, units), pair_wo.reshape(rows, units)])
-        packed = lax.all_gather(packed, ("mp", "chip"), axis=0).reshape(
-            size, chips, 7 * rows, units
-        )
-        wide = gather_parts(hidden[0].astype(BF16), size, 0)
+        vectors = jnp.concatenate([s_u, s_v * math.sqrt(width), alpha_a, alpha_m])
+        wide, full_qkv, packed, vectors = gather_all(
+            hidden[0].astype(BF16), low_qkv, packed, vectors[None], size, chips, 0
+        )
+        full_qkv = full_qkv.reshape(size, part, 3 * part)
         full_wo = packed[:, :, 6 * rows :].reshape(size, width, part)
-        vectors = jnp.concatenate([s_u, s_v * math.sqrt(width), alpha_a, alpha_m])
-        vectors = lax.all_gather(vectors, "mp", axis=0)
+        vectors = vectors[:, 0]
         s_up = lax.dynamic_slice_in_dim(vectors[:, : 2 * units], core * units, units, 1)
         s_gate = lax.dynamic_slice_in_dim(
             vectors[:, 2 * units : 4 * units], core * units, units, 1
@@ -1294,25 +1868,9 @@
         grads, dattended = feed_grads(
             x, dbranch, dup, dgate, hidden_units, grad_merged.reshape(mine, width), chips, 4
         )
-        total = lax.psum_scatter(
-            grads.reshape(size * chips, 6 * rows, units), ("mp", "chip"), scatter_dimension=0
-        )
-        total = total.reshape(3, 2, rows, units)
-        keep = lax.dynamic_index_in_dim(total, core, 1, keepdims=False)
-        got = other_core(lax.dynamic_index_in_dim(total, 1 - core, 1, keepdims=False))
-        owned = jnp.where(
-            core == 0,
-            jnp.concatenate([keep, got], axis=2),
-            jnp.concatenate([got, keep], axis=2),
-        ).astype(F32)
-        owned_upward, owned_gating, owned_downward = owned[0], owned[1], owned[2].T
         grad_wo = jnp.einsum(
             "td,tmh->mdh", grad_branch_attn, merged_parts, preferred_element_type=F32
         ).astype(BF16)
-        owned_output = lax.psum_scatter(
-            grad_wo.reshape(size * chips * 2, rows, part), everyone, scatter_dimension=0
-        )
-        owned_output = owned_output.astype(F32).T
         dq, dk, dv, term, grad_gain = attend_back(
             low,
             qback,
@@ -1336,25 +1894,20 @@
         own = lax.dynamic_slice_in_dim(term, me * mine, mine, 1).astype(F32)
         own = own + grad_resid.reshape(mine, size, part).transpose(1, 0, 2)
         term = lax.dynamic_update_slice_in_dim(term, own.astype(BF16), me * mine, 1)
-        grad_hidden = sum_parts(term, 5)
-
-        grad_qkv = [
-            jnp.einsum("mtd,tf->mdf", wide, d, preferred_element_type=F32)
-            .astype(BF16)
-            .reshape(width, part)
-            for d in (dq, dk, dv)
-        ]
-        owned = lax.psum_scatter(
-            jnp.concatenate(grad_qkv, axis=1), DP, scatter_dimension=0, tiled=True
-        ).astype(F32)
+        grad_qkv = jnp.concatenate(
+            [
+                jnp.einsum("mtd,tf->mdf", wide, d, preferred_element_type=F32)
+                .astype(BF16)
+                .reshape(width, part)
+                for d in (dq, dk, dv)
+            ],
+            axis=1,
+        )
         out_pairs = (
             lambda w: w.reshape(w.shape[0], 2, heads, HALF)
             .transpose(0, 2, 1, 3)
             .reshape(w.shape[0], heads * DK)
         )
-        owned_query = out_pairs(owned[:, :part])
-        owned_keys = out_pairs(owned[:, part : 2 * part])
-        owned_values = owned[:, 2 * part :]
 
         zero = jnp.zeros((size, 2, units), F32)
         placed_u = lax.dynamic_update_slice(zero, grad_u, (0, core, 0))
@@ -1362,22 +1915,34 @@
         placed_qk = lax.dynamic_update_slice(
             jnp.zeros((size, part), F32), out_pairs(grad_gain), (me, 0)
         )
-        summed = lax.psum(
-            jnp.concatenate(
-                [
-                    placed_u.reshape(size, 2 * units),
-                    placed_v.reshape(size, 2 * units),
-                    placed_qk,
-                    grad_alpha_attn.reshape(size, part),
-                    grad_alpha_mlp.reshape(size, part),
-                ],
-                axis=1,
-            ),
-            everyone,
-        )
-        summed = lax.dynamic_index_in_dim(summed, me, 0, keepdims=False)
+        placed = jnp.concatenate(
+            [
+                placed_u.reshape(size, 2 * units),
+                placed_v.reshape(size, 2 * units),
+                placed_qk,
+                grad_alpha_attn.reshape(size, part),
+                grad_alpha_mlp.reshape(size, part),
+            ],
+            axis=1,
+        )
+        grad_hidden, owned, owned_output, owned_qkv, summed = sum_all(
+            term,
+            grads,
+            grad_wo.reshape(size, chips, 2, rows, part),
+            grad_qkv.reshape(chips, 2, rows, 3 * part),
+            placed[:, None],
+            chips,
+            5,
+        )
+        owned_upward, owned_gating, owned_downward = owned[0], owned[1], owned[2].T
+        owned_output = owned_output.T
+        owned_query = out_pairs(owned_qkv[:, :part])
+        owned_keys = out_pairs(owned_qkv[:, part : 2 * part])
+        owned_values = owned_qkv[:, 2 * part :]
         bounds = [2 * units, 4 * units, 4 * units + part, 4 * units + 2 * part]
-        summed_up, summed_gate, summed_qk, summed_attn, summed_mlp = jnp.split(summed, bounds)
+        summed_up, summed_gate, summed_qk, summed_attn, summed_mlp = jnp.split(
+            summed[0], bounds
+        )
         return (
             out_hidden[None],
             grad_hidden[None],

time: 1130 us -> 872 us (0.77)
  the two profiles are of different devices: /device:TPU:0 before, /device:TPU:17 now
where the time goes in v2:
time: 872 us; the launch traced here: 866 us
  Pallas kernels  709 us (81%)
  other arithmetic  62 us (7%)
  local copies, waits for them, and re-layouts  57.8 us (7%)
  matrix products  23.2 us (3%)
  starting transfers between devices  8.74 us (1%)
    pallas_call x1, Pallas kernels, sum_all(): pl.pallas_call(functools.partial(sum_all_kernel, size, chips, chunks, spl...  218 us
    pallas_call x1, Pallas kernels, gather_all(): pl.pallas_call(functools.partial(gather_all_kernel, size, chips, chunks,...  179 us
    pallas_call x1, Pallas kernels, attend_back(): pl.pallas_call(attend_back_kernel, grid_spec=pltpu.PrefetchScalarGridSpec...  85.7 us
    pallas_call x1, Pallas kernels, spread_tokens(): pl.pallas_call(functools.partial(spread_tokens_kernel, size), in_specs=[A...  58.1 us
    pallas_call x1, Pallas kernels, feed_grads(): pl.pallas_call(functools.partial(feed_grads_kernel, size), grid=(3, parts...  41.7 us
    pallas_call x1, Pallas kernels, feed(): pl.pallas_call(functools.partial(feed_kernel, size), grid=(tokens // bloc...  40.4 us
    pallas_call x1, Pallas kernels, feed_back(): pl.pallas_call(functools.partial(feed_back_kernel, size), grid=(tokens //...  40.2 us
    pallas_call x1, Pallas kernels, attend(): pl.pallas_call(attend_kernel, grid_spec=pltpu.PrefetchScalarGridSpec(num_...  25.2 us
  transfers between devices with their start and end apart: 5, of which 1 were waited for; matrix products, arithmetic and copies ran while one was open for 4% of the time, Pallas kernels for 0%

profile of v2, /device:TPU:17, one launch (start us, length us, event | category | flops | bytes accessed | tf_op | source)
XLA Modules:
  0.0 866.0 jit_solution(4516487272075840684)
XLA Ops:
  34.0 179.4 %gather_all.1 = (bf16[4,3072,256]{2,1,0:T(8,128)(2,1)}, bf16[8,128,768]{2,1,0:T(8,128)(2,1)}, bf16[4,4,896,512]{3,2,1,0:T(8,128)(2,1)}, f32[4,1,2560]{2,1,0:T(1,128)}) custom-call(bf16[3072,256]{1,0:T(8,128)(2,1)} %convert_bitcast_fusion.3.hidden, bf16[128,768]{1,0:T(8,128)(2,1)} %pad_maximum_fusion.6.qkv, bf16[896,512]{1,0:T(8,128)(2,1)} %pad_maximum_fusion.3.packed, ...), custom_call_target="tpu_custom_call" | custom-call | tf_op jit(solution)/shard_map/gather_all/pallas_call | solution.py:440
  213.4 20.0 %project.1 = (bf16[4,3072,128]{2,1,0:T(8,128)(2,1)}, bf16[4,3072,128]{2,1,0:T(8,128)(2,1)}, bf16[4,3072,128]{2,1,0:T(8,128)(2,1)}, f32[3072,128]{1,0:T(8,128)}, f32[3072,128]{1,0:T(8,128)}) custom-call(bf16[4,3072,256]{2,1,0:T(8,128)(2,1)} %get-tuple-element.48.wide, bf16[4,256,768]{2,1,0:T(8,128)(2,1)} %bitcast.213, f32[3072,128]{1,0:T(8,128)} %copy.72.cosine, ...), custom_call_target="tpu_custom_call" | custom-call | flops 4831838208 | bytes 20971520 | tf_op jit(solution)/shard_map/project/pallas_call | solution.py:988
  233.4 25.2 %attend.1 = (bf16[3072,256]{1,0:T(8,128)(2,1)}, bf16[4,3072,128]{2,1,0:T(8,128)(2,1)}) custom-call(s32[6]{0:T(128)} %and_select_fusion.low, bf16[4,3072,128]{2,1,0:T(8,128)(2,1)} %get-tuple-element.51.q, bf16[4,3072,128]{2,1,0:T(8,128)(2,1)} %get-tuple-element.52.k, bf16[4,3072,128]{2,1,0:T(8,128)(2,1)} %get-tuple-element.53.v, s32[3072,1]{1,0:T(8,128)} %copy.74.qdoc, ...), custom_call_target="tpu_custom_call" | custom-call | flops 40000000000 | bytes 16777216 | tf_op jit(solution)/shard_map/attend/pallas_call | solution.py:1074
  258.6 58.1 %spread_tokens.1 = bf16[768,1024]{1,0:T(8,128)(2,1)} custom-call(bf16[3072,256]{1,0:T(8,128)(2,1)} %get-tuple-element.54.source.attended), custom_call_target="tpu_custom_call" | custom-call | tf_op jit(solution)/shard_map/spread_tokens/pallas_call | solution.py:167
  316.7 2.6 copy.104
  323.3 4.0 fusion.3
  327.3 2.8 convert_bitcast_fusion
  333.6 5.9 collective-permute-start.1
  339.5 3.2 convert_bitcast_fusion.2.cotangent
  343.9 3.9 pad_maximum_fusion.x
  347.7 40.4 %feed.1 = (bf16[4,1536,512]{2,1,0:T(8,128)(2,1)}, bf16[4,1536,512]{2,1,0:T(8,128)(2,1)}, bf16[4,1536,512]{2,1,0:T(8,128)(2,1)}, bf16[1536,1024]{1,0:T(8,128)(2,1)}, bf16[768,1024]{1,0:T(8,128)(2,1)}) custom-call(bf16[1536,1024]{1,0:T(8,128)(2,1)} %pad_maximum_fusion.x, bf16[4,4,896,512]{3,2,1,0:T(8,128)(2,1)} %get-tuple-element.55.w_up.w_gate.w_down, ...), custom_call_target="tpu_custom_call" | custom-call | flops 19327352832 | bytes 62914560 | tf_op jit(solution)/shard_map/feed/pallas_call | solution.py:1459
  390.7 3.0 collective-permute-done.2
  397.5 3.1 multiply_reduce_fusion
  404.4 2.8 broadcast_select_fusion.kdoc
  407.2 3.9 pad_maximum_fusion.1.dbranch
  411.1 40.2 %feed_back.1 = (bf16[4,1536,512]{2,1,0:T(8,128)(2,1)}, bf16[4,1536,512]{2,1,0:T(8,128)(2,1)}, bf16[1536,1024]{1,0:T(8,128)(2,1)}, f32[4,1,512]{2,1,0:T(1,128)}, ...) custom-call(bf16[1536,1024]{1,0:T(8,128)(2,1)} %pad_maximum_fusion.1.dbranch, ...), custom_call_target="tpu_custom_call" | custom-call | flops 19327352832 | bytes 73400320 | tf_op jit(solution)/shard_map/feed_back/pallas_call | solution.py:1580
  451.3 2.7 slice.92
  455.2 3.5 bitcast_convert_fusion
  458.6 3.0 multiply_reduce_fusion.3
  461.7 4.3 broadcast_multiply_fusion
  470.8 3.1 convert_bitcast_fusion.1
  475.6 41.7 %feed_grads.1 = (bf16[4,4,768,512]{3,2,1,0:T(8,128)(2,1)}, bf16[3072,256]{1,0:T(8,128)(2,1)}) custom-call(bf16[1536,1024]{1,0:T(8,128)(2,1)} %pad_maximum_fusion.x, bf16[1536,1024]{1,0:T(8,128)(2,1)} %pad_maximum_fusion.1.dbranch, bf16[4,1536,512]{2,1,0:T(8,128)(2,1)} %get-tuple-element.62.dup, bf16[4,1536,512]{2,1,0:T(8,128)(2,1)} %get-tuple-element.63.dgate, ...), custom_call_target="tpu_custom_call" | custom-call | flops 19327352832 | bytes 41943040 | tf_op jit(solution)/shard_map/feed_grads/pallas_call | solution.py:1672
  517.3 85.7 %attend_back.1 = (bf16[3072,256]{1,0:T(8,128)(2,1)}, bf16[3072,256]{1,0:T(8,128)(2,1)}, bf16[3072,256]{1,0:T(8,128)(2,1)}, bf16[4,3072,256]{2,1,0:T(8,128)(2,1)}, f32[1,256]{1,0:T(1,128)}) custom-call(s32[6]{0:T(128)} %and_select_fusion.low, bf16[4,3072,128]{2,1,0:T(8,128)(2,1)} %get-tuple-element.61.qback, bf16[3072,256]{1,0:T(8,128)(2,1)} %get-tuple-element.66.dout, ...), custom_call_target="tpu_custom_call" | custom-call | flops 80000000000 | bytes 31457280 | tf_op jit(solution)/shard_map/attend_back/pallas_call | solution.py:1291
  605.9 6.0 fusion.15
  611.9 5.6 fusion.18
  617.5 2.6 fusion.21
  620.2 4.1 copy.85
  624.2 2.4 copy.82
  626.6 2.4 copy.83
  629.0 3.1 fusion.8.term
  633.4 218.1 %sum_all.1 = (f32[3072,256]{1,0:T(8,128)}, f32[3,128,1024]{2,1,0:T(8,128)}, f32[128,256]{1,0:T(8,128)}, f32[128,768]{1,0:T(8,128)}, f32[1,2816]{1,0:T(1,128)}) custom-call(bf16[4,3072,256]{2,1,0:T(8,128)(2,1)} %fusion.8.term, bf16[4,4,768,512]{3,2,1,0:T(8,128)(2,1)} %get-tuple-element.70.grads, bf16[4,4,2,128,256]{4,3,2,1,0:T(8,128)(2,1)} %bitcast.162, ...), custom_call_target="tpu_custom_call" | custom-call | tf_op jit(solution)/shard_map/sum_all/pallas_call | solution.py:871
  854.0 2.7 slice_bitcast_fusion
  (188 shorter events, 74.3 us)
Async XLA Ops:
  0.6 6.3 copy-start.22
  4.0 7.1 copy-start.10
  9.8 5.7 copy-start.27
  9.8 5.7 copy-start.21
  9.8 21.1 %collective-permute-start = (bf16[448,512]{1,0:T(8,128)(2,1)}, bf16[448,512]{1,0:T(8,128)(2,1)}, u32[]{:S(2)}, u32[]{:S(2)}) collective-permute-start(bf16[448,512]{1,0:T(8,128)(2,1)} %pad_maximum_fusion.5), channel_id=1, source_target_pairs={{0,4},{4,0},{1,5},{5,1},{2,6},{6,2},{3,7},{7,3},{8,12},{12,8},{9,1... | collective-permute-start | bytes 1376264 | tf_op jit(solution)/shard_map/ppermute | solution.py:1736
  25.6 1.8 copy-start.28
  327.3 3.7 copy-start.2
  330.5 1.7 copy-start.4
  333.6 10.3 %collective-permute-start.1 = (bf16[768,1024]{1,0:T(8,128)(2,1)}, bf16[768,1024]{1,0:T(8,128)(2,1)}, u32[]{:S(2)}, u32[]{:S(2)}) collective-permute-start(bf16[768,1024]{1,0:T(8,128)(2,1)} %multiply_convert_fusion.3), channel_id=1, source_target_pairs={{0,4},{4,0},{1,5},{5,1},{2,6},{6,2},{3,7},{7,3},{8,12},{12,8},{9,1... | collective-permute-start | bytes 4718600 | tf_op jit(solution)/shard_map/ppermute | solution.py:1736
  388.1 5.6 copy-start.6
  389.8 3.9 collective-permute-start.2
  400.6 2.2 copy-start
  402.7 4.5 collective-permute-start.3
  451.2 3.7 copy-start.24
  451.2 3.7 copy-start.26
  451.3 3.8 copy-start.25
  453.9 4.7 collective-permute-start.4
  455.1 3.5 copy-start.1
  458.6 3.0 copy-start.8
  461.7 4.3 copy-start.3
  461.7 4.3 copy-start.5
  467.3 1.6 copy-start.12
  468.9 1.9 copy-start.18
  605.9 6.0 copy-start.17
  605.9 11.6 %slice-start = ((s8[6291456]{0:T(1024)(128)(4,1)}), s8[4194304]{0:T(1024)(128)(4,1)S(1)}, s32[]{:S(2)}) async-start(s8[6291456]{0:T(1024)(128)(4,1)} %bitcast.157), calls=%async_computation | async-start | bytes 8388608
  611.9 5.6 slice-start.1
  611.9 5.6 copy-start.16
  620.2 4.1 copy-start.7
  629.0 3.1 copy-start.13
  629.0 3.1 copy-start.14
  629.0 3.1 copy-start.15
  854.0 9.8 %copy-start.11 = (f32[3072,256]{1,0:T(8,128)S(1)}, f32[3072,256]{1,0:T(8,128)}, u32[]{:S(2)}) copy-start(f32[3072,256]{1,0:T(8,128)} %get-tuple-element.77) | copy-start | bytes 9437188
  (4 other events, 4.2 us)

commit v3 on v2

--- a/solution.py
+++ b/solution.py
@@ -143,36 +143,6 @@
 
 def column_part(columns):
     return lambda ref, j: ref.at[:, pl.ds(pl.multiple_of(j * columns, columns), columns)]
-
-
-def spread_tokens_kernel(size, source, target, send, receive, local):
-    greet_all(size)
-    tokens, part = source.shape
-    exchange = Exchange(
-        size,
-        source,
-        target,
-        row_part(tokens // size),
-        column_part(part),
-        send,
-        receive,
-        local,
-    )
-    exchange.start()
-    exchange.wait()
-
-
-def spread_tokens(value, size, collective):
-    tokens, part = value.shape
-    return pl.pallas_call(
-        functools.partial(spread_tokens_kernel, size),
-        in_specs=[ANY],
-        out_specs=ANY,
-        out_shape=jax.ShapeDtypeStruct((tokens // size, size * part), value.dtype),
-        scratch_shapes=exchange_semaphores(size),
-        compiler_params=remote_params(collective),
-        name="spread_tokens",
-    )(value)
 
 
 class Gather:
@@ -314,35 +284,21 @@
         ]
 
     own[0].wait()
-    gather_qkv.start(0)
-
-    @pl.when(me < size - 1)
-    def _():
-        packed_hop(me, packed, me + 1, packed_up).start()
-
-    @pl.when(me > 0)
-    def _():
-        packed_hop(me, packed, me - 1, packed_down).start()
-
     own[1].wait()
-    for half in plane(me, 0):
-        half.start(0)
-    for chunk in range(chunks):
-
-        @pl.when(me < size - 1)
-        def _():
-            hidden_hop(me, chunk, hidden, me + 1, hidden_up).start()
-
-        @pl.when(me > 0)
-        def _():
-            hidden_hop(me, chunk, hidden, me - 1, hidden_down).start()
-
-    for copy in vector_copies:
-        copy.start()
-    for stage in range(stages + 1):
-        gather_qkv.arrive(stage)
-        if stage < stages:
-            gather_qkv.start(stage + 1)
+
+    def pass_on(origin, upward):
+        block = full.at[origin, chip]
+        if upward is not False:
+
+            @pl.when(me < size - 1)
+            def _():
+                packed_hop(origin, block, me + 1, packed_up).start()
+
+        if not upward:
+
+            @pl.when(me > 0)
+            def _():
+                packed_hop(origin, block, me - 1, packed_down).start()
 
     def advance(distance, stage):
         for exists, origin, slot, _ in sources[distance]:
@@ -353,27 +309,42 @@
                     half.arrive(stage)
                     half.start(stage + 1)
 
+    pass_on(me, None)
+    gather_qkv.start(0)
+    for half in plane(me, 0):
+        half.start(0)
+    for copy in vector_copies:
+        copy.start()
+    for stage in range(stages):
+        gather_qkv.arrive(stage)
+        gather_qkv.start(stage + 1)
+    advance(0, 0)
     for distance in range(1, size):
         for exists, origin, slot, upward in sources[distance]:
 
             @pl.when(exists)
             def _():
-                block = full.at[origin, chip]
-                packed_hop(origin, block, me, packed_up).wait_recv()
-                if upward:
-
-                    @pl.when(me < size - 1)
-                    def _():
-                        packed_hop(origin, block, me + 1, packed_up).start()
-                else:
-
-                    @pl.when(me > 0)
-                    def _():
-                        packed_hop(origin, block, me - 1, packed_down).start()
-
+                packed_hop(origin, full.at[origin, chip], me, packed_up).wait_recv()
+                pass_on(origin, upward)
                 for half in plane(origin, slot):
                     half.start(0)
 
+        @pl.when(jnp.maximum(me, size - 1 - me) == distance)
+        def _():
+            for chunk in range(chunks):
+
+                @pl.when(me < size - 1)
+                def _():
+                    hidden_hop(me, chunk, hidden, me + 1, hidden_up).start()
+
+                @pl.when(me > 0)
+                def _():
+                    hidden_hop(me, chunk, hidden, me - 1, hidden_down).start()
+
+        if distance > 1:
+            advance(distance - 1, 0)
+    advance(size - 1, 0)
+    for distance in range(1, size):
         for chunk in range(chunks):
             for exists, origin, _, upward in sources[distance]:
 
@@ -392,12 +363,10 @@
                         def _():
                             hidden_hop(origin, chunk, block, me - 1, hidden_down).start()
 
-            if chunk == chunks // 3:
-                for stage in range(stages - 1):
-                    advance(distance - 1, stage)
-        advance(distance - 1, stages - 1)
-    for stage in range(stages):
-        advance(size - 1, stage)
+    for stage in range(1, stages):
+        for distance in range(size):
+            advance(distance, stage)
+    gather_qkv.arrive(stages)
 
     own[2].wait()
     own[3].wait()
@@ -682,7 +651,7 @@
     )
     sum_wo = ChipSum(
         size,
-        bits,
+        bits[::-1],
         lambda m, c: pair_wo.at[m, c],
         acc_wo,
         got_wo,
@@ -1141,16 +1110,17 @@
     collect_plain,
     collect_pair,
     sums,
-    dq_out,
-    dk_out,
-    dv_out,
+    wide,
+    grad_resid,
     term_out,
+    grad_qkv,
     gain_out,
     dk,
     dv,
     dq,
     dox,
     dq_low,
+    total_qkv,
 ):
     heads, rows, _ = qback.shape
     steps = pl.num_programs(0) // 2
@@ -1219,7 +1189,6 @@
             grad, unit, gain[...], rq[...], cosine[...], sine[...], sums[...]
         )
         gain_out[...] += grad_gain
-        dq_out[...] = raw
         dq_low[pl.ds(pl.multiple_of(index * rows, rows), rows), :] = raw
 
     @pl.when(step_at >= steps)
@@ -1234,17 +1203,41 @@
             grad, keys / gain[...], gain[...], rk[...], cosine[...], sine[...], sums[...]
         )
         gain_out[...] += grad_gain
-        dk_out[...] = raw
         dvalues = gather_heads(
             [dv[head, slots, :] for head in range(heads)], collect_plain, heads
         ).astype(BF16)
-        dv_out[...] = dvalues
-        dquery = dq_low[slots, :]
-        for part in range(weight.shape[0]):
-            term = dot(dquery, weight[part, :, :width], NT)
-            term += dot(raw, weight[part, :, width : 2 * width], NT)
-            term += dot(dvalues, weight[part, :, 2 * width :], NT)
-            term_out[part] = term.astype(BF16)
+        together = jnp.concatenate([dq_low[slots, :], raw, dvalues], axis=1)
+        parts, part = weight.shape[:2]
+        for member in range(parts):
+            term_out[member] = dot(together, weight[member], NT).astype(BF16)
+            product = dot(wide[member], together, TN)
+
+            @pl.when(index == 0)
+            def _():
+                total_qkv[member] = product
+
+            @pl.when(index > 0)
+            def _():
+                total_qkv[member] += product
+
+        strip = STRIP
+        first = low[steps] * (grad_resid.shape[0] // strip)
+        for half in range(rows // strip):
+            number = index * (rows // strip) + half - first
+
+            @pl.when((number >= 0) & (number < grad_resid.shape[0] // strip))
+            def _():
+                at = pl.ds(half * strip, strip)
+                own = pl.ds(pl.multiple_of(number * strip, strip), strip)
+                for member in range(parts):
+                    term_out[member, at, :] = (
+                        term_out[member, at, :].astype(F32)
+                        + grad_resid[own, member * part : (member + 1) * part].astype(F32)
+                    ).astype(BF16)
+
+        @pl.when(index == steps - 1)
+        def _():
+            grad_qkv[...] = total_qkv[...].astype(BF16)
 
 
 def attend_back(
@@ -1266,6 +1259,8 @@
     collect_plain,
     collect_pair,
     sums,
+    wide,
+    grad_resid,
 ):
     heads, tokens, _ = k.shape
     block = qdoc.shape[2]
@@ -1311,12 +1306,12 @@
                 whole(collect_plain),
                 whole(collect_pair),
                 whole(sums),
+                pl.BlockSpec((parts, block, part), lambda i, low: (0, after(i), 0)),
+                whole(grad_resid),
             ],
             out_specs=[
-                rows(width, now),
-                rows(width, after),
-                rows(width, after),
                 pl.BlockSpec((parts, block, part), lambda i, low: (0, after(i), 0)),
+                pl.BlockSpec((parts, part, 3 * width), lambda i, low: (0, 0, 0)),
                 pl.BlockSpec((1, width), lambda i, low: (0, 0)),
             ],
             scratch_shapes=[
@@ -1325,13 +1320,12 @@
                 pltpu.VMEM((heads, block, EXT), F32),
                 pltpu.VMEM((heads, block, EXT), BF16),
                 pltpu.VMEM((tokens, width), BF16),
+                pltpu.VMEM((parts, part, 3 * width), F32),
             ],
         ),
         out_shape=[
-            jax.ShapeDtypeStruct((tokens, width), BF16),
-            jax.ShapeDtypeStruct((tokens, width), BF16),
-            jax.ShapeDtypeStruct((tokens, width), BF16),
             jax.ShapeDtypeStruct((parts, tokens, part), BF16),
+            jax.ShapeDtypeStruct((parts, part, 3 * width), BF16),
             jax.ShapeDtypeStruct((1, width), F32),
         ],
         compiler_params=grid_params(1),
@@ -1358,7 +1352,184 @@
         collect_plain,
         collect_pair,
         sums,
+        wide,
+        grad_resid,
     )
+
+
+def row_scale(value):
+    return lax.rsqrt(jnp.sum(value * value, axis=-1, keepdims=True) + EPSILON)
+
+
+def residual_backward(grad_out, result, resid, unit, alpha, branch_scale, mixed_scale):
+    grad_mixed = mixed_scale * (
+        grad_out - result * jnp.sum(grad_out * result, axis=-1, keepdims=True)
+    )
+    grad_alpha = jnp.sum(grad_mixed * (unit - resid), axis=0, keepdims=True)
+    grad_unit = grad_mixed * alpha
+    grad_branch = branch_scale * (
+        grad_unit - unit * jnp.sum(grad_unit * unit, axis=-1, keepdims=True)
+    )
+    return grad_mixed * (1.0 - alpha), grad_branch, grad_alpha
+
+
+STRIP = 256
+
+
+def strips(rows):
+    strip = min(STRIP, rows)
+    return [pl.ds(start, strip) for start in range(0, rows, strip)]
+
+
+def core_semaphores(count):
+    return [pltpu.SemaphoreType.DMA((count,)), pltpu.SemaphoreType.DMA((count,))]
+
+
+def greet_pair_and_line(size):
+    me, core = lax.axis_index("mp"), lax.axis_index("core")
+    for k in range(1, size):
+        greet({"mp": flip(me, k)})
+    greet({"core": 1 - core})
+    pl.semaphore_wait(pltpu.get_barrier_semaphore(), size)
+
+
+def output_matrix(packed_wo, whole):
+    size, chips, rows, both = packed_wo.shape
+    part = both // 2
+    for chip in range(chips):
+        for core in range(2):
+            start = (2 * chip + core) * rows
+            whole[:, start : start + rows, :] = packed_wo[
+                :, chip, :, core * part : (core + 1) * part
+            ]
+
+
+def mix_kernel(
+    size,
+    attended,
+    packed,
+    wide,
+    alpha,
+    cotangent,
+    x,
+    middle_out,
+    unit_out,
+    branch_scale_out,
+    mixed_scale_out,
+    merged,
+    full_wo,
+    resid_out,
+    cotangent_low,
+    packed_wo,
+    middle_low,
+    resid,
+    send,
+    receive,
+    local,
+    own_sems,
+    core_sent,
+    core_got,
+):
+    me, core = lax.axis_index("mp"), lax.axis_index("core")
+    mine, width = middle_out.shape
+    part = width // size
+    rows = packed_wo.shape[2]
+    greet_pair_and_line(size)
+    exchange = Exchange(
+        size, attended, merged, row_part(mine), column_part(part), send, receive, local
+    )
+    exchange.start()
+    own = [
+        pltpu.make_async_copy(
+            packed.at[:, :, pl.ds(packed.shape[2] - rows, rows), :], packed_wo, own_sems.at[0]
+        )
+    ]
+    for member in range(size):
+        own.append(
+            pltpu.make_async_copy(
+                wide.at[member, pl.ds(pl.multiple_of(me * mine, mine), mine), :],
+                resid.at[:, pl.ds(member * part, part)],
+                own_sems.at[1 + member],
+            )
+        )
+    for copy in own:
+        copy.start()
+    for at in strips(cotangent.shape[0]):
+        cotangent_low[at, :] = cotangent[at, :].astype(BF16)
+    for copy in own:
+        copy.wait()
+    output_matrix(packed_wo, full_wo)
+    resid_out[...] = resid[...]
+    exchange.wait()
+
+    swaps = []
+    for order, at in enumerate(strips(mine)):
+        branch = dot(merged[at, :part], full_wo[0], NT)
+        for member in range(1, size):
+            branch += dot(
+                merged[at, member * part : (member + 1) * part], full_wo[member], NT
+            )
+        old = resid[at, :].astype(F32)
+        branch_scale = row_scale(branch)
+        unit = branch * branch_scale
+        mixed = old + alpha[...] * (unit - old)
+        mixed_scale = row_scale(mixed)
+        middle = mixed * mixed_scale
+        middle_out[at, :] = middle
+        unit_out[at, :] = unit.astype(BF16)
+        branch_scale_out[at, :] = branch_scale
+        mixed_scale_out[at, :] = mixed_scale
+        middle_low[at, :] = middle.astype(BF16)
+        there = pl.ds(mine + at.start, at.size)
+        swap = to_device(
+            middle_low.at[at, :],
+            x.at[there, :],
+            core_sent.at[order],
+            core_got.at[order],
+            {"core": 1 - core},
+        )
+        swap.start()
+        swaps.append(swap)
+    keep = pltpu.make_async_copy(middle_low, x.at[pl.ds(0, mine), :], own_sems.at[0])
+    keep.start()
+    keep.wait()
+    for swap in swaps:
+        swap.wait()
+
+
+def mix(attended, packed, rows, wide, alpha, cotangent, collective):
+    size, slots, part = wide.shape
+    chips = packed.shape[1]
+    mine, width = slots // size, size * part
+    vmem = pl.BlockSpec(memory_space=pltpu.VMEM)
+    count = len(strips(mine))
+    scale = jax.ShapeDtypeStruct((mine, 1), F32)
+    return pl.pallas_call(
+        functools.partial(mix_kernel, size),
+        in_specs=[ANY, ANY, ANY, vmem, vmem],
+        out_specs=[ANY, *[vmem] * 8],
+        out_shape=[
+            jax.ShapeDtypeStruct((2 * mine, width), BF16),
+            jax.ShapeDtypeStruct((mine, width), F32),
+            jax.ShapeDtypeStruct((mine, width), BF16),
+            scale,
+            scale,
+            jax.ShapeDtypeStruct((mine, width), BF16),
+            jax.ShapeDtypeStruct((size, width, part), BF16),
+            jax.ShapeDtypeStruct((mine, width), BF16),
+            jax.ShapeDtypeStruct((slots, part), BF16),
+        ],
+        scratch_shapes=[
+            pltpu.VMEM((size, chips, rows, 2 * part), BF16),
+            pltpu.VMEM((mine, width), BF16),
+            pltpu.VMEM((mine, width), BF16),
+            *exchange_semaphores(size),
+            pltpu.SemaphoreType.DMA((1 + size,)),
+            *core_semaphores(count),
+        ],
+        compiler_params=remote_params(collective),
+        name="mix",
+    )(attended, packed, wide, alpha, cotangent)
 
 
 def whole_matrix(ref):
@@ -1373,6 +1544,12 @@
 def last_step():
     return (pl.program_id(0) == pl.num_programs(0) - 1) & (
         pl.program_id(1) == pl.num_programs(1) - 1
+    )
+
+
+def swap_cores(source, target, sems):
+    return to_device(
+        source, target, sems[0], sems[1], {"core": 1 - lax.axis_index("core")}
     )
 
 
@@ -1385,15 +1562,26 @@
     s_u,
     s_v,
     cotangent,
+    middle,
+    alpha,
     up_out,
     gate_out,
     units_out,
-    branch,
+    result_out,
+    grad_middle,
+    dbranch,
+    grad_alpha,
+    acc,
+    given,
+    got,
     spread,
-    acc,
+    low,
     send,
     receive,
     local,
+    core_sent,
+    core_got,
+    keep_sems,
 ):
     exchange = Exchange(
         size,
@@ -1405,13 +1593,14 @@
         receive,
         local,
     )
+    branch_swap = swap_cores(given, got, (core_sent.at[0], core_got.at[0]))
 
     @pl.when(first_step())
     def _():
-        greet_all(size)
+        greet_pair_and_line(size)
         exchange.start()
 
-    part = pl.program_id(1)
+    block, part = pl.program_id(0), pl.program_id(1)
     up = dot(x[...], whole_matrix(w_up))
     gate = dot(x[...], whole_matrix(w_gate))
     up_out[0] = up.astype(BF16)
@@ -1429,13 +1618,58 @@
     def _():
         acc[...] += term
 
-    @pl.when(part == pl.num_programs(1) - 1)
+    last = part == pl.num_programs(1) - 1
+
+    @pl.when(last & (block == 0))
     def _():
-        branch[...] = acc[...].astype(BF16)
-
-    @pl.when(last_step())
+        given[...] = acc[...].astype(BF16)
+        branch_swap.start()
+
+    @pl.when(last & (block == 1))
     def _():
+        mine = acc.shape[0]
+        branch_swap.wait()
         exchange.wait()
+        swaps = []
+        for order, at in enumerate(strips(mine)):
+            branch = acc[at, :] + got[at, :].astype(F32)
+            branch_scale = row_scale(branch)
+            unit = branch * branch_scale
+            old = middle[at, :]
+            mixed = old + alpha[...] * (unit - old)
+            mixed_scale = row_scale(mixed)
+            result = mixed * mixed_scale
+            result_out[at, :] = result.astype(BF16)
+            grad_old, grad_branch, part_alpha = residual_backward(
+                spread[at, :].astype(F32),
+                result,
+                old,
+                unit,
+                alpha[...],
+                branch_scale,
+                mixed_scale,
+            )
+            grad_middle[at, :] = grad_old
+            if order == 0:
+                grad_alpha[...] = part_alpha
+            else:
+                grad_alpha[...] += part_alpha
+            low[at, :] = grad_branch.astype(BF16)
+            there = pl.ds(mine + at.start, at.size)
+            swaps.append(
+                swap_cores(
+                    low.at[at, :],
+                    dbranch.at[there, :],
+                    (core_sent.at[1 + order], core_got.at[1 + order]),
+                )
+            )
+            swaps.append(
+                pltpu.make_async_copy(low.at[at, :], dbranch.at[at, :], keep_sems.at[order])
+            )
+            swaps[-2].start()
+            swaps[-1].start()
+        for swap in swaps:
+            swap.wait()
 
 
 def packed_specs(packed, width):
@@ -1446,35 +1680,48 @@
     ]
 
 
-def feed(x, packed, s_u, s_v, cotangent, collective):
+def feed(x, packed, s_u, s_v, cotangent, middle, alpha, collective):
     tokens, width = x.shape
     parts, _, _, units = packed.shape
     size = parts
-    block = min(512, tokens)
-    rows = pl.BlockSpec((block, width), lambda t, m: (t, 0))
+    block = tokens // 2
+    rows = pl.BlockSpec((block, width), lambda t, m: (1 - t, 0))
     vector = pl.BlockSpec((1, 1, units), lambda t, m: (m, 0, 0))
-    piece = pl.BlockSpec((1, block, units), lambda t, m: (m, t, 0))
+    piece = pl.BlockSpec((1, block, units), lambda t, m: (m, 1 - t, 0))
+    vmem = pl.BlockSpec(memory_space=pltpu.VMEM)
     hidden = jax.ShapeDtypeStruct((parts, tokens, units), BF16)
-    slots, part = cotangent.shape
+    count = len(strips(block))
+    low = pltpu.VMEM((block, width), BF16)
     return pl.pallas_call(
         functools.partial(feed_kernel, size),
-        grid=(tokens // block, parts),
-        in_specs=[rows, *packed_specs(packed, width), vector, vector, ANY],
-        out_specs=[piece, piece, piece, rows, ANY],
+        grid=(2, parts),
+        in_specs=[rows, *packed_specs(packed, width), vector, vector, ANY, vmem, vmem],
+        out_specs=[piece, piece, piece, vmem, vmem, ANY, vmem],
         out_shape=[
             hidden,
             hidden,
             hidden,
+            jax.ShapeDtypeStruct((block, width), BF16),
+            jax.ShapeDtypeStruct((block, width), F32),
             jax.ShapeDtypeStruct((tokens, width), BF16),
-            jax.ShapeDtypeStruct((slots // size, size * part), BF16),
+            jax.ShapeDtypeStruct((1, width), F32),
         ],
-        scratch_shapes=[pltpu.VMEM((block, width), F32), *exchange_semaphores(size)],
+        scratch_shapes=[
+            pltpu.VMEM((block, width), F32),
+            low,
+            low,
+            low,
+            low,
+            *exchange_semaphores(size),
+            *core_semaphores(1 + count),
+            pltpu.SemaphoreType.DMA((count,)),
+        ],
         compiler_params=remote_params(collective),
         cost_estimate=pl.CostEstimate(
             flops=6 * tokens * width * parts * units, bytes_accessed=60 << 20, transcendentals=0
         ),
         name="feed",
-    )(x, packed, packed, packed, s_u, s_v, cotangent)
+    )(x, packed, packed, packed, s_u, s_v, cotangent, middle, alpha)
 
 
 def feed_back_kernel(
@@ -1488,18 +1735,33 @@
     up_in,
     gate_in,
     result,
+    grad_middle,
+    middle,
+    resid,
+    unit,
+    branch_scale,
+    mixed_scale,
+    alpha,
+    full_wo,
     dup_out,
     dgate_out,
-    dx,
     grad_u,
     grad_v,
     spread,
+    grad_resid,
+    dbranch_attn,
+    dmerged,
+    grad_alpha,
     acc,
+    given,
+    got,
     sum_u,
     sum_v,
     send,
     receive,
     local,
+    core_sent,
+    core_got,
 ):
     exchange = Exchange(
         size,
@@ -1511,14 +1773,14 @@
         receive,
         local,
     )
+    dx_swap = swap_cores(given, got, (core_sent.at[0], core_got.at[0]))
 
     @pl.when(first_step())
     def _():
-        greet_all(size)
+        greet_pair_and_line(size)
         exchange.start()
 
-    block = pl.program_id(0)
-    part = pl.program_id(1)
+    block, part = pl.program_id(0), pl.program_id(1)
     dunits = dot(dbranch[...], whole_matrix(w_down))
     up = up_in[0].astype(F32)
     gate = gate_in[0].astype(F32)
@@ -1554,54 +1816,130 @@
     def _():
         acc[...] += term
 
-    @pl.when(part == pl.num_programs(1) - 1)
+    last = part == pl.num_programs(1) - 1
+
+    @pl.when(last & (block == 0))
     def _():
-        dx[...] = acc[...].astype(BF16)
-
-    @pl.when(last_step())
+        given[...] = acc[...].astype(BF16)
+        dx_swap.start()
+
+    @pl.when(last & (block == 1))
     def _():
         grad_u[...] = sum_u[...]
         grad_v[...] = sum_v[...]
+        dx_swap.wait()
+        for order, at in enumerate(strips(acc.shape[0])):
+            grad_old, grad_branch, part_alpha = residual_backward(
+                grad_middle[at, :] + acc[at, :] + got[at, :].astype(F32),
+                middle[at, :],
+                resid[at, :].astype(F32),
+                unit[at, :].astype(F32),
+                alpha[...],
+                branch_scale[at, :],
+                mixed_scale[at, :],
+            )
+            grad_resid[at, :] = grad_old.astype(BF16)
+            if order == 0:
+                grad_alpha[...] = part_alpha
+            else:
+                grad_alpha[...] += part_alpha
+            low = grad_branch.astype(BF16)
+            dbranch_attn[at, :] = low
+            columns = full_wo.shape[2]
+            for member in range(size):
+                dmerged[at, member * columns : (member + 1) * columns] = dot(
+                    low, full_wo[member]
+                ).astype(BF16)
         exchange.wait()
 
 
-def feed_back(dbranch, packed, s_u, s_v, up, gate, result, collective):
+def feed_back(
+    dbranch,
+    packed,
+    s_u,
+    s_v,
+    up,
+    gate,
+    result,
+    grad_middle,
+    middle,
+    resid,
+    unit,
+    branch_scale,
+    mixed_scale,
+    alpha,
+    full_wo,
+    collective,
+):
     tokens, width = dbranch.shape
     parts, _, _, units = packed.shape
     size = parts
-    block = min(512, tokens)
-    rows = pl.BlockSpec((block, width), lambda t, m: (t, 0))
+    block = tokens // 2
+    rows = pl.BlockSpec((block, width), lambda t, m: (1 - t, 0))
     vector = pl.BlockSpec((1, 1, units), lambda t, m: (m, 0, 0))
-    piece = pl.BlockSpec((1, block, units), lambda t, m: (m, t, 0))
-    vectors = pl.BlockSpec((parts, 1, units), lambda t, m: (0, 0, 0))
+    piece = pl.BlockSpec((1, block, units), lambda t, m: (m, 1 - t, 0))
+    vmem = pl.BlockSpec(memory_space=pltpu.VMEM)
     hidden = jax.ShapeDtypeStruct((parts, tokens, units), BF16)
     sums = jax.ShapeDtypeStruct((parts, 1, units), F32)
-    mine = result.shape[0]
+    state = jax.ShapeDtypeStruct((block, width), BF16)
     return pl.pallas_call(
         functools.partial(feed_back_kernel, size),
-        grid=(tokens // block, parts),
-        in_specs=[rows, *packed_specs(packed, width), vector, vector, piece, piece, ANY],
-        out_specs=[piece, piece, rows, vectors, vectors, ANY],
+        grid=(2, parts),
+        in_specs=[
+            rows,
+            *packed_specs(packed, width),
+            vector,
+            vector,
+            piece,
+            piece,
+            ANY,
+            *[vmem] * 8,
+        ],
+        out_specs=[piece, piece, vmem, vmem, ANY, vmem, vmem, vmem, vmem],
         out_shape=[
             hidden,
             hidden,
-            jax.ShapeDtypeStruct((tokens, width), BF16),
             sums,
             sums,
-            jax.ShapeDtypeStruct((size * mine, width // size), BF16),
+            jax.ShapeDtypeStruct((size * block, width // size), BF16),
+            state,
+            state,
+            state,
+            jax.ShapeDtypeStruct((1, width), F32),
         ],
         scratch_shapes=[
             pltpu.VMEM((block, width), F32),
+            pltpu.VMEM((block, width), BF16),
+            pltpu.VMEM((block, width), BF16),
             pltpu.VMEM((parts, 1, units), F32),
             pltpu.VMEM((parts, 1, units), F32),
             *exchange_semaphores(size),
+            *core_semaphores(1),
         ],
         compiler_params=remote_params(collective),
         cost_estimate=pl.CostEstimate(
             flops=6 * tokens * width * parts * units, bytes_accessed=70 << 20, transcendentals=0
         ),
         name="feed_back",
-    )(dbranch, packed, packed, packed, s_u, s_v, up, gate, result)
+    )(
+        dbranch,
+        packed,
+        packed,
+        packed,
+        s_u,
+        s_v,
+        up,
+        gate,
+        result,
+        grad_middle,
+        middle,
+        resid,
+        unit,
+        branch_scale,
+        mixed_scale,
+        alpha,
+        full_wo,
+    )
 
 
 def feed_grads_kernel(
@@ -1611,11 +1949,15 @@
     dup,
     dgate,
     units,
+    dbranch_attn,
+    merged,
     dmerged,
     grads,
+    grad_wo,
     dattended,
     x_turned,
     d_turned,
+    attn_turned,
     send,
     receive,
     local,
@@ -1637,6 +1979,7 @@
         exchange.start()
         x_turned[...] = x[...].T
         d_turned[...] = dbranch[...].T
+        attn_turned[...] = dbranch_attn[...].T
 
     _, chips, rows, _ = grads.shape
     for which, left, right in (
@@ -1650,37 +1993,67 @@
             total = dot(left[...], right[0])
             grads[0] = total.astype(BF16).reshape(chips, rows, total.shape[1])
 
+    @pl.when(pl.program_id(0) == 3)
+    def _():
+        total = dot(attn_turned[...], merged[...])
+        grad_wo[...] = total.astype(BF16).reshape(grad_wo.shape)
+
     @pl.when(last_step())
     def _():
         exchange.wait()
 
 
-def feed_grads(x, dbranch, dup, dgate, units_in, dmerged, chips, collective):
+def feed_grads(
+    x, dbranch, dup, dgate, units_in, dbranch_attn, merged, dmerged, chips, collective
+):
     tokens, width = x.shape
     parts, _, units = dup.shape
     size = parts
     rows = width // chips
     mine = dmerged.shape[0]
-    whole = pl.BlockSpec((tokens, width), lambda w, m: (0, 0))
+    part = width // size
+
+    def whole(array):
+        return pl.BlockSpec(array.shape, lambda w, m: (0, 0))
+
+    def turn(w, m, which):
+        return jnp.where(w == which, m, jnp.where(w < which, 0, parts - 1))
 
     def piece(which):
-        def at(w, m):
-            return (jnp.where(w == which, m, jnp.where(w < which, 0, parts - 1)), 0, 0)
-
-        return pl.BlockSpec((1, tokens, units), at)
+        return pl.BlockSpec((1, tokens, units), lambda w, m: (turn(w, m, which), 0, 0))
 
     return pl.pallas_call(
         functools.partial(feed_grads_kernel, size),
-        grid=(3, parts),
-        in_specs=[whole, whole, piece(0), piece(1), piece(2), ANY],
-        out_specs=[pl.BlockSpec((1, chips, rows, units), lambda w, m: (m, 0, w, 0)), ANY],
+        grid=(4, parts),
+        in_specs=[
+            whole(x),
+            whole(dbranch),
+            piece(0),
+            piece(1),
+            piece(2),
+            whole(dbranch_attn),
+            pl.BlockSpec((mine, part), lambda w, m: (0, turn(w, m, 3))),
+            ANY,
+        ],
+        out_specs=[
+            pl.BlockSpec(
+                (1, chips, rows, units),
+                lambda w, m: (jnp.where(w < 3, m, parts - 1), 0, jnp.minimum(w, 2), 0),
+            ),
+            pl.BlockSpec(
+                (1, chips, 2, rows // 2, part), lambda w, m: (turn(w, m, 3), 0, 0, 0, 0)
+            ),
+            ANY,
+        ],
         out_shape=[
             jax.ShapeDtypeStruct((parts, chips, 3 * rows, units), BF16),
-            jax.ShapeDtypeStruct((size * mine, width // size), BF16),
+            jax.ShapeDtypeStruct((parts, chips, 2, rows // 2, part), BF16),
+            jax.ShapeDtypeStruct((size * mine, part), BF16),
         ],
         scratch_shapes=[
             pltpu.VMEM((width, tokens), BF16),
             pltpu.VMEM((width, tokens), BF16),
+            pltpu.VMEM((width, mine), BF16),
             *exchange_semaphores(size),
         ],
         compiler_params=remote_params(collective),
@@ -1688,7 +2061,7 @@
             flops=6 * tokens * width * parts * units, bytes_accessed=40 << 20, transcendentals=0
         ),
         name="feed_grads",
-    )(x, dbranch, dup, dgate, units_in, dmerged)
+    )(x, dbranch, dup, dgate, units_in, dbranch_attn, merged, dmerged)
 
 
 def rope_tables(positions, head_size):
@@ -1704,32 +2077,6 @@
     earlier = jnp.concatenate([doc_ids[..., :1] - 1, doc_ids[..., :-1]], axis=-1)
     starts = jnp.where(doc_ids != earlier, slot_index, jnp.zeros_like(slot_index))
     return lax.cummax(starts, axis=starts.ndim - 1)
-
-
-def row_scale(value):
-    return lax.rsqrt(jnp.sum(value * value, axis=-1, keepdims=True) + EPSILON)
-
-
-def residual_forward(resid, branch, alpha):
-    branch_scale = row_scale(branch)
-    unit = branch * branch_scale
-    mixed = resid + alpha * (unit - resid)
-    mixed_scale = row_scale(mixed)
-    return (mixed * mixed_scale, (unit, branch_scale, mixed_scale))
-
-
-def residual_backward(grad_out, result, resid, alpha, kept):
-    unit, branch_scale, mixed_scale = kept
-    grad_mixed = mixed_scale * (
-        grad_out - result * jnp.sum(grad_out * result, axis=-1, keepdims=True)
-    )
-    grad_alpha = jnp.sum(grad_mixed * (unit - resid), axis=0)
-    grad_resid = grad_mixed * (1.0 - alpha)
-    grad_unit = grad_mixed * alpha
-    grad_branch = branch_scale * (
-        grad_unit - unit * jnp.sum(grad_unit * unit, axis=-1, keepdims=True)
-    )
-    return (grad_resid, grad_branch, grad_alpha)
 
 
 def other_core(value):
@@ -1775,22 +2122,23 @@
         stacked = jnp.stack([w_up, w_gate, w_down.T]).astype(BF16).reshape(3, rows, 2, units)
         keep = lax.dynamic_index_in_dim(stacked, core, 2, keepdims=False)
         give = lax.dynamic_index_in_dim(stacked, 1 - core, 2, keepdims=False)
-        low_wo = wo.astype(BF16).T.reshape(rows // 2, 2 * part)
-        given = jnp.concatenate([give.reshape(3 * rows, units), low_wo])
+        low_wo = wo.astype(BF16).T
+        wide_wo = jnp.concatenate([low_wo, low_wo], axis=1)
+        given = jnp.concatenate([give.reshape(3 * rows, units), wide_wo])
         got = other_core(given)
 
         def in_order(own, other):
             return jnp.where(core == 0, jnp.stack([own, other], 1), jnp.stack([other, own], 1))
 
         pair = in_order(keep, got[: 3 * rows].reshape(3, rows, units))
-        pair_wo = in_order(low_wo[None], got[3 * rows :][None])
-        packed = jnp.concatenate([pair.reshape(6 * rows, units), pair_wo.reshape(rows, units)])
+        lane = jnp.arange(2 * part) // part
+        pair_wo = jnp.where(lane == core, wide_wo, got[3 * rows :])
+        packed = jnp.concatenate([pair.reshape(6 * rows, units), pair_wo])
         vectors = jnp.concatenate([s_u, s_v * math.sqrt(width), alpha_a, alpha_m])
         wide, full_qkv, packed, vectors = gather_all(
             hidden[0].astype(BF16), low_qkv, packed, vectors[None], size, chips, 0
         )
         full_qkv = full_qkv.reshape(size, part, 3 * part)
-        full_wo = packed[:, :, 6 * rows :].reshape(size, width, part)
         vectors = vectors[:, 0]
         s_up = lax.dynamic_slice_in_dim(vectors[:, : 2 * units], core * units, units, 1)
         s_gate = lax.dynamic_slice_in_dim(
@@ -1798,8 +2146,8 @@
         )
         s_up = s_up[:, None, :]
         s_gate = s_gate[:, None, :]
-        alpha_attn = vectors[:, 4 * units : 4 * units + part].reshape(width)
-        alpha_mlp = vectors[:, 4 * units + part :].reshape(width)
+        alpha_attn = vectors[:, 4 * units : 4 * units + part].reshape(1, width)
+        alpha_mlp = vectors[:, 4 * units + part :].reshape(1, width)
 
         docs = doc_ids[0]
         starts = document_starts(docs)
@@ -1807,7 +2155,7 @@
         cosine, sine = rope_tables(slot - starts, DK)
         cosine = jnp.tile(cosine, (1, heads))
         sine = jnp.tile(sine, (1, heads))
-        low = starts[::block] // block
+        low = jnp.concatenate([starts[::block] // block, me[None]])
         key_docs = jnp.where(valid[0] == 1, docs, -1)
         to_pair = placing_matrix(place, heads)
         to_plain = placing_matrix(np.arange(heads * DK), heads)
@@ -1830,48 +2178,55 @@
             key_docs.reshape(slots // block, 1, block),
             collect_plain,
         )
-        merged = spread_tokens(attended, size, 1)
-        resid = lax.dynamic_slice_in_dim(wide, me * mine, mine, 1)
-        resid = resid.transpose(1, 0, 2).reshape(mine, width).astype(F32)
-        merged_parts = merged.reshape(mine, size, part)
-        branch_attn = jnp.einsum("tmh,mdh->td", merged_parts, full_wo, preferred_element_type=F32)
-        middle, kept_attn = residual_forward(resid, branch_attn, alpha_attn)
-
-        middle_low = middle.astype(BF16)
-        x = jnp.concatenate([middle_low, other_core(middle_low)])
-        up, gate, hidden_units, down_term, spread_cot = feed(
-            x, packed, s_up, s_gate, cotangent[0].astype(BF16), 2
-        )
-        branch_mlp = down_term[:mine].astype(F32) + other_core(down_term[mine:]).astype(F32)
-        result, kept_mlp = residual_forward(middle, branch_mlp, alpha_mlp)
-
-        grad_middle, grad_branch_mlp, grad_alpha_mlp = residual_backward(
-            spread_cot.astype(F32), result, middle, alpha_mlp, kept_mlp
-        )
-        grad_branch_mlp = grad_branch_mlp.astype(BF16)
-        dbranch = jnp.concatenate([grad_branch_mlp, other_core(grad_branch_mlp)])
-        dup, dgate, dx, grad_u, grad_v, out_low = feed_back(
-            dbranch, packed, s_up, s_gate, up, gate, result.astype(BF16), 3
+        (
+            x,
+            middle,
+            unit,
+            branch_scale,
+            mixed_scale,
+            merged,
+            full_wo,
+            resid,
+            cotangent_low,
+        ) = mix(attended, packed, rows, wide, alpha_attn, cotangent[0], 1)
+
+        up, gate, hidden_units, result, grad_middle, dbranch, grad_alpha_mlp = feed(
+            x, packed, s_up, s_gate, cotangent_low, middle, alpha_mlp, 2
+        )
+        (
+            dup,
+            dgate,
+            grad_u,
+            grad_v,
+            out_low,
+            grad_resid,
+            dbranch_attn,
+            dmerged,
+            grad_alpha_attn,
+        ) = feed_back(
+            dbranch,
+            packed,
+            s_up,
+            s_gate,
+            up,
+            gate,
+            result,
+            grad_middle,
+            middle,
+            resid,
+            unit,
+            branch_scale,
+            mixed_scale,
+            alpha_attn,
+            full_wo,
+            3,
         )
         out_hidden = out_low.astype(F32)
-        grad_middle = (
-            grad_middle + dx[:mine].astype(F32) + other_core(dx[mine:]).astype(F32)
-        )
-
-        grad_resid, grad_branch_attn, grad_alpha_attn = residual_backward(
-            grad_middle, middle, resid, alpha_attn, kept_attn
-        )
-        grad_branch_attn = grad_branch_attn.astype(BF16)
-        grad_merged = jnp.einsum(
-            "td,mdh->tmh", grad_branch_attn, full_wo, preferred_element_type=F32
-        ).astype(BF16)
-        grads, dattended = feed_grads(
-            x, dbranch, dup, dgate, hidden_units, grad_merged.reshape(mine, width), chips, 4
-        )
-        grad_wo = jnp.einsum(
-            "td,tmh->mdh", grad_branch_attn, merged_parts, preferred_element_type=F32
-        ).astype(BF16)
-        dq, dk, dv, term, grad_gain = attend_back(
+        grads, grad_wo, dattended = feed_grads(
+            x, dbranch, dup, dgate, hidden_units, dbranch_attn, merged, dmerged, chips, 4
+        )
+
+        term, grad_qkv, grad_gain = attend_back(
             low,
             qback,
             dattended,
@@ -1890,18 +2245,8 @@
             collect_plain,
             collect_pair,
             sums,
-        )
-        own = lax.dynamic_slice_in_dim(term, me * mine, mine, 1).astype(F32)
-        own = own + grad_resid.reshape(mine, size, part).transpose(1, 0, 2)
-        term = lax.dynamic_update_slice_in_dim(term, own.astype(BF16), me * mine, 1)
-        grad_qkv = jnp.concatenate(
-            [
-                jnp.einsum("mtd,tf->mdf", wide, d, preferred_element_type=F32)
-                .astype(BF16)
-                .reshape(width, part)
-                for d in (dq, dk, dv)
-            ],
-            axis=1,
+            wide,
+            grad_resid,
         )
         out_pairs = (
             lambda w: w.reshape(w.shape[0], 2, heads, HALF)
@@ -1928,7 +2273,7 @@
         grad_hidden, owned, owned_output, owned_qkv, summed = sum_all(
             term,
             grads,
-            grad_wo.reshape(size, chips, 2, rows, part),
+            grad_wo,
             grad_qkv.reshape(chips, 2, rows, 3 * part),
             placed[:, None],
             chips,

time: 872 us -> 792 us (0.908)
  other arithmetic: 62 us -> 21.4 us
  local copies, waits for them, and re-layouts: 57.8 us -> 30.6 us
  matrix products: 23.2 us -> 0 us
  Pallas kernels: 709 us -> 732 us
    dot_general x6 -> x0, matrix products: 23.2 us -> none  [the longest x3 14.2 us: on_device(): jnp.einsum('mtd,tf->mdf', wide, d, preferred_element_type=F32).astype(BF16)]
    pallas_call x1, Pallas kernels: 179 us -> 201 us  [gather_all(): pl.pallas_call(functools.partial(gather_all_kernel, size, chips, chunks,...]
    pallas_call x1, Pallas kernels: 218 us -> 207 us  [sum_all(): pl.pallas_call(functools.partial(sum_all_kernel, size, chips, chunks, spl...]
    reduce_sum x6 -> x0, other arithmetic: 10.2 us -> none  [the longest x2 4.31 us: residual_backward(): grad_alpha = jnp.sum(grad_mixed * (unit - resid), axis=0)]
    reshape x5 -> x0, local copies, waits for them, and re-layouts: 9.44 us -> none  [the longest x1 2.6 us: on_device(): merged_parts = merged.reshape(mine, size, part)]
    convert_element_type x5 -> x0, other arithmetic: 9.15 us -> none  [the longest x1 3.19 us: on_device(): cotangent[0].astype(BF16)]
  transfers between devices with their start and end apart: 5 -> 1, of which waited for: 1 -> 0; matrix products, arithmetic and copies ran while one was open for 4% -> 2% of each run, Pallas kernels for 0% -> 0%
where the time goes in v3:
time: 792 us; the launch traced here: 787 us
  Pallas kernels  732 us (92%)
  local copies, waits for them, and re-layouts  30.6 us (4%)
  other arithmetic  21.4 us (3%)
    pallas_call x1, Pallas kernels, sum_all(): pl.pallas_call(functools.partial(sum_all_kernel, size, chips, chunks, spl...  207 us
    pallas_call x1, Pallas kernels, gather_all(): pl.pallas_call(functools.partial(gather_all_kernel, size, chips, chunks,...  201 us
    pallas_call x1, Pallas kernels, attend_back(): pl.pallas_call(attend_back_kernel, grid_spec=pltpu.PrefetchScalarGridSpec...  94.3 us
    pallas_call x1, Pallas kernels, mix(): pl.pallas_call(functools.partial(mix_kernel, size), in_specs=[ANY, ANY, A...  50.6 us
    pallas_call x1, Pallas kernels, feed(): pl.pallas_call(functools.partial(feed_kernel, size), grid=(2, parts), in_...  48.6 us
    pallas_call x1, Pallas kernels, feed_back(): pl.pallas_call(functools.partial(feed_back_kernel, size), grid=(2, parts)...  45.9 us
    pallas_call x1, Pallas kernels, feed_grads(): pl.pallas_call(functools.partial(feed_grads_kernel, size), grid=(4, parts...  41.5 us
    pallas_call x1, Pallas kernels, attend(): pl.pallas_call(attend_kernel, grid_spec=pltpu.PrefetchScalarGridSpec(num_...  24 us
  transfers between devices with their start and end apart: 1, of which 0 were waited for; matrix products, arithmetic and copies ran while one was open for 2% of the time, Pallas kernels for 0%

profile of v3, /device:TPU:17, one launch (start us, length us, event | category | flops | bytes accessed | tf_op | source)
XLA Modules:
  0.0 786.8 jit_solution(16721350518219032506)
XLA Ops:
  0.7 1.2 convert.32
  3.1 0.9 copy.55
  4.7 1.3 pad_maximum_fusion.1
  6.0 1.7 maximum_maximum_fusion
  9.5 1.3 convert_bitcast_fusion.hidden
  10.8 1.0 copy.47
  11.9 1.0 copy.49
  13.1 0.9 convert.31
  17.2 2.1 multiply_sine_fusion
  19.4 1.6 copy.59.cosine
  21.2 1.7 copy.60.sine
  26.9 1.3 broadcast_select_fusion.kdoc
  28.2 1.1 slice.81
  29.5 0.9 slice_select_fusion
  30.4 1.0 pad_maximum_fusion.packed
  31.4 200.6 %gather_all.1 = (bf16[4,3072,256]{2,1,0:T(8,128)(2,1)}, bf16[8,128,768]{2,1,0:T(8,128)(2,1)}, bf16[4,4,896,512]{3,2,1,0:T(8,128)(2,1)}, f32[4,1,2560]{2,1,0:T(1,128)}) custom-call(bf16[3072,256]{1,0:T(8,128)(2,1)} %convert_bitcast_fusion.hidden, bf16[128,768]{1,0:T(8,128)(2,1)} %pad_maximum_fusion.2.qkv, bf16[896,512]{1,0:T(8,128)(2,1)} %pad_maximum_fusion.packed, ...), custom_call_target="tpu_custom_call" | custom-call | tf_op jit(solution)/shard_map/gather_all/pallas_call | solution.py:409
  235.2 19.8 %project.1 = (bf16[4,3072,128]{2,1,0:T(8,128)(2,1)}, bf16[4,3072,128]{2,1,0:T(8,128)(2,1)}, bf16[4,3072,128]{2,1,0:T(8,128)(2,1)}, f32[3072,128]{1,0:T(8,128)}, f32[3072,128]{1,0:T(8,128)}) custom-call(bf16[4,3072,256]{2,1,0:T(8,128)(2,1)} %get-tuple-element.61.wide, bf16[4,256,768]{2,1,0:T(8,128)(2,1)} %bitcast.132, f32[3072,128]{1,0:T(8,128)} %copy.59.cosine, ...), custom_call_target="tpu_custom_call" | custom-call | flops 4831838208 | bytes 20971520 | tf_op jit(solution)/shard_map/project/pallas_call | solution.py:957
  255.1 24.0 %attend.1 = (bf16[3072,256]{1,0:T(8,128)(2,1)}, bf16[4,3072,128]{2,1,0:T(8,128)(2,1)}) custom-call(s32[7]{0:T(128)} %pad_add_fusion.low, bf16[4,3072,128]{2,1,0:T(8,128)(2,1)} %get-tuple-element.63.q, bf16[4,3072,128]{2,1,0:T(8,128)(2,1)} %get-tuple-element.64.k, bf16[4,3072,128]{2,1,0:T(8,128)(2,1)} %get-tuple-element.65.v, s32[3072,1]{1,0:T(8,128)} %copy-done, ...), custom_call_target="tpu_custom_call" | custom-call | flops 40000000000 | bytes 16777216 | tf_op jit(solution)/shard_map/attend/pallas_call | solution.py:1043
  279.0 50.6 %mix.1 = (bf16[1536,1024]{1,0:T(8,128)(2,1)}, f32[768,1024]{1,0:T(8,128)}, bf16[768,1024]{1,0:T(8,128)(2,1)}, f32[768,1]{1,0:T(8,128)}, f32[768,1]{1,0:T(8,128)}...) custom-call(bf16[3072,256]{1,0:T(8,128)(2,1)} %get-tuple-element.66., ...), custom_call_target="tpu_custom_call" | custom-call | tf_op jit(solution)/shard_map/mix/pallas_call | solution.py:1507
  329.7 48.6 %feed.1 = (bf16[4,1536,512]{2,1,0:T(8,128)(2,1)}, bf16[4,1536,512]{2,1,0:T(8,128)(2,1)}, bf16[4,1536,512]{2,1,0:T(8,128)(2,1)}, bf16[768,1024]{1,0:T(8,128)(2,1)...) custom-call(bf16[1536,1024]{1,0:T(8,128)(2,1)} %get-tuple-element.69.x, ...), custom_call_target="tpu_custom_call" | custom-call | flops 19327352832 | bytes 62914560 | tf_op jit(solution)/shard_map/feed/pallas_call | solution.py:1695
  378.2 45.9 %feed_back.1 = (bf16[4,1536,512]{2,1,0:T(8,128)(2,1)}, bf16[4,1536,512]{2,1,0:T(8,128)(2,1)}, f32[4,1,512]{2,1,0:T(1,128)}, f32[4,1,512]{2,1,0:T(1,128)}, bf16[3...) custom-call(bf16[1536,1024]{1,0:T(8,128)(2,1)} %get-tuple-element.72, ...), custom_call_target="tpu_custom_call" | custom-call | flops 19327352832 | bytes 73400320 | tf_op jit(solution)/shard_map/feed_back/pallas_call | solution.py:1885
  425.7 41.5 %feed_grads.1 = (bf16[4,4,768,512]{3,2,1,0:T(8,128)(2,1)}, bf16[4,4,2,128,256]{4,3,2,1,0:T(8,128)(2,1)}, bf16[3072,256]{1,0:T(8,128)(2,1)}) custom-call(bf16[1536,1024]{1,0:T(8,128)(2,1)} %get-tuple-element.69.x, bf16[1536,1024]{1,0:T(8,128)(2,1)} %get-tuple-element.72.dbranch, bf16[4,1536,512]{2,1,0:T(8,128)(2,1)} %get-tuple-element.84.dup, ...), custom_call_target="tpu_custom_call" | custom-call | flops 19327352832 | bytes 41943040 | tf_op jit(solution)/shard_map/feed_grads/pallas_call | solution.py:2025
  467.2 94.3 %attend_back.1 = (bf16[4,3072,256]{2,1,0:T(8,128)(2,1)}, bf16[4,256,768]{2,1,0:T(8,128)(2,1)}, f32[1,256]{1,0:T(1,128)}) custom-call(s32[7]{0:T(128)} %pad_add_fusion.low, bf16[4,3072,128]{2,1,0:T(8,128)(2,1)} %get-tuple-element.83.qback, bf16[3072,256]{1,0:T(8,128)(2,1)} %get-tuple-element.90.dout, bf16[3072,256]{1,0:T(8,128)(2,1)} %get-tuple-element.66.attended, ...), custom_call_target="tpu_custom_call" | custom-call | flops 80000000000 | bytes 31457280 | tf_op jit(solution)/shard_map/attend_back/pallas_call | solution.py:1286
  562.1 1.3 reduce.11
  565.7 206.9 %sum_all.1 = (f32[3072,256]{1,0:T(8,128)}, f32[3,128,1024]{2,1,0:T(8,128)}, f32[128,256]{1,0:T(8,128)}, f32[128,768]{1,0:T(8,128)}, f32[1,2816]{1,0:T(1,128)}) custom-call(bf16[4,3072,256]{2,1,0:T(8,128)(2,1)} %get-tuple-element.94.term, bf16[4,4,768,512]{3,2,1,0:T(8,128)(2,1)} %get-tuple-element.95.grads, ...), custom_call_target="tpu_custom_call" | custom-call | tf_op jit(solution)/shard_map/sum_all/pallas_call | solution.py:840
  772.6 1.3 fusion.9
  773.9 1.3 fusion.8
  775.1 2.5 slice_bitcast_fusion
  777.7 1.0 copy.74
  781.9 1.9 bitcast_convert_fusion
  783.8 1.1 copy-done.2
  784.9 1.7 copy.92
  (113 shorter events, 21.6 us)
Async XLA Ops:
  0.6 1.4 copy-start.5
  0.7 2.4 copy-start.6
  2.0 1.9 copy-start.9
  4.7 4.8 copy-start.1
  7.8 20.5 %collective-permute-start = (bf16[512,512]{1,0:T(8,128)(2,1)}, bf16[512,512]{1,0:T(8,128)(2,1)}, u32[]{:S(2)}, u32[]{:S(2)}) collective-permute-start(bf16[512,512]{1,0:T(8,128)(2,1)} %maximum_maximum_fusion), channel_id=1, source_target_pairs={{0,4},{4,0},{1,5},{5,1},{2,6},{6,2},{3,7},{7,3},{8,12},{12,8},{9,1... | collective-permute-start | bytes 1572872 | tf_op jit(solution)/shard_map/ppermute | solution.py:2083
  9.5 4.5 copy-start.12
  9.5 5.9 copy-start.8
  21.2 1.7 copy-start.15
  21.2 2.5 copy-start.11
  24.3 3.9 copy-start
  28.2 1.3 copy-start.4
  28.2 1.3 copy-start.16
  467.2 96.4 %copy-start.14 = (f32[1,1024]{1,0:T(1,128)S(1)}, f32[1,1024]{1,0:T(1,128)}, u32[]{:S(2)}) copy-start(f32[1,1024]{1,0:T(1,128)} %get-tuple-element.101) | copy-start | bytes 12292
  467.2 97.1 %copy-start.13 = (f32[1,1024]{1,0:T(1,128)S(1)}, f32[1,1024]{1,0:T(1,128)}, u32[]{:S(2)}) copy-start(f32[1,1024]{1,0:T(1,128)} %get-tuple-element.102) | copy-start | bytes 12292
  775.1 3.5 copy-start.7
  777.7 3.4 copy-start.10
  777.7 4.2 copy-start.3
  781.9 3.0 copy-start.2

commit v4 on v3

--- a/solution.py
+++ b/solution.py
@@ -408,7 +408,7 @@
     plane = dma((2 * size - 1, 2, max(chips - 1, 1)))
     return pl.pallas_call(
         functools.partial(gather_all_kernel, size, chips, chunks, height // 32 * 16),
-        in_specs=[ANY] * 4,
+        in_specs=[pl.BlockSpec(memory_space=pltpu.VMEM)] * 4,
         out_specs=[ANY] * 4,
         out_shape=[
             jax.ShapeDtypeStruct((size, *hidden.shape), BF16),
@@ -893,13 +893,27 @@
     return matrix
 
 
+def delta_matrix(heads):
+    lane = np.arange(heads * EXT)
+    head = np.arange(heads * DK) // DK
+    return ((head[:, None] == lane[None, :] // EXT) & (lane % EXT >= DK) & (lane % EXT < DK + 3)).astype(
+        np.float32
+    )
+
+
 def head_sum_matrix(heads):
     lane = np.arange(heads * HALF) // HALF
     return (lane[:, None] == lane[None, :]).astype(np.float32)
 
 
+def split_dot(value, matrix):
+    high = value.astype(BF16)
+    rest = (value - high.astype(F32)).astype(BF16)
+    return dot(high, matrix) + dot(rest, matrix)
+
+
 def project_kernel(
-    wide, weight, cosine, sine, gain, place_pair, place_plain, sums, q, k, v, rq, rk
+    wide, weight, cosine, sine, gain, place_pair, place_plain, sums, q, k, v, q_pair, k_pair, rq, rk
 ):
     parts = wide.shape[0]
     heads = q.shape[0]
@@ -914,21 +928,23 @@
     sin = sine[...]
     gain_first = gain[:, :pair]
     gain_second = gain[:, pair:]
-    for offset, out, scale_out, factor in ((0, q, rq, math.sqrt(DK)), (width, k, rk, 1.0)):
+    for offset, out, pair_out, scale_out, factor in (
+        (0, q, q_pair, rq, math.sqrt(DK)),
+        (width, k, k_pair, rk, 1.0),
+    ):
         first = raw[:, offset : offset + pair]
         second = raw[:, offset + pair : offset + width]
         turned_first = first * cos - second * sin
         turned_second = second * cos + first * sin
-        total = dot(
-            turned_first * turned_first + turned_second * turned_second,
-            sums[...],
-            precision=lax.Precision.HIGHEST,
+        total = split_dot(
+            turned_first * turned_first + turned_second * turned_second, sums[...]
         )
         scale = lax.rsqrt(total + EPSILON)
         scale_out[...] = scale
         both = jnp.concatenate(
             [turned_first * scale * gain_first, turned_second * scale * gain_second], axis=1
         ).astype(BF16)
+        pair_out[...] = both
         padded = dot(both, place_pair[...]) * factor
         for head in range(heads):
             piece = padded[:, head * EXT : (head + 1) * EXT]
@@ -954,6 +970,8 @@
 
     rows = pl.BlockSpec((block, heads * HALF), lambda i: (i, 0))
     headed = pl.BlockSpec((heads, block, EXT), lambda i: (0, i, 0))
+    paired = pl.BlockSpec((block, width), lambda i: (i, 0))
+    both = jax.ShapeDtypeStruct((tokens, width), BF16)
     return pl.pallas_call(
         project_kernel,
         grid=(tokens // block,),
@@ -967,8 +985,8 @@
             whole(place_plain),
             whole(sums),
         ],
-        out_specs=[headed, headed, headed, rows, rows],
-        out_shape=[padded, padded, padded, scale, scale],
+        out_specs=[headed, headed, headed, paired, paired, rows, rows],
+        out_shape=[padded, padded, padded, both, both, scale, scale],
         compiler_params=grid_params(1),
         cost_estimate=pl.CostEstimate(
             flops=2 * tokens * parts * part * width * 3,
@@ -1068,35 +1086,33 @@
     )(low, q, k, v, qdoc, kdoc, collect)
 
 
-def gather_heads(padded, matrix, heads):
-    total = None
-    for head in range(heads):
-        value = padded[head]
-        high = value.astype(BF16)
-        rest = (value - high.astype(F32)).astype(BF16)
-        term = dot(high, matrix[head]) + dot(rest, matrix[head])
-        total = term if total is None else total + term
-    return total
-
-
 def unrope(grad, unit, gain, scale, cos, sin, sums):
     pair = cos.shape[1]
     grad_gain = jnp.sum(grad * unit, axis=0, keepdims=True)
     dy = grad * gain
     prod = dy * unit
-    total = dot(prod[:, :pair] + prod[:, pair:], sums, precision=lax.Precision.HIGHEST)
+    total = split_dot(prod[:, :pair] + prod[:, pair:], sums)
     first = scale * (dy[:, :pair] - unit[:, :pair] * total)
     second = scale * (dy[:, pair:] - unit[:, pair:] * total)
     raw = jnp.concatenate([first * cos + second * sin, second * cos - first * sin], axis=1)
     return raw.astype(BF16), grad_gain
 
 
+def head_lanes(shape, head, paired):
+    lane = lax.broadcasted_iota(jnp.int32, shape, 1)
+    if paired:
+        return lax.div(lax.rem(lane, shape[1] // 2), HALF) == head
+    return lax.div(lane, DK) == head
+
+
 def attend_back_kernel(
     low,
     qback,
+    q_pair,
     dout,
     attended,
     k,
+    k_pair,
     v,
     qdoc,
     kdoc,
@@ -1107,8 +1123,7 @@
     gain,
     weight,
     place_plain,
-    collect_plain,
-    collect_pair,
+    place_delta,
     sums,
     wide,
     grad_resid,
@@ -1119,6 +1134,11 @@
     dv,
     dq,
     dox,
+    q_heads,
+    d_heads,
+    k_heads,
+    probs_all,
+    scores_all,
     dq_low,
     total_qkv,
 ):
@@ -1133,27 +1153,29 @@
         dk[...] = jnp.zeros_like(dk)
         dv[...] = jnp.zeros_like(dv)
         gain_out[...] = jnp.zeros_like(gain_out)
+        keys = k_pair[...]
+        for head in range(heads):
+            k_heads[head] = jnp.where(head_lanes(keys.shape, head, True), keys, 0)
 
     @pl.when(step_at < steps)
     def _():
         index = step_at
         lane = lax.broadcasted_iota(jnp.int32, (rows, EXT), 1)
-        spread_grad = dot(dout[...], place_plain[...])
-        spread_out = dot(attended[...], place_plain[...])
+        grads = dout[...]
+        queries = q_pair[...]
+        spread = dot(grads, place_plain[...])
+        delta = split_dot(grads.astype(F32) * attended[...].astype(F32), place_delta[...])
         for head in range(heads):
-            piece = spread_grad[:, head * EXT : (head + 1) * EXT]
-            other = spread_out[:, head * EXT : (head + 1) * EXT]
-            delta = jnp.sum(piece * other, axis=1, keepdims=True)
-            high, middle, rest = split_three(-delta)
+            at = slice(head * EXT, (head + 1) * EXT)
+            high, middle, rest = split_three(-delta[:, at])
             dox[head] = jnp.where(
                 lane < DK,
-                piece,
-                jnp.where(
-                    lane == DK,
-                    high,
-                    jnp.where(lane == DK + 1, middle, jnp.where(lane == DK + 2, rest, 0.0)),
-                ),
+                spread[:, at],
+                jnp.where(lane == DK, high, jnp.where(lane == DK + 1, middle, rest)),
             ).astype(BF16)
+            stack = slice(head * rows, (head + 1) * rows)
+            q_heads[stack, :] = jnp.where(head_lanes(queries.shape, head, True), queries, 0)
+            d_heads[stack, :] = jnp.where(head_lanes(grads.shape, head, False), grads, 0)
         dq[...] = jnp.zeros_like(dq)
 
         def step(j, diagonal):
@@ -1163,15 +1185,19 @@
                 key = lax.broadcasted_iota(jnp.int32, (rows, rows), 0)
                 query = lax.broadcasted_iota(jnp.int32, (rows, rows), 1)
                 mask = (mask & (key < query)) | (key == query)
+            total = dq[...]
             for head in range(heads):
-                keys = k[head, slots, :]
-                scores = dot(keys, qback[head], NT)
+                scores = dot(k[head, slots, :], qback[head], NT)
                 probs = jnp.where(mask, jnp.exp(scores), 0.0)
-                dv[head, slots, :] += dot(probs.astype(BF16), dox[head])
                 dprobs = dot(v[head, slots, :], dox[head], NT)
                 dscores = (probs * dprobs).astype(BF16)
-                dk[head, slots, :] += dot(dscores, qback[head])
-                dq[head] += dot(dscores, keys, TN)
+                stack = slice(head * rows, (head + 1) * rows)
+                probs_all[:, stack] = probs.astype(BF16)
+                scores_all[:, stack] = dscores
+                total += dot(dscores, k_heads[head, slots, :], TN)
+            dq[...] = total
+            dv[slots, :] += dot(probs_all[...], d_heads[...])
+            dk[slots, :] += dot(scores_all[...], q_heads[...])
 
         def earlier(j, carry):
             step(j, False)
@@ -1180,13 +1206,14 @@
         lax.fori_loop(low[index], index, earlier, 0)
         step(index, True)
 
-        grad = gather_heads(dq, collect_pair, heads) * scale
-        query = dot(qback[0], collect_pair[0])
-        for head in range(1, heads):
-            query += dot(qback[head], collect_pair[head])
-        unit = query * (1.0 / scale) / gain[...]
         raw, grad_gain = unrope(
-            grad, unit, gain[...], rq[...], cosine[...], sine[...], sums[...]
+            dq[...] * scale,
+            queries.astype(F32) / gain[...],
+            gain[...],
+            rq[...],
+            cosine[...],
+            sine[...],
+            sums[...],
         )
         gain_out[...] += grad_gain
         dq_low[pl.ds(pl.multiple_of(index * rows, rows), rows), :] = raw
@@ -1195,18 +1222,17 @@
     def _():
         index = step_at - steps
         slots = pl.ds(pl.multiple_of(index * rows, rows), rows)
-        grad = gather_heads([dk[head, slots, :] for head in range(heads)], collect_pair, heads)
-        keys = dot(k[0, slots, :], collect_pair[0])
-        for head in range(1, heads):
-            keys += dot(k[head, slots, :], collect_pair[head])
         raw, grad_gain = unrope(
-            grad, keys / gain[...], gain[...], rk[...], cosine[...], sine[...], sums[...]
+            dk[slots, :] * scale,
+            k_pair[slots, :].astype(F32) / gain[...],
+            gain[...],
+            rk[...],
+            cosine[...],
+            sine[...],
+            sums[...],
         )
         gain_out[...] += grad_gain
-        dvalues = gather_heads(
-            [dv[head, slots, :] for head in range(heads)], collect_plain, heads
-        ).astype(BF16)
-        together = jnp.concatenate([dq_low[slots, :], raw, dvalues], axis=1)
+        together = jnp.concatenate([dq_low[slots, :], raw, dv[slots, :].astype(BF16)], axis=1)
         parts, part = weight.shape[:2]
         for member in range(parts):
             term_out[member] = dot(together, weight[member], NT).astype(BF16)
@@ -1243,9 +1269,11 @@
 def attend_back(
     low,
     qback,
+    q_pair,
     dout,
     attended,
     k,
+    k_pair,
     v,
     qdoc,
     kdoc,
@@ -1256,8 +1284,7 @@
     gain,
     weight,
     place_plain,
-    collect_plain,
-    collect_pair,
+    place_delta,
     sums,
     wide,
     grad_resid,
@@ -1292,7 +1319,9 @@
                 pl.BlockSpec((heads, block, EXT), lambda i, low: (0, now(i), 0)),
                 rows(width, now),
                 rows(width, now),
+                rows(width, now),
                 whole(k),
+                whole(k_pair),
                 whole(v),
                 pl.BlockSpec((1, 1, block), lambda i, low: (now(i), 0, 0)),
                 whole(kdoc),
@@ -1303,8 +1332,7 @@
                 whole(gain),
                 whole(weight),
                 whole(place_plain),
-                whole(collect_plain),
-                whole(collect_pair),
+                whole(place_delta),
                 whole(sums),
                 pl.BlockSpec((parts, block, part), lambda i, low: (0, after(i), 0)),
                 whole(grad_resid),
@@ -1315,10 +1343,15 @@
                 pl.BlockSpec((1, width), lambda i, low: (0, 0)),
             ],
             scratch_shapes=[
-                pltpu.VMEM((heads, tokens, EXT), F32),
-                pltpu.VMEM((heads, tokens, EXT), F32),
-                pltpu.VMEM((heads, block, EXT), F32),
+                pltpu.VMEM((tokens, width), F32),
+                pltpu.VMEM((tokens, width), F32),
+                pltpu.VMEM((block, width), F32),
                 pltpu.VMEM((heads, block, EXT), BF16),
+                pltpu.VMEM((heads * block, width), BF16),
+                pltpu.VMEM((heads * block, width), BF16),
+                pltpu.VMEM((heads, tokens, width), BF16),
+                pltpu.VMEM((block, heads * block), BF16),
+                pltpu.VMEM((block, heads * block), BF16),
                 pltpu.VMEM((tokens, width), BF16),
                 pltpu.VMEM((parts, part, 3 * width), F32),
             ],
@@ -1336,9 +1369,11 @@
     )(
         low,
         qback,
+        q_pair,
         dout,
         attended,
         k,
+        k_pair,
         v,
         qdoc,
         kdoc,
@@ -1349,8 +1384,7 @@
         gain,
         weight,
         place_plain,
-        collect_plain,
-        collect_pair,
+        place_delta,
         sums,
         wide,
         grad_resid,
@@ -2161,12 +2195,12 @@
         to_plain = placing_matrix(np.arange(heads * DK), heads)
         place_pair = jnp.asarray(to_pair, BF16)
         place_plain = jnp.asarray(to_plain, BF16)
-        collect_pair = jnp.asarray(to_pair.T.reshape(heads, EXT, heads * DK), BF16)
+        place_delta = jnp.asarray(delta_matrix(heads), BF16)
         collect_plain = jnp.asarray(to_plain.T.reshape(heads, EXT, heads * DK), BF16)
-        sums = jnp.asarray(head_sum_matrix(heads))
+        sums = jnp.asarray(head_sum_matrix(heads), BF16)
         gain = in_pairs(s_qk[None, :])
 
-        q, k, v, rq, rk = project(
+        q, k, v, q_pair, k_pair, rq, rk = project(
             wide, full_qkv, cosine, sine, gain, place_pair, place_plain, sums
         )
         attended, qback = attend(
@@ -2229,9 +2263,11 @@
         term, grad_qkv, grad_gain = attend_back(
             low,
             qback,
+            q_pair,
             dattended,
             attended,
             k,
+            k_pair,
             v,
             docs.reshape(slots // block, 1, block),
             key_docs[:, None],
@@ -2242,8 +2278,7 @@
             gain,
             full_qkv,
             place_plain,
-            collect_plain,
-            collect_pair,
+            place_delta,
             sums,
             wide,
             grad_resid,

time: 792 us -> 744 us (0.939)
  Pallas kernels: 732 us -> 688 us
    pallas_call x1, Pallas kernels: 201 us -> 169 us  [gather_all(): pl.pallas_call(functools.partial(gather_all_kernel, size, chips, chunks,...]
    pallas_call x1, Pallas kernels: 94.3 us -> 86 us  [attend_back(): pl.pallas_call(attend_back_kernel, grid_spec=pltpu.PrefetchScalarGridSpec...]
  transfers between devices with their start and end apart: 1 -> 1, of which waited for: 0 -> 0; matrix products, arithmetic and copies ran while one was open for 2% -> 3% of each run, Pallas kernels for 0% -> 0%
where the time goes in v4:
time: 744 us; the launch traced here: 743 us
  Pallas kernels  688 us (92%)
  local copies, waits for them, and re-layouts  31.2 us (4%)
  other arithmetic  21.3 us (3%)
    pallas_call x1, Pallas kernels, sum_all(): pl.pallas_call(functools.partial(sum_all_kernel, size, chips, chunks, spl...  203 us
    pallas_call x1, Pallas kernels, gather_all(): pl.pallas_call(functools.partial(gather_all_kernel, size, chips, chunks,...  169 us
    pallas_call x1, Pallas kernels, attend_back(): pl.pallas_call(attend_back_kernel, grid_spec=pltpu.PrefetchScalarGridSpec...  86 us
    pallas_call x1, Pallas kernels, mix(): pl.pallas_call(functools.partial(mix_kernel, size), in_specs=[ANY, ANY, A...  50.6 us
    pallas_call x1, Pallas kernels, feed(): pl.pallas_call(functools.partial(feed_kernel, size), grid=(2, parts), in_...  48.4 us
    pallas_call x1, Pallas kernels, feed_back(): pl.pallas_call(functools.partial(feed_back_kernel, size), grid=(2, parts)...  45.9 us
    pallas_call x1, Pallas kernels, feed_grads(): pl.pallas_call(functools.partial(feed_grads_kernel, size), grid=(4, parts...  41.4 us
    pallas_call x1, Pallas kernels, attend(): pl.pallas_call(attend_kernel, grid_spec=pltpu.PrefetchScalarGridSpec(num_...  27.8 us
  transfers between devices with their start and end apart: 1, of which 0 were waited for; matrix products, arithmetic and copies ran while one was open for 3% of the time, Pallas kernels for 0%

profile of v4, /device:TPU:17, one launch (start us, length us, event | category | flops | bytes accessed | tf_op | source)
XLA Modules:
  0.0 743.4 jit_solution(16997695940203503169)
XLA Ops:
  0.7 1.1 convert.32
  3.0 0.9 copy.55
  4.6 1.3 pad_maximum_fusion.1
  6.0 1.7 maximum_maximum_fusion
  9.5 1.3 convert_bitcast_fusion.hidden
  10.7 1.0 copy.47
  11.9 1.0 copy.49
  13.0 0.9 convert.31
  17.2 2.1 multiply_sine_fusion
  19.4 1.6 copy.59.cosine
  21.2 1.7 copy.60.sine
  26.9 1.3 broadcast_select_fusion.kdoc
  28.2 1.0 slice.81
  30.0 0.9 slice_select_fusion
  31.0 1.0 pad_maximum_fusion.packed
  32.0 168.5 %gather_all.1 = (bf16[4,3072,256]{2,1,0:T(8,128)(2,1)}, bf16[8,128,768]{2,1,0:T(8,128)(2,1)}, bf16[4,4,896,512]{3,2,1,0:T(8,128)(2,1)}, f32[4,1,2560]{2,1,0:T(1,128)}) custom-call(bf16[3072,256]{1,0:T(8,128)(2,1)} %convert_bitcast_fusion.hidden, bf16[128,768]{1,0:T(8,128)(2,1)} %pad_maximum_fusion.2.qkv, bf16[896,512]{1,0:T(8,128)(2,1)} %pad_maximum_fusion.packed, ...), custom_call_target="tpu_custom_call" | custom-call | tf_op jit(solution)/shard_map/gather_all/pallas_call | solution.py:409
  203.7 16.8 %project.1 = (bf16[4,3072,128]{2,1,0:T(8,128)(2,1)}, bf16[4,3072,128]{2,1,0:T(8,128)(2,1)}, bf16[4,3072,128]{2,1,0:T(8,128)(2,1)}, bf16[3072,256]{1,0:T(8,128)(2...) custom-call(bf16[4,3072,256]{2,1,0:T(8,128)(2,1)} %get-tuple-element.63.wide, ...), custom_call_target="tpu_custom_call" | custom-call | flops 4831838208 | bytes 20971520 | tf_op jit(solution)/shard_map/project/pallas_call | solution.py:975
  220.5 27.8 %attend.1 = (bf16[3072,256]{1,0:T(8,128)(2,1)}, bf16[4,3072,128]{2,1,0:T(8,128)(2,1)}) custom-call(s32[7]{0:T(128)} %pad_add_fusion.low, bf16[4,3072,128]{2,1,0:T(8,128)(2,1)} %get-tuple-element.65.q, bf16[4,3072,128]{2,1,0:T(8,128)(2,1)} %get-tuple-element.66.k, bf16[4,3072,128]{2,1,0:T(8,128)(2,1)} %get-tuple-element.67.v, s32[3072,1]{1,0:T(8,128)} %copy-done, ...), custom_call_target="tpu_custom_call" | custom-call | flops 40000000000 | bytes 16777216 | tf_op jit(solution)/shard_map/attend/pallas_call | solution.py:1061
  248.4 50.6 %mix.1 = (bf16[1536,1024]{1,0:T(8,128)(2,1)}, f32[768,1024]{1,0:T(8,128)}, bf16[768,1024]{1,0:T(8,128)(2,1)}, f32[768,1]{1,0:T(8,128)}, f32[768,1]{1,0:T(8,128)}...) custom-call(bf16[3072,256]{1,0:T(8,128)(2,1)} %get-tuple-element.68., ...), custom_call_target="tpu_custom_call" | custom-call | tf_op jit(solution)/shard_map/mix/pallas_call | solution.py:1541
  299.0 48.4 %feed.1 = (bf16[4,1536,512]{2,1,0:T(8,128)(2,1)}, bf16[4,1536,512]{2,1,0:T(8,128)(2,1)}, bf16[4,1536,512]{2,1,0:T(8,128)(2,1)}, bf16[768,1024]{1,0:T(8,128)(2,1)...) custom-call(bf16[1536,1024]{1,0:T(8,128)(2,1)} %get-tuple-element.71.x, ...), custom_call_target="tpu_custom_call" | custom-call | flops 19327352832 | bytes 62914560 | tf_op jit(solution)/shard_map/feed/pallas_call | solution.py:1729
  347.4 45.9 %feed_back.1 = (bf16[4,1536,512]{2,1,0:T(8,128)(2,1)}, bf16[4,1536,512]{2,1,0:T(8,128)(2,1)}, f32[4,1,512]{2,1,0:T(1,128)}, f32[4,1,512]{2,1,0:T(1,128)}, bf16[3...) custom-call(bf16[1536,1024]{1,0:T(8,128)(2,1)} %get-tuple-element.74, ...), custom_call_target="tpu_custom_call" | custom-call | flops 19327352832 | bytes 73400320 | tf_op jit(solution)/shard_map/feed_back/pallas_call | solution.py:1919
  394.9 41.4 %feed_grads.1 = (bf16[4,4,768,512]{3,2,1,0:T(8,128)(2,1)}, bf16[4,4,2,128,256]{4,3,2,1,0:T(8,128)(2,1)}, bf16[3072,256]{1,0:T(8,128)(2,1)}) custom-call(bf16[1536,1024]{1,0:T(8,128)(2,1)} %get-tuple-element.71.x, bf16[1536,1024]{1,0:T(8,128)(2,1)} %get-tuple-element.74.dbranch, bf16[4,1536,512]{2,1,0:T(8,128)(2,1)} %get-tuple-element.87.dup, ...), custom_call_target="tpu_custom_call" | custom-call | flops 19327352832 | bytes 41943040 | tf_op jit(solution)/shard_map/feed_grads/pallas_call | solution.py:2059
  436.4 86.0 %attend_back.1 = (bf16[4,3072,256]{2,1,0:T(8,128)(2,1)}, bf16[4,256,768]{2,1,0:T(8,128)(2,1)}, f32[1,256]{1,0:T(1,128)}) custom-call(s32[7]{0:T(128)} %pad_add_fusion.low, bf16[4,3072,128]{2,1,0:T(8,128)(2,1)} %get-tuple-element.85.qback, bf16[3072,256]{1,0:T(8,128)(2,1)} %get-tuple-element.86.q_pair, bf16[3072,256]{1,0:T(8,128)(2,1)} %get-tuple-element.93.dout, ...), custom_call_target="tpu_custom_call" | custom-call | flops 80000000000 | bytes 31457280 | tf_op jit(solution)/shard_map/attend_back/pallas_call | solution.py:1313
  522.9 1.3 reduce.11
  526.6 202.7 %sum_all.1 = (f32[3072,256]{1,0:T(8,128)}, f32[3,128,1024]{2,1,0:T(8,128)}, f32[128,256]{1,0:T(8,128)}, f32[128,768]{1,0:T(8,128)}, f32[1,2816]{1,0:T(1,128)}) custom-call(bf16[4,3072,256]{2,1,0:T(8,128)(2,1)} %get-tuple-element.98.term, bf16[4,4,768,512]{3,2,1,0:T(8,128)(2,1)} %get-tuple-element.99.grads, ...), custom_call_target="tpu_custom_call" | custom-call | tf_op jit(solution)/shard_map/sum_all/pallas_call | solution.py:840
  729.2 1.3 fusion.9
  730.5 1.3 fusion.8
  731.8 2.5 slice_bitcast_fusion
  734.3 1.0 copy.74
  738.5 1.9 bitcast_convert_fusion
  740.4 1.1 copy-done.2
  741.5 1.7 copy.92
  (113 shorter events, 22.2 us)
Async XLA Ops:
  0.6 1.4 copy-start.5
  1.8 1.2 copy-start.6
  2.0 1.9 copy-start.9
  4.6 4.8 copy-start.1
  7.7 20.4 %collective-permute-start = (bf16[512,512]{1,0:T(8,128)(2,1)}, bf16[512,512]{1,0:T(8,128)(2,1)}, u32[]{:S(2)}, u32[]{:S(2)}) collective-permute-start(bf16[512,512]{1,0:T(8,128)(2,1)} %maximum_maximum_fusion), channel_id=1, source_target_pairs={{0,4},{4,0},{1,5},{5,1},{2,6},{6,2},{3,7},{7,3},{8,12},{12,8},{9,1... | collective-permute-start | bytes 1572872 | tf_op jit(solution)/shard_map/ppermute | solution.py:2117
  9.4 4.5 copy-start.12
  9.4 5.9 copy-start.8
  21.2 1.7 copy-start.15
  21.2 2.5 copy-start.11
  24.3 3.9 copy-start
  29.2 0.8 copy-start.4
  29.2 0.8 copy-start.16
  436.4 88.0 %copy-start.14 = (f32[1,1024]{1,0:T(1,128)S(1)}, f32[1,1024]{1,0:T(1,128)}, u32[]{:S(2)}) copy-start(f32[1,1024]{1,0:T(1,128)} %get-tuple-element.105) | copy-start | bytes 12292
  436.4 88.7 %copy-start.13 = (f32[1,1024]{1,0:T(1,128)S(1)}, f32[1,1024]{1,0:T(1,128)}, u32[]{:S(2)}) copy-start(f32[1,1024]{1,0:T(1,128)} %get-tuple-element.106) | copy-start | bytes 12292
  731.8 3.5 copy-start.7
  734.3 3.4 copy-start.10
  735.3 3.2 copy-start.3
  738.5 3.0 copy-start.2

commit v5 on v4

--- a/solution.py
+++ b/solution.py
@@ -182,20 +182,58 @@
                 copy.wait_send()
 
 
-def gather_all_kernel(
+def front_kernel(
     size,
     chips,
     chunks,
     split,
     hidden,
-    qkv,
-    packed,
+    wq,
+    wk,
+    wv,
+    wo,
+    w_up,
+    w_gate,
+    w_down,
     vectors,
+    positions,
+    frequency,
+    gain,
+    in_pairs,
+    place_pair,
+    place_plain,
+    sums,
+    wide_out,
+    qkv_out,
+    full,
+    full_vectors,
+    q_out,
+    k_out,
+    v_out,
+    q_pair_out,
+    k_pair_out,
+    rq_out,
+    rk_out,
+    cosine_out,
+    sine_out,
     wide,
     full_qkv,
-    full,
-    full_vectors,
+    packed,
+    matrices,
+    wo_turned,
+    q,
+    k,
+    v,
+    q_pair,
+    k_pair,
+    rq,
+    rk,
+    cosine,
+    sine,
     local,
+    out_sems,
+    core_sent,
+    core_got,
     hidden_up,
     hidden_down,
     hidden_got,
@@ -210,32 +248,63 @@
     vector_got,
 ):
     me, chip, core = (lax.axis_index(name) for name in ("mp", "chip", "core"))
-    tokens = hidden.shape[0]
+    tokens, part = hidden.shape
     rows = tokens // chunks
-    height = packed.shape[0]
+    height, units = packed.shape
+    lines = height // 7
     owner = chip * 2 + core
     bits = bits_below(chips)
     stages = len(bits)
     greet_around(size, chips)
 
-    own = [
-        pltpu.make_async_copy(qkv, full_qkv.at[owner], local.at[0]),
-        pltpu.make_async_copy(packed, full.at[me, chip], local.at[1]),
-        pltpu.make_async_copy(vectors, full_vectors.at[me], local.at[2]),
-        pltpu.make_async_copy(hidden, wide.at[me], local.at[3]),
+    matrices[0] = w_up[...].astype(BF16)
+    matrices[1] = w_gate[...].astype(BF16)
+    matrices[2] = w_down[...].T.astype(BF16)
+    wo_turned[...] = wo[...].T.astype(BF16)
+
+    def half_of(which):
+        return pl.ds(pl.multiple_of(which * units, units), units)
+
+    def place_of(matrix):
+        return pl.ds(pl.multiple_of((2 * matrix + core) * lines, lines), lines)
+
+    wo_place = (
+        pl.ds(6 * lines, lines),
+        pl.ds(pl.multiple_of(core * part, part), part),
+    )
+    given = [
+        to_device(
+            matrices.at[matrix, :, half_of(1 - core)],
+            packed.at[place_of(matrix), :],
+            core_sent.at[matrix],
+            core_got.at[matrix],
+            {"core": 1 - core},
+        )
+        for matrix in range(3)
     ]
-    for copy in own:
+    given.append(
+        to_device(
+            wo_turned, packed.at[wo_place], core_sent.at[3], core_got.at[3], {"core": 1 - core}
+        )
+    )
+    for copy in given:
         copy.start()
-
-    def hidden_hop(origin, chunk, ref, member, send):
-        at = pl.ds(chunk * rows, rows)
-        return to_member(
-            ref.at[at, :],
-            wide.at[origin, at, :],
-            send.at[origin, chunk],
-            hidden_got.at[origin, chunk],
-            member,
-        )
+    for matrix in range(3):
+        packed[place_of(matrix), :] = matrices[matrix, :, half_of(core)]
+    packed[wo_place] = wo_turned[...]
+    full_qkv[owner] = jnp.concatenate(
+        [
+            dot(wq[...].astype(BF16), in_pairs[...]).astype(BF16),
+            dot(wk[...].astype(BF16), in_pairs[...]).astype(BF16),
+            wv[...].astype(BF16),
+        ],
+        axis=1,
+    )
+
+    def hidden_hop(origin, chunk, member, send):
+        at = pl.ds(pl.multiple_of(chunk * rows, rows), rows)
+        ref = wide.at[origin, at, :]
+        return to_member(ref, ref, send.at[origin, chunk], hidden_got.at[origin, chunk], member)
 
     def packed_hop(origin, ref, member, send):
         return to_member(
@@ -283,22 +352,18 @@
             (me + distance < size, me + distance, 2 * distance, False),
         ]
 
-    own[0].wait()
-    own[1].wait()
-
-    def pass_on(origin, upward):
-        block = full.at[origin, chip]
+    def pass_on(origin, ref, upward):
         if upward is not False:
 
             @pl.when(me < size - 1)
             def _():
-                packed_hop(origin, block, me + 1, packed_up).start()
+                packed_hop(origin, ref, me + 1, packed_up).start()
 
         if not upward:
 
             @pl.when(me > 0)
             def _():
-                packed_hop(origin, block, me - 1, packed_down).start()
+                packed_hop(origin, ref, me - 1, packed_down).start()
 
     def advance(distance, stage):
         for exists, origin, slot, _ in sources[distance]:
@@ -309,12 +374,29 @@
                     half.arrive(stage)
                     half.start(stage + 1)
 
-    pass_on(me, None)
+    for copy in given:
+        copy.wait_recv()
+    pass_on(me, packed, None)
+    own = [
+        pltpu.make_async_copy(packed, full.at[me, chip], local.at[0]),
+        pltpu.make_async_copy(vectors, full_vectors.at[me], local.at[1]),
+    ]
+    for copy in own:
+        copy.start()
     gather_qkv.start(0)
+    for copy in vector_copies:
+        copy.start()
+    for chunk in range(chunks):
+        at = pl.ds(chunk * rows, rows)
+        wide[me, at, :] = hidden[at, :].astype(BF16)
+    own[0].wait()
     for half in plane(me, 0):
         half.start(0)
-    for copy in vector_copies:
-        copy.start()
+    for chunk in range(chunks):
+        at = pl.ds(chunk * rows, rows)
+        angles = positions[at, :] * frequency[...]
+        cosine[at, :] = jnp.cos(angles)
+        sine[at, :] = jnp.sin(angles)
     for stage in range(stages):
         gather_qkv.arrive(stage)
         gather_qkv.start(stage + 1)
@@ -324,8 +406,9 @@
 
             @pl.when(exists)
             def _():
-                packed_hop(origin, full.at[origin, chip], me, packed_up).wait_recv()
-                pass_on(origin, upward)
+                block = full.at[origin, chip]
+                packed_hop(origin, block, me, packed_up).wait_recv()
+                pass_on(origin, block, upward)
                 for half in plane(origin, slot):
                     half.start(0)
 
@@ -335,43 +418,99 @@
 
                 @pl.when(me < size - 1)
                 def _():
-                    hidden_hop(me, chunk, hidden, me + 1, hidden_up).start()
+                    hidden_hop(me, chunk, me + 1, hidden_up).start()
 
                 @pl.when(me > 0)
                 def _():
-                    hidden_hop(me, chunk, hidden, me - 1, hidden_down).start()
+                    hidden_hop(me, chunk, me - 1, hidden_down).start()
 
         if distance > 1:
             advance(distance - 1, 0)
+    gather_qkv.arrive(stages)
+    qkv_copy = pltpu.make_async_copy(full_qkv, qkv_out, local.at[2])
+    qkv_copy.start()
     advance(size - 1, 0)
-    for distance in range(1, size):
+
+    def come(distance, chunk):
+        for exists, origin, _, upward in sources[distance]:
+
+            @pl.when(exists)
+            def _():
+                hidden_hop(origin, chunk, me, hidden_up).wait_recv()
+                if upward:
+
+                    @pl.when(me < size - 1)
+                    def _():
+                        hidden_hop(origin, chunk, me + 1, hidden_up).start()
+                else:
+
+                    @pl.when(me > 0)
+                    def _():
+                        hidden_hop(origin, chunk, me - 1, hidden_down).start()
+
+    for distance in range(1, size - 1):
         for chunk in range(chunks):
-            for exists, origin, _, upward in sources[distance]:
-
-                @pl.when(exists)
-                def _():
-                    block = wide.at[origin]
-                    hidden_hop(origin, chunk, block, me, hidden_up).wait_recv()
-                    if upward:
-
-                        @pl.when(me < size - 1)
-                        def _():
-                            hidden_hop(origin, chunk, block, me + 1, hidden_up).start()
-                    else:
-
-                        @pl.when(me > 0)
-                        def _():
-                            hidden_hop(origin, chunk, block, me - 1, hidden_down).start()
-
+            come(distance, chunk)
+
+    results = (
+        (q, q_out),
+        (k, k_out),
+        (v, v_out),
+        (q_pair, q_pair_out),
+        (k_pair, k_pair_out),
+        (rq, rq_out),
+        (rk, rk_out),
+        (cosine, cosine_out),
+        (sine, sine_out),
+        (wide, wide_out),
+    )
+
+    def write_out(chunk):
+        at = pl.ds(pl.multiple_of(chunk * rows, rows), rows)
+        for order, (here, there) in enumerate(results):
+            lead = (slice(None),) * (len(here.shape) - 2)
+            yield pltpu.make_async_copy(
+                here.at[(*lead, at)], there.at[(*lead, at)], out_sems.at[order, chunk]
+            )
+
+    each = part // lines
+
+    def finish(chunk, carry):
+        come(size - 1, chunk)
+        at = pl.ds(pl.multiple_of(chunk * rows, rows), rows)
+        project_block(
+            [wide[member, at, :] for member in range(size)],
+            [
+                full_qkv[member * each : (member + 1) * each].reshape(part, 3 * part)
+                for member in range(size)
+            ],
+            cosine[at, :],
+            sine[at, :],
+            gain[...],
+            place_pair[...],
+            place_plain[...],
+            sums[...],
+            at,
+            [here for here, _ in results[:7]],
+        )
+        for copy in write_out(chunk):
+            copy.start()
+        return carry
+
+    lax.fori_loop(0, chunks, finish, 0)
     for stage in range(1, stages):
         for distance in range(size):
             advance(distance, stage)
-    gather_qkv.arrive(stages)
-
-    own[2].wait()
-    own[3].wait()
+
+    own[1].wait()
+    qkv_copy.wait()
     for copy in vector_copies:
         copy.wait()
+    for copy in given:
+        copy.wait_send()
+    for chunk in range(chunks):
+        for copy in write_out(chunk):
+            copy.wait()
     gather_qkv.close()
     for distance in range(size):
         for exists, origin, slot, upward in sources[distance]:
@@ -380,14 +519,14 @@
             def _():
                 for half in plane(origin, slot):
                     half.close()
-                block = full.at[origin, chip]
+                block = packed if distance == 0 else full.at[origin, chip]
                 if upward is not False:
 
                     @pl.when(me < size - 1)
                     def _():
                         packed_hop(origin, block, me, packed_up).wait_send()
                         for chunk in range(chunks):
-                            hidden_hop(origin, chunk, wide.at[origin], me, hidden_up).wait_send()
+                            hidden_hop(origin, chunk, me, hidden_up).wait_send()
 
                 if not upward:
 
@@ -395,28 +534,64 @@
                     def _():
                         packed_hop(origin, block, me, packed_down).wait_send()
                         for chunk in range(chunks):
-                            hidden_hop(
-                                origin, chunk, wide.at[origin], me, hidden_down
-                            ).wait_send()
-
-
-def gather_all(hidden, qkv, packed, vectors, size, chips, collective):
+                            hidden_hop(origin, chunk, me, hidden_down).wait_send()
+
+
+def front(
+    hidden,
+    weights,
+    vectors,
+    positions,
+    frequency,
+    gain,
+    in_pairs,
+    place_pair,
+    place_plain,
+    sums,
+    size,
+    chips,
+    collective,
+):
     chunks = 6
-    height = packed.shape[0]
+    tokens, part = hidden.shape
+    lines, both = weights[4].shape
+    units = both // 2
+    heads = part // DK
+    height = 7 * lines
     dma = pltpu.SemaphoreType.DMA
     line = dma((size, chunks))
     plane = dma((2 * size - 1, 2, max(chips - 1, 1)))
+    vmem = pl.BlockSpec(memory_space=pltpu.VMEM)
+    padded = ((heads, tokens, EXT), BF16)
+    paired = ((tokens, part), BF16)
+    scale = ((tokens, heads * HALF), F32)
+    wide = ((size, tokens, part), BF16)
+    qkv = ((2 * chips, lines, 3 * part), BF16)
+    results = [padded, padded, padded, paired, paired, scale, scale, scale, scale]
     return pl.pallas_call(
-        functools.partial(gather_all_kernel, size, chips, chunks, height // 32 * 16),
-        in_specs=[pl.BlockSpec(memory_space=pltpu.VMEM)] * 4,
-        out_specs=[ANY] * 4,
+        functools.partial(front_kernel, size, chips, chunks, height // 32 * 16),
+        in_specs=[vmem] * 16,
+        out_specs=[ANY] * 13,
         out_shape=[
-            jax.ShapeDtypeStruct((size, *hidden.shape), BF16),
-            jax.ShapeDtypeStruct((2 * chips, *qkv.shape), BF16),
-            jax.ShapeDtypeStruct((size, chips, *packed.shape), BF16),
-            jax.ShapeDtypeStruct((size, *vectors.shape), F32),
+            jax.ShapeDtypeStruct(*each)
+            for each in [
+                wide,
+                qkv,
+                ((size, chips, height, units), BF16),
+                ((size, *vectors.shape), F32),
+                *results,
+            ]
         ],
         scratch_shapes=[
+            pltpu.VMEM(*wide),
+            pltpu.VMEM(*qkv),
+            pltpu.VMEM((height, units), BF16),
+            pltpu.VMEM((3, lines, both), BF16),
+            pltpu.VMEM((lines, part), BF16),
+            *[pltpu.VMEM(*each) for each in results],
+            dma((3,)),
+            dma((10, chunks)),
+            dma((4,)),
             dma((4,)),
             line,
             line,
@@ -432,8 +607,19 @@
             dma((size,)),
         ],
         compiler_params=remote_params(collective),
-        name="gather_all",
-    )(hidden, qkv, packed, vectors)
+        name="front",
+    )(
+        hidden,
+        *weights,
+        vectors,
+        positions,
+        frequency,
+        gain,
+        in_pairs,
+        place_pair,
+        place_plain,
+        sums,
+    )
 
 
 class LineSum:
@@ -912,22 +1098,14 @@
     return dot(high, matrix) + dot(rest, matrix)
 
 
-def project_kernel(
-    wide, weight, cosine, sine, gain, place_pair, place_plain, sums, q, k, v, q_pair, k_pair, rq, rk
-):
-    parts = wide.shape[0]
+def project_block(wide, weight, cos, sin, gain, place_pair, place_plain, sums, at, outs):
+    q, k, v, q_pair, k_pair, rq, rk = outs
     heads = q.shape[0]
-    pair = heads * HALF
-    width = heads * DK
+    pair, width = heads * HALF, heads * DK
     raw = dot(wide[0], weight[0])
-    for part in range(1, parts):
+    for part in range(1, len(wide)):
         raw += dot(wide[part], weight[part])
-    rows = raw.shape[0]
-    lane = lax.broadcasted_iota(jnp.int32, (rows, EXT), 1)
-    cos = cosine[...]
-    sin = sine[...]
-    gain_first = gain[:, :pair]
-    gain_second = gain[:, pair:]
+    lane = lax.broadcasted_iota(jnp.int32, (raw.shape[0], EXT), 1)
     for offset, out, pair_out, scale_out, factor in (
         (0, q, q_pair, rq, math.sqrt(DK)),
         (width, k, k_pair, rk, 1.0),
@@ -936,65 +1114,27 @@
         second = raw[:, offset + pair : offset + width]
         turned_first = first * cos - second * sin
         turned_second = second * cos + first * sin
-        total = split_dot(
-            turned_first * turned_first + turned_second * turned_second, sums[...]
-        )
+        total = split_dot(turned_first * turned_first + turned_second * turned_second, sums)
         scale = lax.rsqrt(total + EPSILON)
-        scale_out[...] = scale
+        scale_out[at, :] = scale
         both = jnp.concatenate(
-            [turned_first * scale * gain_first, turned_second * scale * gain_second], axis=1
+            [
+                turned_first * scale * gain[:, :pair],
+                turned_second * scale * gain[:, pair:],
+            ],
+            axis=1,
         ).astype(BF16)
-        pair_out[...] = both
-        padded = dot(both, place_pair[...]) * factor
+        pair_out[at, :] = both
+        padded = dot(both, place_pair) * factor
         for head in range(heads):
             piece = padded[:, head * EXT : (head + 1) * EXT]
             if factor == 1.0:
                 piece = jnp.where(lane < DK, piece, 1.0)
-            out[head] = piece.astype(BF16)
-    padded = dot(raw[:, 2 * width :].astype(BF16), place_plain[...])
+            out[head, at, :] = piece.astype(BF16)
+    padded = dot(raw[:, 2 * width :].astype(BF16), place_plain)
     for head in range(heads):
         piece = padded[:, head * EXT : (head + 1) * EXT]
-        v[head] = jnp.where(lane < DK, piece, 1.0).astype(BF16)
-
-
-def project(wide, weight, cosine, sine, gain, place_pair, place_plain, sums):
-    parts, tokens, part = wide.shape
-    width = gain.shape[1]
-    heads = width // DK
-    block = min(512, tokens)
-    padded = jax.ShapeDtypeStruct((heads, tokens, EXT), BF16)
-    scale = jax.ShapeDtypeStruct((tokens, heads * HALF), F32)
-
-    def whole(array):
-        return pl.BlockSpec(array.shape, lambda i: (0,) * array.ndim)
-
-    rows = pl.BlockSpec((block, heads * HALF), lambda i: (i, 0))
-    headed = pl.BlockSpec((heads, block, EXT), lambda i: (0, i, 0))
-    paired = pl.BlockSpec((block, width), lambda i: (i, 0))
-    both = jax.ShapeDtypeStruct((tokens, width), BF16)
-    return pl.pallas_call(
-        project_kernel,
-        grid=(tokens // block,),
-        in_specs=[
-            pl.BlockSpec((parts, block, part), lambda i: (0, i, 0)),
-            whole(weight),
-            rows,
-            rows,
-            whole(gain),
-            whole(place_pair),
-            whole(place_plain),
-            whole(sums),
-        ],
-        out_specs=[headed, headed, headed, paired, paired, rows, rows],
-        out_shape=[padded, padded, padded, both, both, scale, scale],
-        compiler_params=grid_params(1),
-        cost_estimate=pl.CostEstimate(
-            flops=2 * tokens * parts * part * width * 3,
-            bytes_accessed=20 << 20,
-            transcendentals=0,
-        ),
-        name="project",
-    )(wide, weight, cosine, sine, gain, place_pair, place_plain, sums)
+        v[head, at, :] = jnp.where(lane < DK, piece, 1.0).astype(BF16)
 
 
 def split_three(value):
@@ -2098,23 +2238,11 @@
     )(x, dbranch, dup, dgate, units_in, dbranch_attn, merged, dmerged)
 
 
-def rope_tables(positions, head_size):
-    half_size = head_size // 2
-    freq_index = jnp.arange(half_size, dtype=F32)
-    inverse = jnp.exp(freq_index * (-2.0 * math.log(ROPE_BASE) / head_size))
-    angles = positions.astype(F32)[..., None] * inverse
-    return (jnp.cos(angles), jnp.sin(angles))
-
-
 def document_starts(doc_ids):
     slot_index = jnp.arange(doc_ids.shape[-1], dtype=jnp.int32)
     earlier = jnp.concatenate([doc_ids[..., :1] - 1, doc_ids[..., :-1]], axis=-1)
     starts = jnp.where(doc_ids != earlier, slot_index, jnp.zeros_like(slot_index))
     return lax.cummax(starts, axis=starts.ndim - 1)
-
-
-def other_core(value):
-    return lax.ppermute(value, "core", [(0, 1), (1, 0)])
 
 
 def make_on_device(chips, size):
@@ -2147,30 +2275,54 @@
         core = lax.axis_index("core")
 
         place = paired_place(heads)
-        in_pairs = (
-            lambda w: w.reshape(w.shape[0], heads, 2, HALF)
-            .transpose(0, 2, 1, 3)
-            .reshape(w.shape[0], heads * DK)
-        )
-        low_qkv = jnp.concatenate([in_pairs(wq), in_pairs(wk), wv], axis=1).astype(BF16)
-        stacked = jnp.stack([w_up, w_gate, w_down.T]).astype(BF16).reshape(3, rows, 2, units)
-        keep = lax.dynamic_index_in_dim(stacked, core, 2, keepdims=False)
-        give = lax.dynamic_index_in_dim(stacked, 1 - core, 2, keepdims=False)
-        low_wo = wo.astype(BF16).T
-        wide_wo = jnp.concatenate([low_wo, low_wo], axis=1)
-        given = jnp.concatenate([give.reshape(3 * rows, units), wide_wo])
-        got = other_core(given)
-
-        def in_order(own, other):
-            return jnp.where(core == 0, jnp.stack([own, other], 1), jnp.stack([other, own], 1))
-
-        pair = in_order(keep, got[: 3 * rows].reshape(3, rows, units))
-        lane = jnp.arange(2 * part) // part
-        pair_wo = jnp.where(lane == core, wide_wo, got[3 * rows :])
-        packed = jnp.concatenate([pair.reshape(6 * rows, units), pair_wo])
+        to_pair = placing_matrix(place, heads)
+        to_plain = placing_matrix(np.arange(heads * DK), heads)
+        turn = np.zeros((part, part), np.float32)
+        turn[np.arange(part), place] = 1
+        place_pair = jnp.asarray(to_pair, BF16)
+        place_plain = jnp.asarray(to_plain, BF16)
+        place_delta = jnp.asarray(delta_matrix(heads), BF16)
+        collect_plain = jnp.asarray(to_plain.T.reshape(heads, EXT, heads * DK), BF16)
+        sums = jnp.asarray(head_sum_matrix(heads), BF16)
+        gain = s_qk.reshape(heads, 2, HALF).transpose(1, 0, 2).reshape(1, part)
+        docs = doc_ids[0]
+        starts = document_starts(docs)
+        slot = jnp.arange(slots, dtype=jnp.int32)
+        low = jnp.concatenate([starts[::block] // block, me[None]])
+        key_docs = jnp.where(valid[0] == 1, docs, -1)
+        inverse = jnp.exp(
+            jnp.arange(HALF, dtype=F32) * (-2.0 * math.log(ROPE_BASE) / DK)
+        )
+
         vectors = jnp.concatenate([s_u, s_v * math.sqrt(width), alpha_a, alpha_m])
-        wide, full_qkv, packed, vectors = gather_all(
-            hidden[0].astype(BF16), low_qkv, packed, vectors[None], size, chips, 0
+        (
+            wide,
+            full_qkv,
+            packed,
+            vectors,
+            q,
+            k,
+            v,
+            q_pair,
+            k_pair,
+            rq,
+            rk,
+            cosine,
+            sine,
+        ) = front(
+            hidden[0],
+            (wq, wk, wv, wo, w_up, w_gate, w_down),
+            vectors[None],
+            (slot - starts).astype(F32)[:, None],
+            jnp.tile(inverse, heads)[None],
+            gain,
+            jnp.asarray(turn, BF16),
+            place_pair,
+            place_plain,
+            sums,
+            size,
+            chips,
+            0,
         )
         full_qkv = full_qkv.reshape(size, part, 3 * part)
         vectors = vectors[:, 0]
@@ -2183,26 +2335,6 @@
         alpha_attn = vectors[:, 4 * units : 4 * units + part].reshape(1, width)
         alpha_mlp = vectors[:, 4 * units + part :].reshape(1, width)
 
-        docs = doc_ids[0]
-        starts = document_starts(docs)
-        slot = jnp.arange(slots, dtype=jnp.int32)
-        cosine, sine = rope_tables(slot - starts, DK)
-        cosine = jnp.tile(cosine, (1, heads))
-        sine = jnp.tile(sine, (1, heads))
-        low = jnp.concatenate([starts[::block] // block, me[None]])
-        key_docs = jnp.where(valid[0] == 1, docs, -1)
-        to_pair = placing_matrix(place, heads)
-        to_plain = placing_matrix(np.arange(heads * DK), heads)
-        place_pair = jnp.asarray(to_pair, BF16)
-        place_plain = jnp.asarray(to_plain, BF16)
-        place_delta = jnp.asarray(delta_matrix(heads), BF16)
-        collect_plain = jnp.asarray(to_plain.T.reshape(heads, EXT, heads * DK), BF16)
-        sums = jnp.asarray(head_sum_matrix(heads), BF16)
-        gain = in_pairs(s_qk[None, :])
-
-        q, k, v, q_pair, k_pair, rq, rk = project(
-            wide, full_qkv, cosine, sine, gain, place_pair, place_plain, sums
-        )
         attended, qback = attend(
             low,
             q,

time: 744 us -> 715 us (0.961); the launches traced: 743 us -> 701 us
  Pallas kernels: 688 us -> 667 us
  other arithmetic: 21.3 us -> 10.4 us
  local copies, waits for them, and re-layouts: 31.2 us -> 21.6 us
    pallas_call x2 -> x1, Pallas kernels: 185 us -> 175 us  [front(): pl.pallas_call(functools.partial(front_kernel, size, chips, chunks, heigh...]
  transfers between devices with their start and end apart: 1 -> 0, of which waited for: 0 -> 0; matrix products, arithmetic and copies ran while one was open for 3% -> 0% of each run, Pallas kernels for 0% -> 0%
where the time goes in v5:
time: 715 us; the launch traced here: 701 us
  Pallas kernels  667 us (93%)
  local copies, waits for them, and re-layouts  21.6 us (3%)
  other arithmetic  10.4 us (1%)
    pallas_call x1, Pallas kernels, sum_all(): pl.pallas_call(functools.partial(sum_all_kernel, size, chips, chunks, spl...  197 us
    pallas_call x1, Pallas kernels, front(): pl.pallas_call(functools.partial(front_kernel, size, chips, chunks, heigh...  175 us
    pallas_call x1, Pallas kernels, attend_back(): pl.pallas_call(attend_back_kernel, grid_spec=pltpu.PrefetchScalarGridSpec...  79.1 us
    pallas_call x1, Pallas kernels, mix(): pl.pallas_call(functools.partial(mix_kernel, size), in_specs=[ANY, ANY, A...  54.6 us
    pallas_call x1, Pallas kernels, feed(): pl.pallas_call(functools.partial(feed_kernel, size), grid=(2, parts), in_...  48.5 us
    pallas_call x1, Pallas kernels, feed_back(): pl.pallas_call(functools.partial(feed_back_kernel, size), grid=(2, parts)...  46 us
    pallas_call x1, Pallas kernels, feed_grads(): pl.pallas_call(functools.partial(feed_grads_kernel, size), grid=(4, parts...  41.7 us
    pallas_call x1, Pallas kernels, attend(): pl.pallas_call(attend_kernel, grid_spec=pltpu.PrefetchScalarGridSpec(num_...  25.3 us

profile of v5, /device:TPU:17, one launch (start us, length us, event | category | flops | bytes accessed | tf_op | source)
XLA Modules:
  0.0 701.0 jit_solution(8485833690339864289)
XLA Ops:
  0.6 1.2 slice.55
  2.5 0.9 add_select_fusion
  4.5 1.2 convert_element_type.11.positions
  5.9 0.6 reshape.181.gain
  6.5 0.6 broadcast_in_dim.43.vectors
  7.8 174.6 %front.1 = (bf16[4,3072,256]{2,1,0:T(8,128)(2,1)}, bf16[8,128,768]{2,1,0:T(8,128)(2,1)}, bf16[4,4,896,512]{3,2,1,0:T(8,128)(2,1)}, f32[4,1,2560]{2,1,0:T(1,128)}...) custom-call(f32[3072,256]{1,0:T(8,128)} %bitcast.69, ...), custom_call_target="tpu_custom_call" | custom-call | tf_op jit(solution)/shard_map/front/pallas_call | solution.py:571
  183.2 0.6 broadcast_select_fusion.1.kdoc
  183.8 1.7 copy.57.qdoc
  185.5 25.3 %attend.1 = (bf16[3072,256]{1,0:T(8,128)(2,1)}, bf16[4,3072,128]{2,1,0:T(8,128)(2,1)}) custom-call(s32[7]{0:T(128)} %pad_add_fusion.low, bf16[4,3072,128]{2,1,0:T(8,128)(2,1)} %get-tuple-element.65.q, bf16[4,3072,128]{2,1,0:T(8,128)(2,1)} %get-tuple-element.66.k, bf16[4,3072,128]{2,1,0:T(8,128)(2,1)} %get-tuple-element.67.v, s32[3072,1]{1,0:T(8,128)} %copy.57.qdoc, ...), custom_call_target="tpu_custom_call" | custom-call | flops 40000000000 | bytes 16777216 | tf_op jit(solution)/shard_map/attend/pallas_call | solution.py:1201
  211.4 54.6 %mix.1 = (bf16[1536,1024]{1,0:T(8,128)(2,1)}, f32[768,1024]{1,0:T(8,128)}, bf16[768,1024]{1,0:T(8,128)(2,1)}, f32[768,1]{1,0:T(8,128)}, f32[768,1]{1,0:T(8,128)}...) custom-call(bf16[3072,256]{1,0:T(8,128)(2,1)} %get-tuple-element.68., ...), custom_call_target="tpu_custom_call" | custom-call | tf_op jit(solution)/shard_map/mix/pallas_call | solution.py:1681
  267.9 48.5 %feed.1 = (bf16[4,1536,512]{2,1,0:T(8,128)(2,1)}, bf16[4,1536,512]{2,1,0:T(8,128)(2,1)}, bf16[4,1536,512]{2,1,0:T(8,128)(2,1)}, bf16[768,1024]{1,0:T(8,128)(2,1)...) custom-call(bf16[1536,1024]{1,0:T(8,128)(2,1)} %get-tuple-element.72.x, ...), custom_call_target="tpu_custom_call" | custom-call | flops 19327352832 | bytes 62914560 | tf_op jit(solution)/shard_map/feed/pallas_call | solution.py:1869
  316.4 46.0 %feed_back.1 = (bf16[4,1536,512]{2,1,0:T(8,128)(2,1)}, bf16[4,1536,512]{2,1,0:T(8,128)(2,1)}, f32[4,1,512]{2,1,0:T(1,128)}, f32[4,1,512]{2,1,0:T(1,128)}, bf16[3...) custom-call(bf16[1536,1024]{1,0:T(8,128)(2,1)} %get-tuple-element.75, ...), custom_call_target="tpu_custom_call" | custom-call | flops 19327352832 | bytes 73400320 | tf_op jit(solution)/shard_map/feed_back/pallas_call | solution.py:2059
  362.5 0.8 dynamic_update_slice.9
  363.3 0.7 broadcast_multiply_fusion
  364.1 41.7 %feed_grads.1 = (bf16[4,4,768,512]{3,2,1,0:T(8,128)(2,1)}, bf16[4,4,2,128,256]{4,3,2,1,0:T(8,128)(2,1)}, bf16[3072,256]{1,0:T(8,128)(2,1)}) custom-call(bf16[1536,1024]{1,0:T(8,128)(2,1)} %get-tuple-element.72.x, bf16[1536,1024]{1,0:T(8,128)(2,1)} %get-tuple-element.75.dbranch, bf16[4,1536,512]{2,1,0:T(8,128)(2,1)} %get-tuple-element.88.dup, ...), custom_call_target="tpu_custom_call" | custom-call | flops 19327352832 | bytes 41943040 | tf_op jit(solution)/shard_map/feed_grads/pallas_call | solution.py:2199
  405.8 0.7 copy.58
  406.5 1.3 broadcast_select_fusion.kdoc
  407.8 79.1 %attend_back.1 = (bf16[4,3072,256]{2,1,0:T(8,128)(2,1)}, bf16[4,256,768]{2,1,0:T(8,128)(2,1)}, f32[1,256]{1,0:T(1,128)}) custom-call(s32[7]{0:T(128)} %pad_add_fusion.low, bf16[4,3072,128]{2,1,0:T(8,128)(2,1)} %get-tuple-element.86.qback, bf16[3072,256]{1,0:T(8,128)(2,1)} %get-tuple-element.87.q_pair, bf16[3072,256]{1,0:T(8,128)(2,1)} %get-tuple-element.94.dout, ...), custom_call_target="tpu_custom_call" | custom-call | flops 80000000000 | bytes 31457280 | tf_op jit(solution)/shard_map/attend_back/pallas_call | solution.py:1453
  487.4 1.3 reduce.11
  489.0 0.7 reduce.12
  489.7 0.7 reduce.13
  490.4 0.7 broadcast_in_dim.52.vectors
  491.0 196.9 %sum_all.1 = (f32[3072,256]{1,0:T(8,128)}, f32[3,128,1024]{2,1,0:T(8,128)}, f32[128,256]{1,0:T(8,128)}, f32[128,768]{1,0:T(8,128)}, f32[1,2816]{1,0:T(1,128)}) custom-call(bf16[4,3072,256]{2,1,0:T(8,128)(2,1)} %get-tuple-element.102.term, bf16[4,4,768,512]{3,2,1,0:T(8,128)(2,1)} %get-tuple-element.103.grads, ...), custom_call_target="tpu_custom_call" | custom-call | tf_op jit(solution)/shard_map/sum_all/pallas_call | solution.py:1026
  688.0 2.5 slice_bitcast_fusion
  690.5 1.0 copy.68
  691.5 0.7 fusion.2
  692.3 0.8 copy.65
  693.2 0.8 copy.66
  693.9 0.8 copy.67
  695.9 1.9 bitcast_convert_fusion
  697.8 1.1 copy-done.1
  698.9 1.7 copy.86
  (82 shorter events, 7.4 us)
Async XLA Ops:
  4.5 1.3 copy-start.13
  4.5 2.0 copy-start.9
  4.5 2.0 copy-start.12
  4.5 2.0 copy-start.14
  4.5 2.0 copy-start.15
  7.8 175.4 %copy-start.7 = (s32[1,3072]{1,0:T(1,128)S(1)}, s32[1,3072]{1,0:T(1,128)}, u32[]{:S(2)}) copy-start(s32[1,3072]{1,0:T(1,128)} %param.36) | copy-start | bytes 36868
  7.8 175.4 %copy-start.4 = (s32[1,3072]{1,0:T(1,128)S(1)}, s32[1,3072]{1,0:T(1,128)}, u32[]{:S(2)}) copy-start(s32[1,3072]{1,0:T(1,128)} %param.35) | copy-start | bytes 36868
  185.5 25.3 %copy-start.6 = (f32[4,1,2560]{2,1,0:T(1,128)S(1)}, f32[4,1,2560]{2,1,0:T(1,128)}, u32[]{:S(2)}) copy-start(f32[4,1,2560]{2,1,0:T(1,128)} %get-tuple-element.71) | copy-start | bytes 122884
  364.1 42.4 %copy-start = (s32[3072,1]{1,0:T(8,128)S(1)}, s32[3072,1]{1,0:T(8,128)}, u32[]{:S(2)}) copy-start(s32[3072,1]{1,0:T(8,128)} %copy.57.qdoc) | copy-start | bytes 36868
  407.8 81.2 %copy-start.11 = (f32[1,1024]{1,0:T(1,128)S(1)}, f32[1,1024]{1,0:T(1,128)}, u32[]{:S(2)}) copy-start(f32[1,1024]{1,0:T(1,128)} %get-tuple-element.109) | copy-start | bytes 12292
  407.8 81.9 %copy-start.10 = (f32[1,1024]{1,0:T(1,128)S(1)}, f32[1,1024]{1,0:T(1,128)}, u32[]{:S(2)}) copy-start(f32[1,1024]{1,0:T(1,128)} %get-tuple-element.110) | copy-start | bytes 12292
  688.0 3.5 copy-start.3
  690.5 3.4 copy-start.5
  691.5 3.2 copy-start.8
  691.5 4.4 copy-start.2
  695.9 3.0 copy-start.1

commit v6 on v5

--- a/solution.py
+++ b/solution.py
@@ -182,6 +182,9 @@
                 copy.wait_send()
 
 
+EARLY = 2
+
+
 def front_kernel(
     size,
     chips,
@@ -196,7 +199,7 @@
     w_gate,
     w_down,
     vectors,
-    positions,
+    columns,
     frequency,
     gain,
     in_pairs,
@@ -257,6 +260,25 @@
     stages = len(bits)
     greet_around(size, chips)
 
+    def hidden_hop(origin, chunk, member, send):
+        at = pl.ds(pl.multiple_of(chunk * rows, rows), rows)
+        ref = wide.at[origin, at, :]
+        return to_member(ref, ref, send.at[origin, chunk], hidden_got.at[origin, chunk], member)
+
+    def send_hidden(chunk):
+        @pl.when(me < size - 1)
+        def _():
+            hidden_hop(me, chunk, me + 1, hidden_up).start()
+
+        @pl.when(me > 0)
+        def _():
+            hidden_hop(me, chunk, me - 1, hidden_down).start()
+
+    for chunk in range(EARLY):
+        at = pl.ds(chunk * rows, rows)
+        wide[me, at, :] = hidden[at, :].astype(BF16)
+        send_hidden(chunk)
+
     matrices[0] = w_up[...].astype(BF16)
     matrices[1] = w_gate[...].astype(BF16)
     matrices[2] = w_down[...].T.astype(BF16)
@@ -300,11 +322,6 @@
         ],
         axis=1,
     )
-
-    def hidden_hop(origin, chunk, member, send):
-        at = pl.ds(pl.multiple_of(chunk * rows, rows), rows)
-        ref = wide.at[origin, at, :]
-        return to_member(ref, ref, send.at[origin, chunk], hidden_got.at[origin, chunk], member)
 
     def packed_hop(origin, ref, member, send):
         return to_member(
@@ -386,7 +403,7 @@
     gather_qkv.start(0)
     for copy in vector_copies:
         copy.start()
-    for chunk in range(chunks):
+    for chunk in range(EARLY, chunks):
         at = pl.ds(chunk * rows, rows)
         wide[me, at, :] = hidden[at, :].astype(BF16)
     own[0].wait()
@@ -394,7 +411,7 @@
         half.start(0)
     for chunk in range(chunks):
         at = pl.ds(chunk * rows, rows)
-        angles = positions[at, :] * frequency[...]
+        angles = columns[at, 0:1] * frequency[...]
         cosine[at, :] = jnp.cos(angles)
         sine[at, :] = jnp.sin(angles)
     for stage in range(stages):
@@ -414,15 +431,8 @@
 
         @pl.when(jnp.maximum(me, size - 1 - me) == distance)
         def _():
-            for chunk in range(chunks):
-
-                @pl.when(me < size - 1)
-                def _():
-                    hidden_hop(me, chunk, me + 1, hidden_up).start()
-
-                @pl.when(me > 0)
-                def _():
-                    hidden_hop(me, chunk, me - 1, hidden_down).start()
+            for chunk in range(EARLY, chunks):
+                send_hidden(chunk)
 
         if distance > 1:
             advance(distance - 1, 0)
@@ -659,6 +669,14 @@
                     slots[goal, at, :].astype(F32) + self.term(goal, at).astype(F32)
                 ).astype(BF16)
 
+            if order > 0:
+                older = goal + 1 if upward else goal - 1
+                sent = (me < older) if upward else (me > older)
+
+                @pl.when(sent)
+                def _():
+                    self.hop(upward, older, chunk, member).wait_send()
+
             @pl.when(ahead)
             def _():
                 self.hop(upward, goal, chunk, member).start()
@@ -678,16 +696,19 @@
             out[out_at, :] += self.down[me, at, :].astype(F32)
 
     def close(self):
-        for order in range(self.size - 1):
-            for chunk in range(self.chunks):
-
-                @pl.when(self.me < self.size - 1 - order)
-                def _():
-                    self.hop(True, self.size - 1 - order, chunk, self.me).wait_send()
-
-                @pl.when(self.me > order)
-                def _():
-                    self.hop(False, order, chunk, self.me).wait_send()
+        order = self.size - 2
+        for chunk in range(self.chunks):
+
+            @pl.when(self.me < self.size - 1 - order)
+            def _():
+                self.hop(True, self.size - 1 - order, chunk, self.me).wait_send()
+
+            @pl.when(self.me > order)
+            def _():
+                self.hop(False, order, chunk, self.me).wait_send()
+
+
+MIDDLE, LATE = 4, 5
 
 
 class ChipSum:
@@ -701,7 +722,7 @@
                 acc.at[layer, slot],
                 load.at[layer, slot],
             )
-            for layer in range(layers)
+            for layer in layers
             for slot in range(self.half)
         ]
         self.source, self.sent, self.received = source, send, receive
@@ -714,7 +735,7 @@
         count = self.half >> stage
         offset = 2 * self.half - 2 * count
         where = {"chip": flip(self.chip, self.bits[stage])}
-        for layer in range(self.layers):
+        for layer in self.layers:
             for slot in range(count):
                 if stage == 0:
                     other = flip(self.chip, self.bits[0] | self.combo(slot))
@@ -763,10 +784,15 @@
     grad_wo,
     grad_qkv,
     vectors,
+    out_pairs,
     out,
-    owned,
+    owned_up,
+    owned_gate,
+    owned_down,
     owned_wo,
-    owned_qkv,
+    owned_q,
+    owned_k,
+    owned_v,
     owned_vectors,
     term_up,
     term_down,
@@ -789,6 +815,8 @@
     acc_qkv,
     got_qkv,
     whole,
+    owned,
+    turned_wo,
     vector_sum,
     vector_got,
     vector_line,
@@ -815,28 +843,36 @@
     line = LineSum(
         size, chunks, lambda goal, at: term[goal, at, :], term_up, term_down, sems(term_sems, 0)
     )
-    sum_a = ChipSum(
-        size,
-        bits,
-        lambda m, c: grads.at[m, c, pl.ds(0, split), :],
-        acc_a,
-        got_a,
-        load_sems.at[0],
-        chip_sent.at[0],
-        chip_got.at[0],
-    )
-    sum_b = ChipSum(
-        size,
-        bits[::-1],
-        lambda m, c: grads.at[m, c, pl.ds(split, grads.shape[2] - split), :],
-        acc_b,
-        got_b,
-        load_sems.at[1],
-        chip_sent.at[1],
-        chip_got.at[1],
-    )
+    ends = sorted({0, size - 1})
+    inner = [layer for layer in range(size) if layer not in ends]
+
+    def plane_sums(layers):
+        return [
+            ChipSum(
+                layers,
+                bits,
+                lambda m, c: grads.at[m, c, pl.ds(0, split), :],
+                acc_a,
+                got_a,
+                load_sems.at[0],
+                chip_sent.at[0],
+                chip_got.at[0],
+            ),
+            ChipSum(
+                layers,
+                bits[::-1],
+                lambda m, c: grads.at[m, c, pl.ds(split, grads.shape[2] - split), :],
+                acc_b,
+                got_b,
+                load_sems.at[1],
+                chip_sent.at[1],
+                chip_got.at[1],
+            ),
+        ]
+
+    sums_ends, sums_inner = plane_sums(ends), plane_sums(inner)
     sum_wo = ChipSum(
-        size,
+        range(size),
         bits[::-1],
         lambda m, c: pair_wo.at[m, c],
         acc_wo,
@@ -846,7 +882,7 @@
         chip_got.at[2],
     )
     sum_qkv = ChipSum(
-        1,
+        range(1),
         bits,
         lambda m, c: pair_qkv.at[c],
         acc_qkv,
@@ -893,8 +929,8 @@
     ]
     for copy in own + given:
         copy.start()
-    sum_a.start(0)
-    sum_b.start(0)
+    for part in sums_ends:
+        part.start(0)
     for copy in vector_copies:
         copy.start()
 
@@ -924,46 +960,61 @@
         if stage < len(vector_bits):
             vector_copy(stage).start()
 
-    for chunk in range(chunks):
-        line.step(0, chunk)
-    for copy in own:
-        copy.wait()
-    for copy in given:
-        copy.wait_recv()
-    pair_wo[...] = (pair_wo[...].astype(F32) + other_wo[...].astype(F32)).astype(BF16)
-    pair_qkv[...] = (pair_qkv[...].astype(F32) + other_qkv[...].astype(F32)).astype(BF16)
-    sum_wo.start(0)
-    sum_qkv.start(0)
-    vector_step(0)
-    vector_step(1)
-    for order in range(1, size - 1):
-        for chunk in range(chunks):
-            line.step(order, chunk)
-        if order - 1 < stages:
-            for part in (sum_a, sum_b, sum_wo, sum_qkv):
-                part.add(order - 1)
-                if order < stages:
-                    part.start(order)
-    for stage in range(size - 2, stages):
-        for part in (sum_a, sum_b, sum_wo, sum_qkv):
+    def add(group, stage):
+        for part in group:
             part.add(stage)
             if stage + 1 < stages:
                 part.start(stage + 1)
-    lines[0].step(0, 0)
-    lines[1].step(0, 0)
-    lines[2].step(0, 0)
-    for stage in range(2, len(vector_bits) + 1):
+
+    small = [sum_wo, sum_qkv]
+    rest = [*sums_inner, *small]
+    vector_at = 0
+    for order in range(size - 1):
+        for chunk in range(chunks):
+            line.step(order, chunk)
+            if order == 0 and chunk >= 1 and vector_at <= len(vector_bits):
+                vector_step(vector_at)
+                vector_at += 1
+            if order == 1 and chunk == MIDDLE:
+                for stage in range(1, stages):
+                    add(sums_ends, stage)
+                for part in rest:
+                    part.start(0)
+            if order == 2 and chunk == LATE:
+                add(rest, 0)
+        if order == 0:
+            for copy in own:
+                copy.wait()
+            for copy in given:
+                copy.wait_recv()
+            pair_wo[...] = (pair_wo[...].astype(F32) + other_wo[...].astype(F32)).astype(BF16)
+            pair_qkv[...] = (pair_qkv[...].astype(F32) + other_qkv[...].astype(F32)).astype(
+                BF16
+            )
+            add(sums_ends, 0)
+        if order == 1:
+            lines[0].step(0, 0)
+            lines[1].step(0, 0)
+    for stage in range(1, stages):
+        add(rest, stage)
+    for order in range(size - 1):
+        if order > 0:
+            lines[0].step(order, 0)
+            lines[1].step(order, 0)
+        lines[2].step(order, 0)
+    for stage in range(vector_at, len(vector_bits) + 1):
         vector_step(stage)
     for chunk in range(chunks):
         line.result(chunk, out, line.at(chunk))
-    for order in range(1, size - 1):
-        for part in lines:
-            part.step(order, 0)
     owned_vectors[...] = vector_sum[len(vector_bits)]
-    owned_qkv[...] = acc_qkv[0, 0].astype(F32)
+    part = owned_v.shape[1]
+    total_qkv = acc_qkv[0, 0]
+    owned_q[...] = dot(total_qkv[:, :part], out_pairs[...])
+    owned_k[...] = dot(total_qkv[:, part : 2 * part], out_pairs[...])
+    owned_v[...] = total_qkv[:, 2 * part :].astype(F32)
     lines[0].result(0, whole, pl.ds(0, split))
     lines[1].result(0, whole, pl.ds(split, whole.shape[0] - split))
-    lines[2].result(0, owned_wo, slice(None))
+    lines[2].result(0, turned_wo, slice(None))
 
     matrices, rows, columns = owned.shape
     columns = columns // 2
@@ -987,21 +1038,25 @@
         )
         copy.start()
         swaps.append(copy)
+    owned_wo[...] = turned_wo[...].T
     for copy in swaps:
         copy.wait()
+    owned_up[...] = owned[0]
+    owned_gate[...] = owned[1]
+    owned_down[...] = owned[2].T
 
     for copy in given + vector_copies:
         copy.wait_send()
     for stage in range(len(vector_bits)):
         vector_copy(stage).wait_send()
-    for part in (sum_a, sum_b, sum_wo, sum_qkv):
+    for part in [*sums_ends, *rest]:
         part.close()
     line.close()
     for part in lines:
         part.close()
 
 
-def sum_all(term, grads, grad_wo, grad_qkv, vectors, chips, collective):
+def sum_all(term, grads, grad_wo, grad_qkv, vectors, out_pairs, chips, collective):
     size, tokens, part = term.shape
     height, units = grads.shape[2:]
     rows = height // 6
@@ -1025,13 +1080,15 @@
 
     return pl.pallas_call(
         functools.partial(sum_all_kernel, size, chips, chunks, split),
-        in_specs=[vmem, ANY, ANY, ANY, vmem],
-        out_specs=[vmem] * 5,
+        in_specs=[vmem, ANY, ANY, ANY, vmem, vmem],
+        out_specs=[vmem] * 9,
         out_shape=[
             jax.ShapeDtypeStruct((tokens, part), F32),
-            jax.ShapeDtypeStruct((3, rows, 2 * units), F32),
-            jax.ShapeDtypeStruct(wo_block, F32),
-            jax.ShapeDtypeStruct(qkv_block, F32),
+            jax.ShapeDtypeStruct((rows, 2 * units), F32),
+            jax.ShapeDtypeStruct((rows, 2 * units), F32),
+            jax.ShapeDtypeStruct((2 * units, rows), F32),
+            jax.ShapeDtypeStruct(wo_block[::-1], F32),
+            *[jax.ShapeDtypeStruct((qkv_block[0], part), F32)] * 3,
             jax.ShapeDtypeStruct(long, F32),
         ],
         scratch_shapes=[
@@ -1048,6 +1105,8 @@
             pltpu.VMEM((chips, *qkv_block), BF16),
             *sums(1, qkv_block),
             pltpu.VMEM((height, units), F32),
+            pltpu.VMEM((3, rows, 2 * units), F32),
+            pltpu.VMEM(wo_block, F32),
             pltpu.VMEM((stages + 1, *long), F32),
             pltpu.VMEM((stages + 1, *long), F32),
             pltpu.VMEM((size, *long), F32),
@@ -1064,7 +1123,7 @@
         ],
         compiler_params=remote_params(collective),
         name="sum_all",
-    )(term, grads, grad_wo, grad_qkv, vectors)
+    )(term, grads, grad_wo, grad_qkv, vectors, out_pairs)
 
 
 def paired_place(heads):
@@ -1144,30 +1203,36 @@
     return high, middle, rest - middle
 
 
-def attend_kernel(low, q, k, v, qdoc, kdoc, collect, attended, qback, acc):
+def attend_kernel(low, q, k, v, columns, kdoc, collect, attended, qback, acc):
     heads, rows, _ = q.shape
     block = kdoc.shape[2]
     index = pl.program_id(0)
     acc[...] = jnp.zeros_like(acc)
 
-    def step(j, diagonal):
+    def earlier(j, carry):
         slots = pl.ds(pl.multiple_of(j * block, block), block)
-        mask = qdoc[...] == kdoc[j]
-        if diagonal:
-            row = lax.broadcasted_iota(jnp.int32, (rows, block), 0)
-            column = lax.broadcasted_iota(jnp.int32, (rows, block), 1)
-            mask = (mask & (column < row)) | (column == row)
+        mask = columns[:, 1:2] == kdoc[j]
         for head in range(heads):
             scores = dot(q[head], k[head, slots, :], NT)
             weight = jnp.where(mask, jnp.exp(scores), 0.0).astype(BF16)
             acc[head] += dot(weight, v[head, slots, :])
-
-    def earlier(j, carry):
-        step(j, False)
         return carry
 
     lax.fori_loop(low[index], index, earlier, 0)
-    step(index, True)
+
+    strip = max(rows // 2, min(rows, 128))
+    for start in range(0, rows, strip):
+        at = slice(start, start + strip)
+        end = start + strip
+        slots = pl.ds(pl.multiple_of(index * block, block), end)
+        row = start + lax.broadcasted_iota(jnp.int32, (strip, end), 0)
+        column = lax.broadcasted_iota(jnp.int32, (strip, end), 1)
+        mask = columns[at, 1:2] == kdoc[index][:, :end]
+        mask = (mask & (column < row)) | (column == row)
+        for head in range(heads):
+            scores = dot(q[head, at, :], k[head, slots, :], NT)
+            weight = jnp.where(mask, jnp.exp(scores), 0.0).astype(BF16)
+            acc[head, at, :] += dot(weight, v[head, slots, :])
 
     lane = lax.broadcasted_iota(jnp.int32, (rows, EXT), 1)
     merged = jnp.zeros((rows, heads * DK), F32)
@@ -1189,7 +1254,7 @@
     attended[...] = merged.astype(BF16)
 
 
-def attend(low, q, k, v, qdoc, kdoc, collect):
+def attend(low, q, k, v, columns, kdoc, collect):
     heads, tokens, _ = q.shape
     block = kdoc.shape[2]
     width = heads * DK
@@ -1207,7 +1272,7 @@
                 headed,
                 whole(k),
                 whole(v),
-                pl.BlockSpec((block, 1), lambda i, low: (i, 0)),
+                pl.BlockSpec((block, columns.shape[1]), lambda i, low: (i, 0)),
                 whole(kdoc),
                 whole(collect),
             ],
@@ -1223,7 +1288,7 @@
             flops=40_000_000_000, bytes_accessed=16 << 20, transcendentals=0
         ),
         name="attend",
-    )(low, q, k, v, qdoc, kdoc, collect)
+    )(low, q, k, v, columns, kdoc, collect)
 
 
 def unrope(grad, unit, gain, scale, cos, sin, sums):
@@ -1255,7 +1320,7 @@
     k_pair,
     v,
     qdoc,
-    kdoc,
+    columns,
     cosine,
     sine,
     rq,
@@ -1318,13 +1383,9 @@
             d_heads[stack, :] = jnp.where(head_lanes(grads.shape, head, False), grads, 0)
         dq[...] = jnp.zeros_like(dq)
 
-        def step(j, diagonal):
+        def earlier(j, carry):
             slots = pl.ds(pl.multiple_of(j * rows, rows), rows)
-            mask = kdoc[slots, :] == qdoc[0]
-            if diagonal:
-                key = lax.broadcasted_iota(jnp.int32, (rows, rows), 0)
-                query = lax.broadcasted_iota(jnp.int32, (rows, rows), 1)
-                mask = (mask & (key < query)) | (key == query)
+            mask = columns[slots, 2:3] == qdoc[0]
             total = dq[...]
             for head in range(heads):
                 scores = dot(k[head, slots, :], qback[head], NT)
@@ -1338,17 +1399,46 @@
             dq[...] = total
             dv[slots, :] += dot(probs_all[...], d_heads[...])
             dk[slots, :] += dot(scores_all[...], q_heads[...])
-
-        def earlier(j, carry):
-            step(j, False)
             return carry
 
         lax.fori_loop(low[index], index, earlier, 0)
-        step(index, True)
+
+        strip = max(rows // 2, min(rows, 128))
+        for start in range(0, rows, strip):
+            after_start = slice(start, rows)
+            count = rows - start
+            slots = pl.ds(pl.multiple_of(index * rows + start, strip), strip)
+            key = start + lax.broadcasted_iota(jnp.int32, (strip, count), 0)
+            query = start + lax.broadcasted_iota(jnp.int32, (strip, count), 1)
+            mask = columns[slots, 2:3] == qdoc[0][:, after_start]
+            mask = (mask & (key < query)) | (key == query)
+            values, keys, queries_grad = None, None, None
+            for head in range(heads):
+                scores = dot(k[head, slots, :], qback[head, after_start, :], NT)
+                probs = jnp.where(mask, jnp.exp(scores), 0.0)
+                dprobs = dot(v[head, slots, :], dox[head, after_start, :], NT)
+                dscores = (probs * dprobs).astype(BF16)
+                stack = slice(head * rows + start, (head + 1) * rows)
+                terms = (
+                    dot(probs.astype(BF16), d_heads[stack, :]),
+                    dot(dscores, q_heads[stack, :]),
+                    dot(dscores, k_heads[head, slots, :], TN),
+                )
+                if head == 0:
+                    values, keys, queries_grad = terms
+                else:
+                    values, keys, queries_grad = (
+                        values + terms[0],
+                        keys + terms[1],
+                        queries_grad + terms[2],
+                    )
+            dv[slots, :] += values
+            dk[slots, :] += keys
+            dq[after_start, :] += queries_grad
 
         raw, grad_gain = unrope(
             dq[...] * scale,
-            queries.astype(F32) / gain[...],
+            queries.astype(F32) * (1.0 / gain[...]),
             gain[...],
             rq[...],
             cosine[...],
@@ -1364,7 +1454,7 @@
         slots = pl.ds(pl.multiple_of(index * rows, rows), rows)
         raw, grad_gain = unrope(
             dk[slots, :] * scale,
-            k_pair[slots, :].astype(F32) / gain[...],
+            k_pair[slots, :].astype(F32) * (1.0 / gain[...]),
             gain[...],
             rk[...],
             cosine[...],
@@ -1416,7 +1506,7 @@
     k_pair,
     v,
     qdoc,
-    kdoc,
+    columns,
     cosine,
     sine,
     rq,
@@ -1464,7 +1554,7 @@
                 whole(k_pair),
                 whole(v),
                 pl.BlockSpec((1, 1, block), lambda i, low: (now(i), 0, 0)),
-                whole(kdoc),
+                whole(columns),
                 rows(width // 2, both),
                 rows(width // 2, both),
                 rows(width // 2, now),
@@ -1516,7 +1606,7 @@
         k_pair,
         v,
         qdoc,
-        kdoc,
+        columns,
         cosine,
         sine,
         rq,
@@ -1609,10 +1699,24 @@
     part = width // size
     rows = packed_wo.shape[2]
     greet_pair_and_line(size)
-    exchange = Exchange(
-        size, attended, merged, row_part(mine), column_part(part), send, receive, local
-    )
-    exchange.start()
+    every = strips(mine)
+
+    def exchange(order):
+        at = every[order]
+        return Exchange(
+            size,
+            attended,
+            merged,
+            lambda ref, j: ref.at[
+                pl.ds(pl.multiple_of(j * mine + at.start, at.size), at.size), :
+            ],
+            lambda ref, j: ref.at[at, pl.ds(pl.multiple_of(j * part, part), part)],
+            send.at[order],
+            receive.at[order],
+            local.at[order],
+        )
+
+    exchange(0).start()
     own = [
         pltpu.make_async_copy(
             packed.at[:, :, pl.ds(packed.shape[2] - rows, rows), :], packed_wo, own_sems.at[0]
@@ -1634,10 +1738,12 @@
         copy.wait()
     output_matrix(packed_wo, full_wo)
     resid_out[...] = resid[...]
-    exchange.wait()
 
     swaps = []
-    for order, at in enumerate(strips(mine)):
+    for order, at in enumerate(every):
+        exchange(order).wait()
+        if order + 1 < len(every):
+            exchange(order + 1).start()
         branch = dot(merged[at, :part], full_wo[0], NT)
         for member in range(1, size):
             branch += dot(
@@ -1697,7 +1803,9 @@
             pltpu.VMEM((size, chips, rows, 2 * part), BF16),
             pltpu.VMEM((mine, width), BF16),
             pltpu.VMEM((mine, width), BF16),
-            *exchange_semaphores(size),
+            pltpu.SemaphoreType.DMA((count, size)),
+            pltpu.SemaphoreType.DMA((count, size)),
+            pltpu.SemaphoreType.DMA((count,)),
             pltpu.SemaphoreType.DMA((1 + size,)),
             *core_semaphores(count),
         ],
@@ -1909,14 +2017,14 @@
     up_in,
     gate_in,
     result,
-    grad_middle,
-    middle,
-    resid,
-    unit,
+    grad_middle_in,
+    middle_in,
+    resid_in,
+    unit_in,
     branch_scale,
     mixed_scale,
     alpha,
-    full_wo,
+    full_wo_in,
     dup_out,
     dgate_out,
     grad_u,
@@ -1931,12 +2039,30 @@
     got,
     sum_u,
     sum_v,
+    grad_middle,
+    middle,
+    resid,
+    unit,
+    full_wo,
     send,
     receive,
     local,
     core_sent,
     core_got,
+    load_sems,
 ):
+    loads = [
+        pltpu.make_async_copy(there, here, load_sems.at[order])
+        for order, (there, here) in enumerate(
+            (
+                (grad_middle_in, grad_middle),
+                (middle_in, middle),
+                (resid_in, resid),
+                (unit_in, unit),
+                (full_wo_in, full_wo),
+            )
+        )
+    ]
     exchange = Exchange(
         size,
         result,
@@ -1951,6 +2077,8 @@
 
     @pl.when(first_step())
     def _():
+        for copy in loads:
+            copy.start()
         greet_pair_and_line(size)
         exchange.start()
 
@@ -2001,6 +2129,8 @@
     def _():
         grad_u[...] = sum_u[...]
         grad_v[...] = sum_v[...]
+        for copy in loads:
+            copy.wait()
         dx_swap.wait()
         for order, at in enumerate(strips(acc.shape[0])):
             grad_old, grad_branch, part_alpha = residual_backward(
@@ -2056,6 +2186,7 @@
     hidden = jax.ShapeDtypeStruct((parts, tokens, units), BF16)
     sums = jax.ShapeDtypeStruct((parts, 1, units), F32)
     state = jax.ShapeDtypeStruct((block, width), BF16)
+    kept = (grad_middle, middle, resid, unit, full_wo)
     return pl.pallas_call(
         functools.partial(feed_back_kernel, size),
         grid=(2, parts),
@@ -2067,7 +2198,9 @@
             piece,
             piece,
             ANY,
-            *[vmem] * 8,
+            *[ANY] * 4,
+            *[vmem] * 3,
+            ANY,
         ],
         out_specs=[piece, piece, vmem, vmem, ANY, vmem, vmem, vmem, vmem],
         out_shape=[
@@ -2087,8 +2220,10 @@
             pltpu.VMEM((block, width), BF16),
             pltpu.VMEM((parts, 1, units), F32),
             pltpu.VMEM((parts, 1, units), F32),
+            *[pltpu.VMEM(each.shape, each.dtype) for each in kept],
             *exchange_semaphores(size),
             *core_semaphores(1),
+            pltpu.SemaphoreType.DMA((len(kept),)),
         ],
         compiler_params=remote_params(collective),
         cost_estimate=pl.CostEstimate(
@@ -2290,6 +2425,7 @@
         slot = jnp.arange(slots, dtype=jnp.int32)
         low = jnp.concatenate([starts[::block] // block, me[None]])
         key_docs = jnp.where(valid[0] == 1, docs, -1)
+        columns = jnp.stack([slot - starts, docs, key_docs], axis=1).astype(F32)
         inverse = jnp.exp(
             jnp.arange(HALF, dtype=F32) * (-2.0 * math.log(ROPE_BASE) / DK)
         )
@@ -2313,7 +2449,7 @@
             hidden[0],
             (wq, wk, wv, wo, w_up, w_gate, w_down),
             vectors[None],
-            (slot - starts).astype(F32)[:, None],
+            columns,
             jnp.tile(inverse, heads)[None],
             gain,
             jnp.asarray(turn, BF16),
@@ -2340,8 +2476,8 @@
             q,
             k,
             v,
-            docs[:, None],
-            key_docs.reshape(slots // block, 1, block),
+            columns,
+            key_docs.astype(F32).reshape(slots // block, 1, block),
             collect_plain,
         )
         (
@@ -2401,8 +2537,8 @@
             k,
             k_pair,
             v,
-            docs.reshape(slots // block, 1, block),
-            key_docs[:, None],
+            docs.astype(F32).reshape(slots // block, 1, block),
+            columns,
             cosine,
             sine,
             rq,
@@ -2437,20 +2573,26 @@
             ],
             axis=1,
         )
-        grad_hidden, owned, owned_output, owned_qkv, summed = sum_all(
+        (
+            grad_hidden,
+            owned_upward,
+            owned_gating,
+            owned_downward,
+            owned_output,
+            owned_query,
+            owned_keys,
+            owned_values,
+            summed,
+        ) = sum_all(
             term,
             grads,
             grad_wo,
             grad_qkv.reshape(chips, 2, rows, 3 * part),
             placed[:, None],
+            jnp.asarray(turn.T, BF16),
             chips,
             5,
         )
-        owned_upward, owned_gating, owned_downward = owned[0], owned[1], owned[2].T
-        owned_output = owned_output.T
-        owned_query = out_pairs(owned_qkv[:, :part])
-        owned_keys = out_pairs(owned_qkv[:, part : 2 * part])
-        owned_values = owned_qkv[:, 2 * part :]
         bounds = [2 * units, 4 * units, 4 * units + part, 4 * units + 2 * part]
         summed_up, summed_gate, summed_qk, summed_attn, summed_mlp = jnp.split(
             summed[0], bounds

time: 715 us -> 700 us (0.979); the launches traced: 701 us -> 698 us
    pallas_call x1, Pallas kernels: 197 us -> 211 us  [sum_all(): pl.pallas_call(functools.partial(sum_all_kernel, size, chips, chunks, spl...]
    pallas_call x1, Pallas kernels: 175 us -> 166 us  [front(): pl.pallas_call(functools.partial(front_kernel, size, chips, chunks, heigh...]
where the time goes in v6:
time: 700 us; the launch traced here: 698 us
  Pallas kernels  666 us (95%)
  local copies, waits for them, and re-layouts  19 us (3%)
  other arithmetic  10.6 us (2%)
    pallas_call x1, Pallas kernels, sum_all(): pl.pallas_call(functools.partial(sum_all_kernel, size, chips, chunks, spl...  211 us
    pallas_call x1, Pallas kernels, front(): pl.pallas_call(functools.partial(front_kernel, size, chips, chunks, heigh...  166 us
    pallas_call x1, Pallas kernels, attend_back(): pl.pallas_call(attend_back_kernel, grid_spec=pltpu.PrefetchScalarGridSpec...  75.5 us
    pallas_call x1, Pallas kernels, mix(): pl.pallas_call(functools.partial(mix_kernel, size), in_specs=[ANY, ANY, A...  54.8 us
    pallas_call x1, Pallas kernels, feed(): pl.pallas_call(functools.partial(feed_kernel, size), grid=(2, parts), in_...  48.7 us
    pallas_call x1, Pallas kernels, feed_back(): pl.pallas_call(functools.partial(feed_back_kernel, size), grid=(2, parts)...  42.4 us
    pallas_call x1, Pallas kernels, feed_grads(): pl.pallas_call(functools.partial(feed_grads_kernel, size), grid=(4, parts...  41.6 us
    pallas_call x1, Pallas kernels, attend(): pl.pallas_call(attend_kernel, grid_spec=pltpu.PrefetchScalarGridSpec(num_...  25.5 us

profile of v6, /device:TPU:17, one launch (start us, length us, event | category | flops | bytes accessed | tf_op | source)
XLA Modules:
  0.0 697.8 jit_solution(4939885315602754237)
XLA Ops:
  0.6 1.2 slice.37
  2.5 0.9 add_select_fusion
  3.9 0.8 bitcast_select_fusion
  4.7 0.7 pad_add_fusion
  6.0 1.3 convert_element_type.30.columns
  7.3 0.6 reshape.184.gain
  9.3 166.5 %front.1 = (bf16[4,3072,256]{2,1,0:T(8,128)(2,1)}, bf16[8,128,768]{2,1,0:T(8,128)(2,1)}, bf16[4,4,896,512]{3,2,1,0:T(8,128)(2,1)}, f32[4,1,2560]{2,1,0:T(1,128)}...) custom-call(f32[3072,256]{1,0:T(8,128)} %bitcast.53, ...), custom_call_target="tpu_custom_call" | custom-call | tf_op jit(solution)/shard_map/front/pallas_call | solution.py:581
  177.1 25.5 %attend.1 = (bf16[3072,256]{1,0:T(8,128)(2,1)}, bf16[4,3072,128]{2,1,0:T(8,128)(2,1)}) custom-call(s32[7]{0:T(128)} %pad_add_fusion.1.low, bf16[4,3072,128]{2,1,0:T(8,128)(2,1)} %get-tuple-element.69.q, bf16[4,3072,128]{2,1,0:T(8,128)(2,1)} %get-tuple-element.70.k, bf16[4,3072,128]{2,1,0:T(8,128)(2,1)} %get-tuple-element.71.v, ...), custom_call_target="tpu_custom_call" | custom-call | flops 40000000000 | bytes 16777216 | tf_op jit(solution)/shard_map/attend/pallas_call | solution.py:1266
  203.2 54.8 %mix.1 = (bf16[1536,1024]{1,0:T(8,128)(2,1)}, f32[768,1024]{1,0:T(8,128)}, bf16[768,1024]{1,0:T(8,128)(2,1)}, f32[768,1]{1,0:T(8,128)}, f32[768,1]{1,0:T(8,128)}...) custom-call(bf16[3072,256]{1,0:T(8,128)(2,1)} %get-tuple-element.72., ...), custom_call_target="tpu_custom_call" | custom-call | tf_op jit(solution)/shard_map/mix/pallas_call | solution.py:1787
  259.9 48.7 %feed.1 = (bf16[4,1536,512]{2,1,0:T(8,128)(2,1)}, bf16[4,1536,512]{2,1,0:T(8,128)(2,1)}, bf16[4,1536,512]{2,1,0:T(8,128)(2,1)}, bf16[768,1024]{1,0:T(8,128)(2,1)...) custom-call(bf16[1536,1024]{1,0:T(8,128)(2,1)} %get-tuple-element.76.x, ...), custom_call_target="tpu_custom_call" | custom-call | flops 19327352832 | bytes 62914560 | tf_op jit(solution)/shard_map/feed/pallas_call | solution.py:1977
  308.6 42.4 %feed_back.1 = (bf16[4,1536,512]{2,1,0:T(8,128)(2,1)}, bf16[4,1536,512]{2,1,0:T(8,128)(2,1)}, f32[4,1,512]{2,1,0:T(1,128)}, f32[4,1,512]{2,1,0:T(1,128)}, bf16[3...) custom-call(bf16[1536,1024]{1,0:T(8,128)(2,1)} %get-tuple-element.79, ...), custom_call_target="tpu_custom_call" | custom-call | flops 19327352832 | bytes 73400320 | tf_op jit(solution)/shard_map/feed_back/pallas_call | solution.py:2190
  351.0 0.8 dynamic_update_slice.9
  351.8 0.7 broadcast_multiply_fusion
  352.6 41.6 %feed_grads.1 = (bf16[4,4,768,512]{3,2,1,0:T(8,128)(2,1)}, bf16[4,4,2,128,256]{4,3,2,1,0:T(8,128)(2,1)}, bf16[3072,256]{1,0:T(8,128)(2,1)}) custom-call(bf16[1536,1024]{1,0:T(8,128)(2,1)} %get-tuple-element.76.x, bf16[1536,1024]{1,0:T(8,128)(2,1)} %get-tuple-element.79.dbranch, bf16[4,1536,512]{2,1,0:T(8,128)(2,1)} %get-tuple-element.92.dup, ...), custom_call_target="tpu_custom_call" | custom-call | flops 19327352832 | bytes 41943040 | tf_op jit(solution)/shard_map/feed_grads/pallas_call | solution.py:2334
  394.2 75.5 %attend_back.1 = (bf16[4,3072,256]{2,1,0:T(8,128)(2,1)}, bf16[4,256,768]{2,1,0:T(8,128)(2,1)}, f32[1,256]{1,0:T(1,128)}) custom-call(s32[7]{0:T(128)} %pad_add_fusion.1.low, bf16[4,3072,128]{2,1,0:T(8,128)(2,1)} %get-tuple-element.90.qback, bf16[3072,256]{1,0:T(8,128)(2,1)} %get-tuple-element.91.q_pair, bf16[3072,256]{1,0:T(8,128)(2,1)} %get-tuple-element.98.dout, ...), custom_call_target="tpu_custom_call" | custom-call | flops 80000000000 | bytes 31457280 | tf_op jit(solution)/shard_map/attend_back/pallas_call | solution.py:1543
  470.3 1.3 reduce.11
  471.8 0.7 reduce.12
  472.5 0.7 reduce.13
  473.2 0.7 broadcast_in_dim.50.vectors
  473.9 211.2 %sum_all.1 = (f32[3072,256]{1,0:T(8,128)}, f32[128,1024]{1,0:T(8,128)}, f32[128,1024]{1,0:T(8,128)}, f32[1024,128]{1,0:T(8,128)}, f32[256,128]{1,0:T(8,128)}, /*...) custom-call(bf16[4,3072,256]{2,1,0:T(8,128)(2,1)} %get-tuple-element.106.term, ...), custom_call_target="tpu_custom_call" | custom-call | tf_op jit(solution)/shard_map/sum_all/pallas_call | solution.py:1081
  685.1 1.3 fusion.5
  686.4 1.3 fusion.4
  687.7 1.9 bitcast_convert_fusion
  689.6 1.1 copy-done
  690.7 1.7 copy.71
  692.4 0.7 copy.72
  693.0 0.7 copy.73
  693.7 0.7 copy.74
  694.3 0.7 copy.75
  695.0 0.8 copy.76
  695.8 0.8 copy.77
  696.6 0.8 copy.78
  (83 shorter events, 7.2 us)
Async XLA Ops:
  5.4 1.8 copy-start.16
  5.4 2.5 copy-start.12
  5.5 2.5 copy-start.15
  5.5 2.5 copy-start.17
  5.5 2.5 copy-start.18
  9.3 167.2 %copy-start.5 = (s32[1,3072]{1,0:T(1,128)S(1)}, s32[1,3072]{1,0:T(1,128)}, u32[]{:S(2)}) copy-start(s32[1,3072]{1,0:T(1,128)} %param.36) | copy-start | bytes 36868
  9.3 167.2 %copy-start.10 = (s32[1,3072]{1,0:T(1,128)S(1)}, s32[1,3072]{1,0:T(1,128)}, u32[]{:S(2)}) copy-start(s32[1,3072]{1,0:T(1,128)} %param.37) | copy-start | bytes 36868
  177.1 25.5 %copy-start.11 = (f32[4,1,2560]{2,1,0:T(1,128)S(1)}, f32[4,1,2560]{2,1,0:T(1,128)}, u32[]{:S(2)}) copy-start(f32[4,1,2560]{2,1,0:T(1,128)} %get-tuple-element.75) | copy-start | bytes 122884
  394.2 77.6 %copy-start.14 = (f32[1,1024]{1,0:T(1,128)S(1)}, f32[1,1024]{1,0:T(1,128)}, u32[]{:S(2)}) copy-start(f32[1,1024]{1,0:T(1,128)} %get-tuple-element.113) | copy-start | bytes 12292
  394.2 78.3 %copy-start.13 = (f32[1,1024]{1,0:T(1,128)S(1)}, f32[1,1024]{1,0:T(1,128)}, u32[]{:S(2)}) copy-start(f32[1,1024]{1,0:T(1,128)} %get-tuple-element.114) | copy-start | bytes 12292
  473.9 213.8 %copy-start.1 = (bf16[3072,256]{1,0:T(8,128)(2,1)S(1)}, bf16[3072,256]{1,0:T(8,128)(2,1)}, u32[]{:S(2)}) copy-start(bf16[3072,256]{1,0:T(8,128)(2,1)} %get-tuple-element.89) | copy-start | bytes 4718596
  687.6 3.0 copy-start
  690.7 1.7 copy-start.9
  690.7 2.4 copy-start.8
  690.7 3.0 copy-start.7
  690.7 3.7 copy-start.6
  690.7 4.3 copy-start.4
  692.4 3.4 copy-start.3
  692.4 4.2 copy-start.2

commit v7 on v6

--- a/solution.py
+++ b/solution.py
@@ -190,7 +190,7 @@
     chips,
     chunks,
     split,
-    hidden,
+    hidden_in,
     wq,
     wk,
     wv,
@@ -219,6 +219,7 @@
     rk_out,
     cosine_out,
     sine_out,
+    hidden,
     wide,
     full_qkv,
     packed,
@@ -249,10 +250,21 @@
     qkv_got,
     vector_sent,
     vector_got,
+    load_sems,
 ):
     me, chip, core = (lax.axis_index(name) for name in ("mp", "chip", "core"))
-    tokens, part = hidden.shape
+    tokens, part = hidden_in.shape
     rows = tokens // chunks
+    hidden_loads = [
+        pltpu.make_async_copy(
+            hidden_in.at[pl.ds(chunk * rows, rows), :],
+            hidden.at[pl.ds(chunk * rows, rows), :],
+            load_sems.at[chunk],
+        )
+        for chunk in range(chunks)
+    ]
+    for copy in hidden_loads:
+        copy.start()
     height, units = packed.shape
     lines = height // 7
     owner = chip * 2 + core
@@ -276,6 +288,7 @@
 
     for chunk in range(EARLY):
         at = pl.ds(chunk * rows, rows)
+        hidden_loads[chunk].wait()
         wide[me, at, :] = hidden[at, :].astype(BF16)
         send_hidden(chunk)
 
@@ -405,6 +418,7 @@
         copy.start()
     for chunk in range(EARLY, chunks):
         at = pl.ds(chunk * rows, rows)
+        hidden_loads[chunk].wait()
         wide[me, at, :] = hidden[at, :].astype(BF16)
     own[0].wait()
     for half in plane(me, 0):
@@ -580,7 +594,7 @@
     results = [padded, padded, padded, paired, paired, scale, scale, scale, scale]
     return pl.pallas_call(
         functools.partial(front_kernel, size, chips, chunks, height // 32 * 16),
-        in_specs=[vmem] * 16,
+        in_specs=[ANY, *[vmem] * 15],
         out_specs=[ANY] * 13,
         out_shape=[
             jax.ShapeDtypeStruct(*each)
@@ -593,6 +607,7 @@
             ]
         ],
         scratch_shapes=[
+            pltpu.VMEM((tokens, part), F32),
             pltpu.VMEM(*wide),
             pltpu.VMEM(*qkv),
             pltpu.VMEM((height, units), BF16),
@@ -615,6 +630,7 @@
             dma((2 * chips - 1,)),
             dma((size,)),
             dma((size,)),
+            dma((chunks,)),
         ],
         compiler_params=remote_params(collective),
         name="front",
@@ -779,13 +795,17 @@
     chips,
     chunks,
     split,
-    term,
+    term_in,
     grads,
     grad_wo,
     grad_qkv,
-    vectors,
+    grad_u,
+    grad_v,
+    grad_gain,
+    grad_alpha_a,
+    grad_alpha_m,
     out_pairs,
-    out,
+    out_there,
     owned_up,
     owned_gate,
     owned_down,
@@ -794,6 +814,9 @@
     owned_k,
     owned_v,
     owned_vectors,
+    term,
+    out,
+    vectors,
     term_up,
     term_down,
     acc_a,
@@ -840,6 +863,10 @@
     def sems(ref, which):
         return [ref.at[which, k] for k in range(4)]
 
+    term_loads = [
+        pltpu.make_async_copy(term_in.at[goal], term.at[goal], local.at[5 + goal])
+        for goal in range(size)
+    ]
     line = LineSum(
         size, chunks, lambda goal, at: term[goal, at, :], term_up, term_down, sems(term_sems, 0)
     )
@@ -931,8 +958,27 @@
         copy.start()
     for part in sums_ends:
         part.start(0)
+    for copy in term_loads:
+        copy.start()
+
+    units = grad_u.shape[2]
+    columns = out_pairs.shape[0]
+    at_gain = 4 * units
+    vectors[...] = jnp.zeros_like(vectors)
+    for member in range(size):
+        half = pl.multiple_of(core * units, units)
+        vectors[member, :, pl.ds(half, units)] = grad_u[member]
+        vectors[member, :, pl.ds(2 * units + half, units)] = grad_v[member] * math.sqrt(
+            size * columns
+        )
+        these = slice(member * columns, (member + 1) * columns)
+        vectors[member, :, at_gain + columns : at_gain + 2 * columns] = grad_alpha_a[:, these]
+        vectors[member, :, at_gain + 2 * columns :] = grad_alpha_m[:, these]
+    vectors[me, :, at_gain : at_gain + columns] = split_dot(grad_gain[...], out_pairs[...])
     for copy in vector_copies:
         copy.start()
+    for copy in term_loads:
+        copy.wait()
 
     owner = chip * 2 + core
     vector_bits = [1] + [2 * bit for bit in bits]
@@ -1006,6 +1052,8 @@
         vector_step(stage)
     for chunk in range(chunks):
         line.result(chunk, out, line.at(chunk))
+    out_copy = pltpu.make_async_copy(out, out_there, local.at[5 + size])
+    out_copy.start()
     owned_vectors[...] = vector_sum[len(vector_bits)]
     part = owned_v.shape[1]
     total_qkv = acc_qkv[0, 0]
@@ -1039,6 +1087,7 @@
         copy.start()
         swaps.append(copy)
     owned_wo[...] = turned_wo[...].T
+    out_copy.wait()
     for copy in swaps:
         copy.wait()
     owned_up[...] = owned[0]
@@ -1056,7 +1105,7 @@
         part.close()
 
 
-def sum_all(term, grads, grad_wo, grad_qkv, vectors, out_pairs, chips, collective):
+def sum_all(term, grads, grad_wo, grad_qkv, shares, out_pairs, chips, collective):
     size, tokens, part = term.shape
     height, units = grads.shape[2:]
     rows = height // 6
@@ -1067,7 +1116,7 @@
     dma = pltpu.SemaphoreType.DMA
     vmem = pl.BlockSpec(memory_space=pltpu.VMEM)
     wo_block, qkv_block = grad_wo.shape[3:], grad_qkv.shape[2:]
-    long = vectors.shape[1:]
+    long = (1, 4 * units + 3 * part)
 
     def sums(layers, block):
         return [
@@ -1080,8 +1129,8 @@
 
     return pl.pallas_call(
         functools.partial(sum_all_kernel, size, chips, chunks, split),
-        in_specs=[vmem, ANY, ANY, ANY, vmem, vmem],
-        out_specs=[vmem] * 9,
+        in_specs=[ANY, ANY, ANY, ANY, *[vmem] * (len(shares) + 1)],
+        out_specs=[ANY, *[vmem] * 8],
         out_shape=[
             jax.ShapeDtypeStruct((tokens, part), F32),
             jax.ShapeDtypeStruct((rows, 2 * units), F32),
@@ -1092,6 +1141,9 @@
             jax.ShapeDtypeStruct(long, F32),
         ],
         scratch_shapes=[
+            pltpu.VMEM((size, tokens, part), BF16),
+            pltpu.VMEM((tokens, part), F32),
+            pltpu.VMEM((size, *long), F32),
             *line((tokens, part)),
             *sums(size, (split, units)),
             *line((split, units)),
@@ -1110,7 +1162,7 @@
             pltpu.VMEM((stages + 1, *long), F32),
             pltpu.VMEM((stages + 1, *long), F32),
             pltpu.VMEM((size, *long), F32),
-            dma((5,)),
+            dma((6 + size,)),
             dma((5,)),
             dma((5,)),
             dma((size + stages,)),
@@ -1123,7 +1175,7 @@
         ],
         compiler_params=remote_params(collective),
         name="sum_all",
-    )(term, grads, grad_wo, grad_qkv, vectors, out_pairs)
+    )(term, grads, grad_wo, grad_qkv, *shares, out_pairs)
 
 
 def paired_place(heads):
@@ -1678,21 +1730,27 @@
     x,
     middle_out,
     unit_out,
+    merged_out,
+    full_wo_out,
+    resid_out,
+    cotangent_out,
     branch_scale_out,
     mixed_scale_out,
-    merged,
-    full_wo,
-    resid_out,
-    cotangent_low,
     packed_wo,
     middle_low,
     resid,
+    middle_kept,
+    unit_kept,
+    merged,
+    full_wo,
+    cotangent_low,
     send,
     receive,
     local,
     own_sems,
     core_sent,
     core_got,
+    out_sems,
 ):
     me, core = lax.axis_index("mp"), lax.axis_index("core")
     mine, width = middle_out.shape
@@ -1737,7 +1795,14 @@
     for copy in own:
         copy.wait()
     output_matrix(packed_wo, full_wo)
-    resid_out[...] = resid[...]
+    leaving = [
+        pltpu.make_async_copy(here, there, out_sems.at[order])
+        for order, (here, there) in enumerate(
+            ((full_wo, full_wo_out), (resid, resid_out), (cotangent_low, cotangent_out))
+        )
+    ]
+    for copy in leaving:
+        copy.start()
 
     swaps = []
     for order, at in enumerate(every):
@@ -1755,8 +1820,8 @@
         mixed = old + alpha[...] * (unit - old)
         mixed_scale = row_scale(mixed)
         middle = mixed * mixed_scale
-        middle_out[at, :] = middle
-        unit_out[at, :] = unit.astype(BF16)
+        middle_kept[at, :] = middle
+        unit_kept[at, :] = unit.astype(BF16)
         branch_scale_out[at, :] = branch_scale
         mixed_scale_out[at, :] = mixed_scale
         middle_low[at, :] = middle.astype(BF16)
@@ -1770,11 +1835,19 @@
         )
         swap.start()
         swaps.append(swap)
+        for kind, (here, there) in enumerate(
+            ((middle_kept, middle_out), (unit_kept, unit_out), (merged, merged_out))
+        ):
+            copy = pltpu.make_async_copy(
+                here.at[at, :], there.at[at, :], out_sems.at[3 + 3 * order + kind]
+            )
+            copy.start()
+            leaving.append(copy)
     keep = pltpu.make_async_copy(middle_low, x.at[pl.ds(0, mine), :], own_sems.at[0])
     keep.start()
     keep.wait()
-    for swap in swaps:
-        swap.wait()
+    for copy in swaps + leaving:
+        copy.wait()
 
 
 def mix(attended, packed, rows, wide, alpha, cotangent, collective):
@@ -1787,27 +1860,33 @@
     return pl.pallas_call(
         functools.partial(mix_kernel, size),
         in_specs=[ANY, ANY, ANY, vmem, vmem],
-        out_specs=[ANY, *[vmem] * 8],
+        out_specs=[*[ANY] * 7, vmem, vmem],
         out_shape=[
             jax.ShapeDtypeStruct((2 * mine, width), BF16),
             jax.ShapeDtypeStruct((mine, width), F32),
             jax.ShapeDtypeStruct((mine, width), BF16),
-            scale,
-            scale,
             jax.ShapeDtypeStruct((mine, width), BF16),
             jax.ShapeDtypeStruct((size, width, part), BF16),
             jax.ShapeDtypeStruct((mine, width), BF16),
             jax.ShapeDtypeStruct((slots, part), BF16),
+            scale,
+            scale,
         ],
         scratch_shapes=[
             pltpu.VMEM((size, chips, rows, 2 * part), BF16),
             pltpu.VMEM((mine, width), BF16),
             pltpu.VMEM((mine, width), BF16),
+            pltpu.VMEM((mine, width), F32),
+            pltpu.VMEM((mine, width), BF16),
+            pltpu.VMEM((mine, width), BF16),
+            pltpu.VMEM((size, width, part), BF16),
+            pltpu.VMEM((slots, part), BF16),
             pltpu.SemaphoreType.DMA((count, size)),
             pltpu.SemaphoreType.DMA((count, size)),
             pltpu.SemaphoreType.DMA((count,)),
             pltpu.SemaphoreType.DMA((1 + size,)),
             *core_semaphores(count),
+            pltpu.SemaphoreType.DMA((3 + 3 * count,)),
         ],
         compiler_params=remote_params(collective),
         name="mix",
@@ -2484,12 +2563,12 @@
             x,
             middle,
             unit,
-            branch_scale,
-            mixed_scale,
             merged,
             full_wo,
             resid,
             cotangent_low,
+            branch_scale,
+            mixed_scale,
         ) = mix(attended, packed, rows, wide, alpha_attn, cotangent[0], 1)
 
         up, gate, hidden_units, result, grad_middle, dbranch, grad_alpha_mlp = feed(
@@ -2551,28 +2630,6 @@
             wide,
             grad_resid,
         )
-        out_pairs = (
-            lambda w: w.reshape(w.shape[0], 2, heads, HALF)
-            .transpose(0, 2, 1, 3)
-            .reshape(w.shape[0], heads * DK)
-        )
-
-        zero = jnp.zeros((size, 2, units), F32)
-        placed_u = lax.dynamic_update_slice(zero, grad_u, (0, core, 0))
-        placed_v = lax.dynamic_update_slice(zero, grad_v * math.sqrt(width), (0, core, 0))
-        placed_qk = lax.dynamic_update_slice(
-            jnp.zeros((size, part), F32), out_pairs(grad_gain), (me, 0)
-        )
-        placed = jnp.concatenate(
-            [
-                placed_u.reshape(size, 2 * units),
-                placed_v.reshape(size, 2 * units),
-                placed_qk,
-                grad_alpha_attn.reshape(size, part),
-                grad_alpha_mlp.reshape(size, part),
-            ],
-            axis=1,
-        )
         (
             grad_hidden,
             owned_upward,
@@ -2588,7 +2645,7 @@
             grads,
             grad_wo,
             grad_qkv.reshape(chips, 2, rows, 3 * part),
-            placed[:, None],
+            (grad_u, grad_v, grad_gain, grad_alpha_attn, grad_alpha_mlp),
             jnp.asarray(turn.T, BF16),
             chips,
             5,

time: 700 us -> 697 us (level)
  no operation moved by 1% of the time
where the time goes in v7:
time: 697 us; the launch traced here: 693 us
  Pallas kernels  661 us (95%)
  local copies, waits for them, and re-layouts  19.2 us (3%)
  other arithmetic  10.9 us (2%)
    pallas_call x1, Pallas kernels, sum_all(): pl.pallas_call(functools.partial(sum_all_kernel, size, chips, chunks, spl...  211 us
    pallas_call x1, Pallas kernels, front(): pl.pallas_call(functools.partial(front_kernel, size, chips, chunks, heigh...  166 us
    pallas_call x1, Pallas kernels, attend_back(): pl.pallas_call(attend_back_kernel, grid_spec=pltpu.PrefetchScalarGridSpec...  75.5 us
    pallas_call x1, Pallas kernels, mix(): pl.pallas_call(functools.partial(mix_kernel, size), in_specs=[ANY, ANY, A...  51.1 us
    pallas_call x1, Pallas kernels, feed(): pl.pallas_call(functools.partial(feed_kernel, size), grid=(2, parts), in_...  48.7 us
    pallas_call x1, Pallas kernels, feed_back(): pl.pallas_call(functools.partial(feed_back_kernel, size), grid=(2, parts)...  42.4 us
    pallas_call x1, Pallas kernels, feed_grads(): pl.pallas_call(functools.partial(feed_grads_kernel, size), grid=(4, parts...  41.6 us
    pallas_call x1, Pallas kernels, attend(): pl.pallas_call(attend_kernel, grid_spec=pltpu.PrefetchScalarGridSpec(num_...  25.3 us

profile of v7, /device:TPU:17, one launch (start us, length us, event | category | flops | bytes accessed | tf_op | source)
XLA Modules:
  0.0 693.1 jit_solution(3073114656461872563)
XLA Ops:
  0.7 1.2 slice.37
  3.1 0.8 reshape.165
  3.9 0.6 reshape.166.gain
  4.5 0.7 broadcast_multiply_fusion
  5.2 0.7 pad_maximum_fusion
  5.9 0.6 broadcast_in_dim.32.vectors
  6.5 0.9 add_select_fusion
  8.8 0.8 bitcast_select_fusion
  9.5 0.7 pad_add_fusion
  10.3 1.4 fusion.3
  12.2 1.3 convert_element_type.30.columns
  13.4 165.7 %front.1 = (bf16[4,3072,256]{2,1,0:T(8,128)(2,1)}, bf16[8,128,768]{2,1,0:T(8,128)(2,1)}, bf16[4,4,896,512]{3,2,1,0:T(8,128)(2,1)}, f32[4,1,2560]{2,1,0:T(1,128)}...) custom-call(f32[3072,256]{1,0:T(8,128)} %bitcast.46, ...), custom_call_target="tpu_custom_call" | custom-call | tf_op jit(solution)/shard_map/front/pallas_call | solution.py:595
  179.2 0.8 copy.48
  180.0 0.6 broadcast_in_dim.35.s_u
  182.4 25.3 %attend.1 = (bf16[3072,256]{1,0:T(8,128)(2,1)}, bf16[4,3072,128]{2,1,0:T(8,128)(2,1)}) custom-call(s32[7]{0:T(128)} %pad_add_fusion.1.low, bf16[4,3072,128]{2,1,0:T(8,128)(2,1)} %get-tuple-element.69.q, bf16[4,3072,128]{2,1,0:T(8,128)(2,1)} %get-tuple-element.70.k, bf16[4,3072,128]{2,1,0:T(8,128)(2,1)} %get-tuple-element.71.v, ...), custom_call_target="tpu_custom_call" | custom-call | flops 40000000000 | bytes 16777216 | tf_op jit(solution)/shard_map/attend/pallas_call | solution.py:1318
  207.7 51.1 %mix.1 = (bf16[1536,1024]{1,0:T(8,128)(2,1)}, f32[768,1024]{1,0:T(8,128)}, bf16[768,1024]{1,0:T(8,128)(2,1)}, bf16[768,1024]{1,0:T(8,128)(2,1)}, bf16[4,1024,256...) custom-call(bf16[3072,256]{1,0:T(8,128)(2,1)} %get-tuple-element.72., ...), custom_call_target="tpu_custom_call" | custom-call | tf_op jit(solution)/shard_map/mix/pallas_call | solution.py:1860
  258.9 48.7 %feed.1 = (bf16[4,1536,512]{2,1,0:T(8,128)(2,1)}, bf16[4,1536,512]{2,1,0:T(8,128)(2,1)}, bf16[4,1536,512]{2,1,0:T(8,128)(2,1)}, bf16[768,1024]{1,0:T(8,128)(2,1)...) custom-call(bf16[1536,1024]{1,0:T(8,128)(2,1)} %get-tuple-element.76.x, ...), custom_call_target="tpu_custom_call" | custom-call | flops 19327352832 | bytes 62914560 | tf_op jit(solution)/shard_map/feed/pallas_call | solution.py:2056
  307.6 42.4 %feed_back.1 = (bf16[4,1536,512]{2,1,0:T(8,128)(2,1)}, bf16[4,1536,512]{2,1,0:T(8,128)(2,1)}, f32[4,1,512]{2,1,0:T(1,128)}, f32[4,1,512]{2,1,0:T(1,128)}, bf16[3...) custom-call(bf16[1536,1024]{1,0:T(8,128)(2,1)} %get-tuple-element.79, ...), custom_call_target="tpu_custom_call" | custom-call | flops 19327352832 | bytes 73400320 | tf_op jit(solution)/shard_map/feed_back/pallas_call | solution.py:2269
  350.0 3.3 bitcast_convert_fusion
  353.3 41.6 %feed_grads.1 = (bf16[4,4,768,512]{3,2,1,0:T(8,128)(2,1)}, bf16[4,4,2,128,256]{4,3,2,1,0:T(8,128)(2,1)}, bf16[3072,256]{1,0:T(8,128)(2,1)}) custom-call(bf16[1536,1024]{1,0:T(8,128)(2,1)} %get-tuple-element.76.x, bf16[1536,1024]{1,0:T(8,128)(2,1)} %get-tuple-element.79.dbranch, bf16[4,1536,512]{2,1,0:T(8,128)(2,1)} %get-tuple-element.92.dup, ...), custom_call_target="tpu_custom_call" | custom-call | flops 19327352832 | bytes 41943040 | tf_op jit(solution)/shard_map/feed_grads/pallas_call | solution.py:2413
  394.9 75.5 %attend_back.1 = (bf16[4,3072,256]{2,1,0:T(8,128)(2,1)}, bf16[4,256,768]{2,1,0:T(8,128)(2,1)}, f32[1,256]{1,0:T(1,128)}) custom-call(s32[7]{0:T(128)} %pad_add_fusion.1.low, bf16[4,3072,128]{2,1,0:T(8,128)(2,1)} %get-tuple-element.90.qback, bf16[3072,256]{1,0:T(8,128)(2,1)} %get-tuple-element.91.q_pair, bf16[3072,256]{1,0:T(8,128)(2,1)} %get-tuple-element.98.dout, ...), custom_call_target="tpu_custom_call" | custom-call | flops 80000000000 | bytes 31457280 | tf_op jit(solution)/shard_map/attend_back/pallas_call | solution.py:1595
  470.4 210.8 %sum_all.1 = (f32[3072,256]{1,0:T(8,128)}, f32[128,1024]{1,0:T(8,128)}, f32[128,1024]{1,0:T(8,128)}, f32[1024,128]{1,0:T(8,128)}, f32[256,128]{1,0:T(8,128)}, /*...) custom-call(bf16[4,3072,256]{2,1,0:T(8,128)(2,1)} %get-tuple-element.106.term_in, ...), custom_call_target="tpu_custom_call" | custom-call | tf_op jit(solution)/shard_map/sum_all/pallas_call | solution.py:1130
  681.2 1.3 fusion.4
  682.4 1.3 fusion.5
  683.7 3.8 copy.57
  687.6 0.7 copy.58
  688.3 0.7 copy.59
  688.9 0.7 copy.60
  689.6 0.7 copy.61
  690.2 0.8 copy.62
  691.0 0.8 copy.63
  691.8 0.8 copy.64
  (35 shorter events, 4.3 us)
Async XLA Ops:
  683.7 3.9 copy-start.6
  683.7 4.5 copy-start.5
  683.7 5.2 copy-start.4
  683.7 5.8 copy-start.3
  683.7 6.5 copy-start.2
  687.6 3.4 copy-start.1
  687.6 4.2 copy-start

commit v8 on v7

--- a/solution.py
+++ b/solution.py
@@ -1384,9 +1384,11 @@
     sums,
     wide,
     grad_resid,
+    out_low,
     term_out,
     grad_qkv,
     gain_out,
+    out_hidden,
     dk,
     dv,
     dq,
@@ -1417,6 +1419,7 @@
     @pl.when(step_at < steps)
     def _():
         index = step_at
+        out_hidden[...] = out_low[...].astype(F32)
         lane = lax.broadcasted_iota(jnp.int32, (rows, EXT), 1)
         grads = dout[...]
         queries = q_pair[...]
@@ -1570,6 +1573,7 @@
     sums,
     wide,
     grad_resid,
+    out_low,
 ):
     heads, tokens, _ = k.shape
     block = qdoc.shape[2]
@@ -1618,11 +1622,13 @@
                 whole(sums),
                 pl.BlockSpec((parts, block, part), lambda i, low: (0, after(i), 0)),
                 whole(grad_resid),
+                rows(out_low.shape[1], now),
             ],
             out_specs=[
                 pl.BlockSpec((parts, block, part), lambda i, low: (0, after(i), 0)),
                 pl.BlockSpec((parts, part, 3 * width), lambda i, low: (0, 0, 0)),
                 pl.BlockSpec((1, width), lambda i, low: (0, 0)),
+                rows(out_low.shape[1], now),
             ],
             scratch_shapes=[
                 pltpu.VMEM((tokens, width), F32),
@@ -1642,6 +1648,7 @@
             jax.ShapeDtypeStruct((parts, tokens, part), BF16),
             jax.ShapeDtypeStruct((parts, part, 3 * width), BF16),
             jax.ShapeDtypeStruct((1, width), F32),
+            jax.ShapeDtypeStruct(out_low.shape, F32),
         ],
         compiler_params=grid_params(1),
         cost_estimate=pl.CostEstimate(
@@ -1670,6 +1677,7 @@
         sums,
         wide,
         grad_resid,
+        out_low,
     )
 
 
@@ -1923,7 +1931,7 @@
     s_u,
     s_v,
     cotangent,
-    middle,
+    middle_in,
     alpha,
     up_out,
     gate_out,
@@ -1937,13 +1945,16 @@
     got,
     spread,
     low,
+    middle,
     send,
     receive,
     local,
     core_sent,
     core_got,
     keep_sems,
+    load_sem,
 ):
+    load = pltpu.make_async_copy(middle_in, middle, load_sem)
     exchange = Exchange(
         size,
         cotangent,
@@ -1958,6 +1969,7 @@
 
     @pl.when(first_step())
     def _():
+        load.start()
         greet_pair_and_line(size)
         exchange.start()
 
@@ -1989,6 +2001,7 @@
     @pl.when(last & (block == 1))
     def _():
         mine = acc.shape[0]
+        load.wait()
         branch_swap.wait()
         exchange.wait()
         swaps = []
@@ -2056,7 +2069,7 @@
     return pl.pallas_call(
         functools.partial(feed_kernel, size),
         grid=(2, parts),
-        in_specs=[rows, *packed_specs(packed, width), vector, vector, ANY, vmem, vmem],
+        in_specs=[rows, *packed_specs(packed, width), vector, vector, ANY, ANY, vmem],
         out_specs=[piece, piece, piece, vmem, vmem, ANY, vmem],
         out_shape=[
             hidden,
@@ -2073,9 +2086,11 @@
             low,
             low,
             low,
+            pltpu.VMEM((block, width), F32),
             *exchange_semaphores(size),
             *core_semaphores(1 + count),
             pltpu.SemaphoreType.DMA((count,)),
+            pltpu.SemaphoreType.DMA,
         ],
         compiler_params=remote_params(collective),
         cost_estimate=pl.CostEstimate(
@@ -2602,12 +2617,11 @@
             full_wo,
             3,
         )
-        out_hidden = out_low.astype(F32)
         grads, grad_wo, dattended = feed_grads(
             x, dbranch, dup, dgate, hidden_units, dbranch_attn, merged, dmerged, chips, 4
         )
 
-        term, grad_qkv, grad_gain = attend_back(
+        term, grad_qkv, grad_gain, out_hidden = attend_back(
             low,
             qback,
             q_pair,
@@ -2629,6 +2643,7 @@
             sums,
             wide,
             grad_resid,
+            out_low,
         )
         (
             grad_hidden,

time: 697 us -> 695 us (level)
  no operation moved by 1% of the time
where the time goes in v8:
time: 695 us; the launch traced here: 689 us
  Pallas kernels  661 us (95%)
  local copies, waits for them, and re-layouts  19.2 us (3%)
  other arithmetic  7.54 us (1%)
    pallas_call x1, Pallas kernels, sum_all(): pl.pallas_call(functools.partial(sum_all_kernel, size, chips, chunks, spl...  211 us
    pallas_call x1, Pallas kernels, front(): pl.pallas_call(functools.partial(front_kernel, size, chips, chunks, heigh...  166 us
    pallas_call x1, Pallas kernels, attend_back(): pl.pallas_call(attend_back_kernel, grid_spec=pltpu.PrefetchScalarGridSpec...  75.9 us
    pallas_call x1, Pallas kernels, mix(): pl.pallas_call(functools.partial(mix_kernel, size), in_specs=[ANY, ANY, A...  51.1 us
    pallas_call x1, Pallas kernels, feed(): pl.pallas_call(functools.partial(feed_kernel, size), grid=(2, parts), in_...  47.5 us
    pallas_call x1, Pallas kernels, feed_back(): pl.pallas_call(functools.partial(feed_back_kernel, size), grid=(2, parts)...  42.6 us
    pallas_call x1, Pallas kernels, feed_grads(): pl.pallas_call(functools.partial(feed_grads_kernel, size), grid=(4, parts...  41.8 us
    pallas_call x1, Pallas kernels, attend(): pl.pallas_call(attend_kernel, grid_spec=pltpu.PrefetchScalarGridSpec(num_...  25.3 us

profile of v8, /device:TPU:17, one launch (start us, length us, event | category | flops | bytes accessed | tf_op | source)
XLA Modules:
  0.0 689.0 jit_solution(94068547067542510)
XLA Ops:
  0.7 1.2 slice.37
  3.1 0.8 reshape.165
  3.9 0.6 reshape.166.gain
  4.5 0.7 broadcast_multiply_fusion
  5.2 0.7 pad_maximum_fusion
  5.9 0.6 broadcast_in_dim.29.vectors
  6.5 0.9 add_select_fusion
  8.8 0.8 bitcast_select_fusion
  9.5 0.7 pad_add_fusion
  10.3 1.4 fusion.3
  12.2 1.3 convert_element_type.29.columns
  13.4 165.7 %front.1 = (bf16[4,3072,256]{2,1,0:T(8,128)(2,1)}, bf16[8,128,768]{2,1,0:T(8,128)(2,1)}, bf16[4,4,896,512]{3,2,1,0:T(8,128)(2,1)}, f32[4,1,2560]{2,1,0:T(1,128)}...) custom-call(f32[3072,256]{1,0:T(8,128)} %bitcast.44, ...), custom_call_target="tpu_custom_call" | custom-call | tf_op jit(solution)/shard_map/front/pallas_call | solution.py:595
  179.2 0.8 copy.48
  180.0 0.6 broadcast_in_dim.32.s_u
  180.6 0.6 broadcast_in_dim.33.s_v
  182.4 25.3 %attend.1 = (bf16[3072,256]{1,0:T(8,128)(2,1)}, bf16[4,3072,128]{2,1,0:T(8,128)(2,1)}) custom-call(s32[7]{0:T(128)} %pad_add_fusion.1.low, bf16[4,3072,128]{2,1,0:T(8,128)(2,1)} %get-tuple-element.70.q, bf16[4,3072,128]{2,1,0:T(8,128)(2,1)} %get-tuple-element.71.k, bf16[4,3072,128]{2,1,0:T(8,128)(2,1)} %get-tuple-element.72.v, ...), custom_call_target="tpu_custom_call" | custom-call | flops 40000000000 | bytes 16777216 | tf_op jit(solution)/shard_map/attend/pallas_call | solution.py:1318
  207.7 51.1 %mix.1 = (bf16[1536,1024]{1,0:T(8,128)(2,1)}, f32[768,1024]{1,0:T(8,128)}, bf16[768,1024]{1,0:T(8,128)(2,1)}, bf16[768,1024]{1,0:T(8,128)(2,1)}, bf16[4,1024,256...) custom-call(bf16[3072,256]{1,0:T(8,128)(2,1)} %get-tuple-element.75., ...), custom_call_target="tpu_custom_call" | custom-call | tf_op jit(solution)/shard_map/mix/pallas_call | solution.py:1868
  258.9 47.5 %feed.1 = (bf16[4,1536,512]{2,1,0:T(8,128)(2,1)}, bf16[4,1536,512]{2,1,0:T(8,128)(2,1)}, bf16[4,1536,512]{2,1,0:T(8,128)(2,1)}, bf16[768,1024]{1,0:T(8,128)(2,1)...) custom-call(bf16[1536,1024]{1,0:T(8,128)(2,1)} %get-tuple-element.79.x, ...), custom_call_target="tpu_custom_call" | custom-call | flops 19327352832 | bytes 62914560 | tf_op jit(solution)/shard_map/feed/pallas_call | solution.py:2069
  306.3 42.6 %feed_back.1 = (bf16[4,1536,512]{2,1,0:T(8,128)(2,1)}, bf16[4,1536,512]{2,1,0:T(8,128)(2,1)}, f32[4,1,512]{2,1,0:T(1,128)}, f32[4,1,512]{2,1,0:T(1,128)}, bf16[3...) custom-call(bf16[1536,1024]{1,0:T(8,128)(2,1)} %get-tuple-element.82, ...), custom_call_target="tpu_custom_call" | custom-call | flops 19327352832 | bytes 73400320 | tf_op jit(solution)/shard_map/feed_back/pallas_call | solution.py:2284
  348.9 41.8 %feed_grads.1 = (bf16[4,4,768,512]{3,2,1,0:T(8,128)(2,1)}, bf16[4,4,2,128,256]{4,3,2,1,0:T(8,128)(2,1)}, bf16[3072,256]{1,0:T(8,128)(2,1)}) custom-call(bf16[1536,1024]{1,0:T(8,128)(2,1)} %get-tuple-element.79.x, bf16[1536,1024]{1,0:T(8,128)(2,1)} %get-tuple-element.82.dbranch, bf16[4,1536,512]{2,1,0:T(8,128)(2,1)} %get-tuple-element.92.dup, ...), custom_call_target="tpu_custom_call" | custom-call | flops 19327352832 | bytes 41943040 | tf_op jit(solution)/shard_map/feed_grads/pallas_call | solution.py:2428
  390.7 75.9 %attend_back.1 = (bf16[4,3072,256]{2,1,0:T(8,128)(2,1)}, bf16[4,256,768]{2,1,0:T(8,128)(2,1)}, f32[1,256]{1,0:T(1,128)}, f32[3072,256]{1,0:T(8,128)}) custom-call(s32[7]{0:T(128)} %pad_add_fusion.1.low, bf16[4,3072,128]{2,1,0:T(8,128)(2,1)} %get-tuple-element.73.qback, bf16[3072,256]{1,0:T(8,128)(2,1)} %get-tuple-element.74.q_pair, ...), custom_call_target="tpu_custom_call" | custom-call | flops 80000000000 | bytes 31457280 | tf_op jit(solution)/shard_map/attend_back/pallas_call | solution.py:1599
  466.6 210.7 %sum_all.1 = (f32[3072,256]{1,0:T(8,128)}, f32[128,1024]{1,0:T(8,128)}, f32[128,1024]{1,0:T(8,128)}, f32[1024,128]{1,0:T(8,128)}, f32[256,128]{1,0:T(8,128)}, /*...) custom-call(bf16[4,3072,256]{2,1,0:T(8,128)(2,1)} %get-tuple-element.108.term_in, ...), custom_call_target="tpu_custom_call" | custom-call | tf_op jit(solution)/shard_map/sum_all/pallas_call | solution.py:1130
  677.3 1.3 fusion.4
  678.6 1.3 fusion.5
  679.9 3.8 copy.57
  683.7 0.7 copy.58
  684.4 0.7 copy.59
  685.1 0.7 copy.60
  685.7 0.7 copy.61
  686.4 0.8 copy.62
  687.2 0.8 copy.63
  688.0 0.8 copy.64
  (34 shorter events, 3.7 us)
Async XLA Ops:
  679.9 3.9 copy-start.6
  679.9 4.5 copy-start.5
  679.9 5.2 copy-start.4
  679.9 5.8 copy-start.3
  679.9 6.5 copy-start.2
  683.7 3.4 copy-start.1
  683.7 4.2 copy-start
